TPU v7x, 32 devices: a whole 2x2x4 slice. The times are simulated.
32 devices in a mesh: dp: 16 (over z, y, x), mp: 2 (over core).
Axes of the slice: x: 2, y: 2, z: 4, core: 2. Of those that a mesh axis runs over, the one named last changes fastest.
Arguments:
- pixels: bfloat16 [2, 64, 384, 324], P(None, ('dp', 'mp')), may hold values from -6 to 6
- grid_class: int32 [2, 64], P(None, 'dp'), may hold values from 0 to 2
- extent: int32 [384], P('mp'), may hold values from 1 to 18
- ssm_rate: float32 [2, 384, 64], P(None, 'mp'), may hold values from 0.5 to 20
- ssm_freq: float32 [2, 384, 64], P(None, 'mp'), may hold values from 0 to 8
- ssm_coef: float32 [2, 384, 64], P(None, 'mp'), may hold values from -0.75 to 0.75
- skip_gain: float32 [384], P('mp'), may hold values from -4 to 4
- norm_gain: float32 [384], replicated, may hold values from 0.5 to 1.5
- norm_bias: float32 [384], replicated, may hold values from -3 to 3
- w_in: bfloat16 [384, 1536], P(None, 'mp'), may hold values from -0.3125 to 0.3125
- b_in: float32 [1536], P('mp'), may hold values from -3 to 3
- w_out: bfloat16 [1536, 384], P('mp'), may hold values from -0.15625 to 0.15625
- b_out: float32 [384], replicated, may hold values from -3 to 3
- layer_scale: float32 [384], replicated, may hold values from 0.5 to 1.5
- cotangent: bfloat16 [2, 64, 384, 324], P(None, ('dp', 'mp')), may hold values from -6 to 6
Outputs:
- block_out: bfloat16 [2, 64, 384, 324], P(None, ('dp', 'mp'))
- pixels_grad: bfloat16 [2, 64, 384, 324], P(None, ('dp', 'mp'))
- rate_grad: float32 [2, 384, 64], P(None, 'mp')
- freq_grad: float32 [2, 384, 64], P(None, 'mp')
- coef_grad: float32 [2, 384, 64], P(None, 'mp')
- skip_grad: float32 [384], P('mp')
- gain_grad: float32 [384], replicated
- bias_grad: float32 [384], replicated
- w_in_grad: float32 [384, 1536], P(None, 'mp')
- b_in_grad: float32 [1536], P('mp')
- w_out_grad: float32 [1536, 384], P('mp')
- b_out_grad: float32 [384], replicated
- scale_grad: float32 [384], replicated
All inputs are finite; a program needn't handle non-finite values.
Results may differ from a plain program's by a relative error of at most 0.012.
Values may be sent and summed in bfloat16 or wider, within the bound.
A program may use at most 256 MiB of HBM per device.

v0:
```python
from functools import partial

import jax
import jax.numpy as jnp
import numpy as np
from jax import lax
from jax.sharding import PartitionSpec as P

GRID = 18


HIGH = lax.Precision.HIGHEST


def lag_selector(grid_cells):
    positions = np.arange(grid_cells)
    distance = np.abs(positions[:, None] - positions[None, :])
    return (distance[None, :, :] == positions[:, None, None]).astype(np.float32)


def kernel_tables(decay_rate, frequency, coef_in, extent):
    lag_values = jnp.arange(GRID, dtype=jnp.float32)
    lag_whole = jnp.arange(GRID, dtype=jnp.int32)
    selector = jnp.asarray(lag_selector(GRID))
    tables = []
    for category in range(3):
        grid_side = 10 + 4 * category
        scaled = lag_values / grid_side
        wave_terms = jnp.exp(-decay_rate[..., None] * scaled) * jnp.cos(
            frequency[..., None] * scaled
        )
        kernel_row = jnp.sum(coef_in[..., None] * wave_terms, axis=2)
        within = (lag_whole[None, None, :] < extent[None, :, None]) & (
            lag_whole[None, None, :] < grid_side
        )
        kernel_row = jnp.where(within, kernel_row, 0.0)
        toeplitz = jnp.einsum("acl,lip->acip", kernel_row, selector, precision=HIGH)
        inside = np.arange(GRID) < grid_side
        square_mask = (inside[:, None] & inside[None, :]).astype(np.float32)
        tables.append(toeplitz * jnp.asarray(square_mask))
    return jnp.stack(tables)


def mix_channels(field_in, classes, decay_rate, frequency, coef_in, skip_in, extent):
    tables = kernel_tables(decay_rate, frequency, coef_in, extent)
    onehot = (classes[:, None] == jnp.arange(3, dtype=jnp.int32)[None, :]).astype(jnp.float32)
    rows_op = jnp.einsum("nk,kcip->ncip", onehot, tables[:, 0], precision=HIGH)
    cols_op = jnp.einsum("nk,kcip->ncip", onehot, tables[:, 1], precision=HIGH)
    count = field_in.shape[0]
    channels = field_in.shape[1]
    grid_view = field_in.reshape(count, channels, GRID, GRID)
    partial_rows = jnp.einsum("ncip,ncpq->nciq", rows_op, grid_view, precision=HIGH)
    mixed_out = jnp.einsum("nciq,ncjq->ncij", partial_rows, cols_op, precision=HIGH)
    mixed_out = mixed_out + skip_in[None, :, None, None] * grid_view
    return mixed_out.reshape(count, channels, GRID * GRID)


def layer_norm(field_in, gain_in, bias_in):
    channel_mean = jnp.mean(field_in, axis=1, keepdims=True)
    centered = field_in - channel_mean
    variance = jnp.mean(centered * centered, axis=1, keepdims=True)
    return centered * lax.rsqrt(variance + 1e-06) * gain_in[None, :, None] + bias_in[None, :, None]


def pixel_mask(classes):
    grid_side = 10 + 4 * classes
    pixel_index = jnp.arange(GRID * GRID, dtype=jnp.int32)
    pixel_row = pixel_index // GRID
    pixel_col = pixel_index % GRID
    valid = (pixel_row[None, :] < grid_side[:, None]) & (pixel_col[None, :] < grid_side[:, None])
    return valid.astype(jnp.float32)[:, None, :]


def on_device(
    pixels,
    grid_class,
    extent,
    ssm_rate,
    ssm_freq,
    ssm_coef,
    skip_gain,
    norm_gain,
    norm_bias,
    w_in,
    b_in,
    w_out,
    b_out,
    layer_scale,
    cotangent,
):
    micro_count = pixels.shape[0]
    tok_images = pixels.shape[1]
    my_index = lax.axis_index("mp")
    gelu_exact = partial(jax.nn.gelu, approximate=False)
    rate_use, freq_use, coef_use, skip_use, extent_use = (
        ssm_rate,
        ssm_freq,
        ssm_coef,
        skip_gain,
        extent,
    )
    acc_rate = jnp.zeros_like(rate_use)
    acc_freq = jnp.zeros_like(freq_use)
    acc_coef = jnp.zeros_like(coef_use)
    acc_skip = jnp.zeros_like(skip_use)
    acc_gain = jnp.zeros_like(norm_gain)
    acc_bias = jnp.zeros_like(norm_bias)
    acc_scale = jnp.zeros_like(layer_scale)
    acc_b_out = jnp.zeros_like(b_out)
    acc_w_in = jnp.zeros(w_in.shape, jnp.float32)
    acc_b_in = jnp.zeros(b_in.shape, jnp.float32)
    acc_w_out = jnp.zeros(w_out.shape, jnp.float32)
    outputs = []
    input_grads = []
    for micro in range(micro_count):
        classes_all = grid_class[micro]
        classes_own = lax.dynamic_slice_in_dim(classes_all, my_index * tok_images, tok_images)
        valid = pixel_mask(classes_own)
        field_tok = pixels[micro]
        cot_f = cotangent[micro].astype(jnp.float32)
        field_ch = lax.all_to_all(field_tok, "mp", split_axis=1, concat_axis=0, tiled=True)

        def mixer_local(field_in, decay_rate, frequency, coef_in, skip_in):
            return mix_channels(
                field_in, classes_all, decay_rate, frequency, coef_in, skip_in, extent_use
            )

        mixed_ch, mixer_back = jax.vjp(
            mixer_local, field_ch.astype(jnp.float32), rate_use, freq_use, coef_use, skip_use
        )
        mixed_tok = lax.all_to_all(
            mixed_ch.astype(jnp.bfloat16), "mp", split_axis=0, concat_axis=1, tiled=True
        ).astype(jnp.float32)
        normed, norm_back = jax.vjp(layer_norm, mixed_tok, norm_gain, norm_bias)
        normed_b = normed.astype(jnp.bfloat16)
        normed_all = lax.all_gather(normed_b, "mp", axis=0, tiled=True)
        pre_act = (
            jnp.einsum("ncp,cf->nfp", normed_all, w_in, preferred_element_type=jnp.float32)
            + b_in[None, :, None]
        )
        activated, gelu_back = jax.vjp(gelu_exact, pre_act)
        act_b = activated.astype(jnp.bfloat16)
        piece = lax.slice_in_dim(act_b, 0, lax.axis_size("mp") * tok_images, axis=0)
        mlp_out = (
            lax.psum_scatter(
                jnp.einsum("nfp,fc->ncp", piece, w_out, preferred_element_type=jnp.float32).astype(
                    jnp.bfloat16
                ),
                "mp",
                scatter_dimension=0,
                tiled=True,
            ).astype(jnp.float32)
            + b_out[None, :, None]
        )
        block_f = field_tok.astype(jnp.float32) + layer_scale[None, :, None] * mlp_out * valid
        outputs.append(block_f.astype(jnp.bfloat16))
        acc_scale = acc_scale + jnp.sum(cot_f * mlp_out * valid, axis=(0, 2))
        grad_mlp = (cot_f * layer_scale[None, :, None] * valid).astype(jnp.bfloat16)
        acc_b_out = acc_b_out + jnp.sum(grad_mlp.astype(jnp.float32), axis=(0, 2))
        grad_all = lax.all_gather(grad_mlp, "mp", axis=0, tiled=True)
        acc_w_out = acc_w_out + jnp.einsum(
            "nfp,ncp->fc", act_b, grad_all, preferred_element_type=jnp.float32
        )
        grad_act = jnp.einsum("ncp,fc->nfp", grad_all, w_out, preferred_element_type=jnp.float32)
        (grad_pre,) = gelu_back(grad_act)
        grad_pre_b = grad_pre.astype(jnp.bfloat16)
        acc_b_in = acc_b_in + jnp.sum(grad_pre_b.astype(jnp.float32), axis=(0, 2))
        acc_w_in = acc_w_in + jnp.einsum(
            "ncp,nfp->cf", normed_all, grad_pre_b, preferred_element_type=jnp.float32
        )
        grad_normed = lax.psum_scatter(
            jnp.einsum("nfp,cf->ncp", grad_pre_b, w_in, preferred_element_type=jnp.float32).astype(
                jnp.bfloat16
            ),
            "mp",
            scatter_dimension=0,
            tiled=True,
        ).astype(jnp.float32)
        grad_mixed, grad_gain, grad_bias = norm_back(grad_normed)
        acc_gain = acc_gain + grad_gain
        acc_bias = acc_bias + grad_bias
        grad_mixed_ch = lax.all_to_all(
            grad_mixed.astype(jnp.bfloat16), "mp", split_axis=1, concat_axis=0, tiled=True
        )
        grad_field_ch, grad_rate, grad_freq, grad_coef, grad_skip = mixer_back(
            grad_mixed_ch.astype(jnp.float32)
        )
        grad_field_tok = lax.all_to_all(
            grad_field_ch.astype(jnp.bfloat16), "mp", split_axis=0, concat_axis=1, tiled=True
        )
        acc_rate = acc_rate + grad_rate
        acc_freq = acc_freq + grad_freq
        acc_coef = acc_coef + grad_coef
        acc_skip = acc_skip + grad_skip
        input_grads.append((cot_f + grad_field_tok.astype(jnp.float32)).astype(jnp.bfloat16))
    summed_w_in, summed_b_in, summed_w_out, summed_rate, summed_freq, summed_coef, summed_skip = (
        lax.psum((acc_w_in, acc_b_in, acc_w_out, acc_rate, acc_freq, acc_coef, acc_skip), "dp")
    )
    summed_gain, summed_bias, summed_scale, summed_b_out = lax.psum(
        (acc_gain, acc_bias, acc_scale, acc_b_out), ("dp", "mp")
    )
    return (
        jnp.stack(outputs),
        jnp.stack(input_grads),
        summed_rate,
        summed_freq,
        summed_coef,
        summed_skip,
        summed_gain,
        summed_bias,
        summed_w_in,
        summed_b_in,
        summed_w_out,
        summed_b_out,
        summed_scale,
    )


def solution(mesh):
    placed = (
        P(None, ("dp", "mp"), None, None),
        P(None, "dp"),
        P("mp"),
        P(None, "mp", None),
        P(None, "mp", None),
        P(None, "mp", None),
        P("mp"),
        P(),
        P(),
        P(None, "mp"),
        P("mp"),
        P("mp", None),
        P(),
        P(),
        P(None, ("dp", "mp"), None, None),
    )
    return jax.shard_map(
        on_device,
        mesh=mesh,
        in_specs=placed,
        out_specs=(
            P(None, ("dp", "mp"), None, None),
            P(None, ("dp", "mp"), None, None),
            P(None, "mp", None),
            P(None, "mp", None),
            P(None, "mp", None),
            P("mp"),
            P(),
            P(),
            P(None, "mp"),
            P("mp"),
            P("mp", None),
            P(),
            P(),
        ),
        check_vma=False,
    )
```

profile of v0, /device:TPU:0, one launch (start us, length us, event | category | flops | bytes accessed | tf_op | source)
XLA Modules:
  0.0 689.0 jit_solution(17211035120291493984)
XLA Ops:
  11.9 3.6 all-to-all-start.2
  16.3 24.5 %multiply_reduce_fusion.8 = (f32[2,192,18]{1,2,0:T(8,128)S(1)}, f32[2,192,18]{1,2,0:T(8,128)S(1)}, f32[2,192,18]{1,2,0:T(8,128)S(1)}) fusion(f32[2,192,64]{1,2,0:T(8,128)S(1)} %copy-done.66, f32[18]{0:T(128)S(1)} %iota_multiply_fusion.2, f32[2,192,64]{1,2,0:T(8,128)S(1)} %neg.85, f32[2,192,64]{1,2,0:T(8,128)S(1)} %copy-done.67, ...), kind=kLoop, calls=%fused_computation.146 | loop fusion | flops 6614784 | bytes 378072 | tf_op jit(solution)/shard_map/jvp()/reduce_sum | solution.py:32
  58.0 3.5 all-to-all-start
  68.2 5.7 copy.403
  73.9 5.7 copy.418
  79.7 7.8 %copy.432 = f32[4,192,18,18]{2,3,1,0:T(8,128)} copy(f32[4,192,18,18]{1,0,3,2:T(4,128)} %fusion.111) | data formatting | bytes 1990656 | tf_op jit(solution)/shard_map/jvp(nk,kcip->ncip)/dot_general | solution.py:47
  87.5 7.8 %copy.443 = f32[4,192,18,18]{2,3,1,0:T(8,128)} copy(f32[4,192,18,18]{1,0,3,2:T(4,128)} %fusion.109) | data formatting | bytes 1990656 | tf_op jit(solution)/shard_map/jvp(nk,kcip->ncip)/dot_general | solution.py:47
  95.3 7.6 %copy.406 = f32[4,192,18,18]{3,2,1,0:T(8,128)} copy(f32[4,192,18,18]{1,0,3,2:T(4,128)} %fusion.107) | data formatting | bytes 1990656 | tf_op jit(solution)/shard_map/jvp(nk,kcip->ncip)/dot_general | solution.py:48
  102.9 7.7 %copy.421 = f32[4,192,18,18]{3,2,1,0:T(8,128)} copy(f32[4,192,18,18]{1,0,3,2:T(4,128)} %fusion.105) | data formatting | bytes 1990656 | tf_op jit(solution)/shard_map/jvp(nk,kcip->ncip)/dot_general | solution.py:48
  110.6 13.4 %fusion.227 = f32[4,192,18,18]{3,2,1,0:T(8,128)} fusion(f32[4,192,18,18]{2,3,1,0:T(8,128)} %copy.432, bf16[4,192,18,18]{3,2,1,0:T(8,128)(2,1)} %copy.403), kind=kOutput, calls=%fused_computation.363 | convolution fusion | flops 53747712 | bytes 2488320 | tf_op jit(solution)/shard_map/jvp(ncip,ncpq->nciq)/dot_general | solution.py:52
  124.0 19.7 %fusion.228 = f32[4,192,18,18]{3,2,1,0:T(8,128)} fusion(f32[4,192,18,18]{3,2,1,0:T(8,128)} %fusion.227, f32[4,192,18,18]{3,2,1,0:T(8,128)S(1)} %bitcast.486), kind=kOutput, calls=%fused_computation.364 | convolution fusion | flops 53747712 | bytes 2985984 | tf_op jit(solution)/shard_map/jvp(nciq,ncjq->ncij)/dot_general | solution.py:53
  143.7 8.6 %copy.407 = f32[4,192,18,18]{1,0,3,2:T(4,128)} copy(f32[4,192,18,18]{3,2,1,0:T(8,128)} %fusion.228) | data formatting | bytes 1990656 | tf_op jit(solution)/shard_map/jvp(nciq,ncjq->ncij)/dot_general | solution.py:53
  152.3 13.4 %fusion.229 = f32[4,192,18,18]{3,2,1,0:T(8,128)} fusion(f32[4,192,18,18]{2,3,1,0:T(8,128)} %copy.443, bf16[4,192,18,18]{3,2,1,0:T(8,128)(2,1)} %copy.418), kind=kOutput, calls=%fused_computation.365 | convolution fusion | flops 53747712 | bytes 2488320 | tf_op jit(solution)/shard_map/jvp(ncip,ncpq->nciq)/dot_general | solution.py:52
  165.7 19.5 %fusion.230 = f32[4,192,18,18]{3,2,1,0:T(8,128)} fusion(f32[4,192,18,18]{3,2,1,0:T(8,128)} %fusion.229, f32[4,192,18,18]{3,2,1,0:T(8,128)S(1)} %bitcast.490), kind=kOutput, calls=%fused_computation.366 | convolution fusion | flops 53747712 | bytes 2985984 | tf_op jit(solution)/shard_map/jvp(nciq,ncjq->ncij)/dot_general | solution.py:53
  185.2 8.5 %copy.422 = f32[4,192,18,18]{1,0,3,2:T(4,128)} copy(f32[4,192,18,18]{3,2,1,0:T(8,128)} %fusion.230) | data formatting | bytes 1990656 | tf_op jit(solution)/shard_map/jvp(nciq,ncjq->ncij)/dot_general | solution.py:53
  199.1 3.5 all-to-all-start.3
  204.4 3.5 all-to-all-start.1
  221.1 20.9 %fusion.19 = (bf16[4,768,324]{1,2,0:T(8,128)(2,1)S(1)}, f32[4,768,324]{1,2,0:T(8,128)}, bf16[4,768,324]{1,2,0:T(8,128)(2,1)}, f32[4,768,324]{1,2,0:T(8,128)}, f32[4,324,768]{2,1,0:T(8,128)}) fusion(f32[768]{0:T(1024)S(1)} %copy-done.68, f32[4,324,768]{2,1,0:T(8,128)S(1)} %fusion.163, bf16[4,384,324]{1,2,0:T(8,128)(2,1)S(1)} %all_gather.12, ...), kind=kOutput, calls=%fused_computation.35 | convolution fusion | flops 895795200 | bytes 21494784 | tf_op jit(solution)/shard_map/ncp,cf->nfp/dot_general | solution.py:138
  245.6 3.8 fusion.90
  252.4 4.5 reduce-scatter.5.cloned.1.call-done
  256.9 12.5 %reduce-scatter.7.cloned.1.call-done = bf16[2,384,324]{1,2,0:T(8,128)(2,1)} async-done(((bf16[4,384,324]{1,2,0:T(8,128)(2,1)}), bf16[2,384,324]{1,2,0:T(8,128)(2,1)}) %reduce-scatter.7.cloned.1.call-update) | async-done | bytes 497680 | tf_op jit(solution)/shard_map/reduce_scatter | solution.py:145
  269.4 3.8 fusion.124
  275.8 4.4 convert_reduce_fusion
  286.4 5.1 convert_reduce_fusion.1
  315.3 4.4 all_to_all.102
  321.4 5.5 copy.457
  327.0 15.3 %fusion.233 = f32[4,192,18,18]{3,2,1,0:T(8,128)} fusion(bf16[4,192,18,18]{2,3,1,0:T(8,128)(2,1)} %copy.457, f32[4,192,18,18]{3,2,1,0:T(8,128)} %copy.421), kind=kOutput, calls=%fused_computation.369 | convolution fusion | flops 53747712 | bytes 2488320 | tf_op jit(solution)/shard_map/transpose(jvp(nciq,ncjq->ncij))/dot_general | solution.py:53
  342.3 12.4 %fusion.237 = f32[4,192,18,18]{3,2,1,0:T(8,128)} fusion(bf16[4,192,18,18]{2,3,1,0:T(8,128)(2,1)S(1)} %copy-done.2, f32[4,192,18,18]{3,2,1,0:T(8,128)} %fusion.229), kind=kOutput, calls=%fused_computation.373 | convolution fusion | flops 53747712 | bytes 2488320 | tf_op jit(solution)/shard_map/transpose(jvp(nciq,ncjq->ncij))/dot_general | solution.py:53
  354.7 19.2 %fusion.234 = f32[4,192,18,18]{3,2,1,0:T(8,128)} fusion(f32[4,192,18,18]{2,3,1,0:T(8,128)S(1)} %bitcast.488, f32[4,192,18,18]{3,2,1,0:T(8,128)} %fusion.233), kind=kOutput, calls=%fused_computation.370 | convolution fusion | flops 53747712 | bytes 2985984 | tf_op jit(solution)/shard_map/transpose(jvp(ncip,ncpq->nciq))/dot_general | solution.py:52
  374.0 12.5 %fusion.238 = f32[4,192,18,18]{3,2,1,0:T(8,128)} fusion(f32[4,192,18,18]{3,2,1,0:T(8,128)} %fusion.233, bf16[4,192,18,18]{3,2,1,0:T(8,128)(2,1)S(1)} %bitcast.494), kind=kOutput, calls=%fused_computation.374 | convolution fusion | flops 53747712 | bytes 2488320 | tf_op jit(solution)/shard_map/transpose(jvp(ncip,ncpq->nciq))/dot_general | solution.py:52
  386.5 8.1 %copy.458 = f32[4,192,18,18]{1,0,3,2:T(4,128)S(1)} copy(f32[4,192,18,18]{3,2,1,0:T(8,128)} %fusion.237) | data formatting | bytes 1990656 | tf_op jit(solution)/shard_map/transpose(jvp(nciq,ncjq->ncij))/dot_general | solution.py:53
  396.1 8.9 %copy.461 = f32[4,192,18,18]{1,0,3,2:T(4,128)} copy(f32[4,192,18,18]{3,2,1,0:T(8,128)} %fusion.238) | data formatting | bytes 1990656 | tf_op jit(solution)/shard_map/transpose(jvp(ncip,ncpq->nciq))/dot_general | solution.py:52
  410.9 4.2 all_to_all.103
  416.9 5.6 copy.448
  422.5 15.2 %fusion.231 = f32[4,192,18,18]{3,2,1,0:T(8,128)} fusion(bf16[4,192,18,18]{2,3,1,0:T(8,128)(2,1)} %copy.448, f32[4,192,18,18]{3,2,1,0:T(8,128)} %copy.406), kind=kOutput, calls=%fused_computation.367 | convolution fusion | flops 53747712 | bytes 2488320 | tf_op jit(solution)/shard_map/transpose(jvp(nciq,ncjq->ncij))/dot_general | solution.py:53
  437.7 10.0 %fusion.235 = f32[4,192,18,18]{3,2,1,0:T(8,128)} fusion(bf16[4,192,18,18]{2,3,1,0:T(8,128)(2,1)S(1)} %copy-done.3, f32[4,192,18,18]{3,2,1,0:T(8,128)S(1)} %bitcast.492), kind=kOutput, calls=%fused_computation.371 | convolution fusion | flops 53747712 | bytes 2488320 | tf_op jit(solution)/shard_map/transpose(jvp(nciq,ncjq->ncij))/dot_general | solution.py:53
  447.7 8.1 %copy.449 = f32[4,192,18,18]{1,0,3,2:T(4,128)S(1)} copy(f32[4,192,18,18]{3,2,1,0:T(8,128)} %fusion.235) | data formatting | bytes 1990656 | tf_op jit(solution)/shard_map/transpose(jvp(nciq,ncjq->ncij))/dot_general | solution.py:53
  457.4 13.1 %fusion.236 = f32[4,192,18,18]{3,2,1,0:T(8,128)} fusion(f32[4,192,18,18]{3,2,1,0:T(8,128)} %fusion.231, bf16[4,192,18,18]{3,2,1,0:T(8,128)(2,1)} %copy.403), kind=kOutput, calls=%fused_computation.372 | convolution fusion | flops 53747712 | bytes 2488320 | tf_op jit(solution)/shard_map/transpose(jvp(ncip,ncpq->nciq))/dot_general | solution.py:52
  470.5 8.5 %copy.452 = f32[4,192,18,18]{1,0,3,2:T(4,128)} copy(f32[4,192,18,18]{3,2,1,0:T(8,128)} %fusion.236) | data formatting | bytes 1990656 | tf_op jit(solution)/shard_map/transpose(jvp(ncip,ncpq->nciq))/dot_general | solution.py:52
  485.3 8.2 %copy.444 = f32[4,192,18,18]{1,0,3,2:T(4,128)S(1)} copy(f32[4,192,18,18]{3,2,1,0:T(8,128)} %fusion.234) | data formatting | bytes 1990656 | tf_op jit(solution)/shard_map/transpose(jvp(ncip,ncpq->nciq))/dot_general | solution.py:52
  493.5 34.1 %fusion.58 = (f32[2,192,64]{1,2,0:T(8,128)S(1)}, f32[2,192,64]{1,2,0:T(8,128)S(1)}, f32[2,192,64]{1,2,0:T(8,128)S(1)}, f32[2,192,64]{1,2,0:T(8,128)S(1)}, f32[2,...) fusion(f32[2,192,18]{1,2,0:T(8,128)} %fusion.117, ...), kind=kLoop, calls=%fused_computation.105 | loop fusion | flops 35389440 | bytes 2230488 | tf_op jit(solution)/shard_map/transpose(jvp())/reduce_sum | solution.py:30
  529.8 21.5 %fusion.232 = f32[4,192,18,18]{3,2,1,0:T(8,128)} fusion(f32[4,192,18,18]{2,3,1,0:T(8,128)} %copy.432, f32[4,192,18,18]{3,2,1,0:T(8,128)} %fusion.231), kind=kOutput, calls=%fused_computation.368 | convolution fusion | flops 53747712 | bytes 2985984 | tf_op jit(solution)/shard_map/transpose(jvp(ncip,ncpq->nciq))/dot_general | solution.py:52
  551.2 8.6 %copy.433 = f32[4,192,18,18]{1,0,3,2:T(4,128)} copy(f32[4,192,18,18]{3,2,1,0:T(8,128)} %fusion.232) | data formatting | bytes 1990656 | tf_op jit(solution)/shard_map/transpose(jvp(ncip,ncpq->nciq))/dot_general | solution.py:52
  566.8 4.2 all_to_all.104
  571.0 3.8 all-to-all-start.7
  584.0 40.8 %all-reduce.4 = (f32[384]{0:T(512)}, f32[384]{0:T(512)}, f32[384]{0:T(512)}, f32[384]{0:T(512)}) all-reduce(f32[384]{0:T(512)S(1)} %add.225, f32[384]{0:T(512)S(1)} %add.226, f32[384]{0:T(512)S(1)} %add.230, f32[384]{0:T(512)S(1)} %add.231), channel_id=1, replica_groups=mesh['dp'=16,'mp'=2] {'dp','mp'}, use_global_device_ids=true, to_apply=%region_41.42 | all-reduce | flops 1536 | bytes 12288 | tf_op jit(solution)/shard_map/psum | solution.py:199
  624.8 42.9 %all-reduce.5 = (f32[192]{0:T(256)}, f32[768]{0:T(1024)}) all-reduce(f32[192]{0:T(256)S(1)} %add.224, f32[768]{0:T(1024)S(1)} %add.228), channel_id=1, replica_groups=mesh['dp'=16,'mp'=2] {'dp'}, use_global_device_ids=true, to_apply=%region_38.39 | all-reduce | flops 960 | bytes 7680 | tf_op jit(solution)/shard_map/psum | solution.py:197
  667.7 4.9 all-reduce.9.cloned.1.call-done
  (327 shorter events, 134.2 us)
Async XLA Ops:
  7.2 212.7 %copy-start = (bf16[384,768]{1,0:T(8,128)(2,1)S(1)}, bf16[384,768]{1,0:T(8,128)(2,1)}, u32[]{:S(2)}) copy-start(bf16[384,768]{1,0:T(8,128)(2,1)} %param.32) | copy-start | bytes 1769476
  9.2 47.0 %copy-start.21 = (bf16[1,2,384,324]{2,1,3,0:T(2,128)(2,1)}, bf16[1,2,384,324]{2,1,3,0:T(2,128)(2,1)S(1)}, u32[]{:S(2)}) copy-start(bf16[1,2,384,324]{2,1,3,0:T(2,128)(2,1)S(1)} %get-tuple-element.159) | copy-start | bytes 1492996
  10.1 30.8 %copy-start.4 = (f32[18,18,18,1]{0,2,1,3:T(8,128)S(1)}, f32[18,18,18,1]{0,2,1,3:T(8,128)}, u32[]{:S(2)}) copy-start(f32[18,18,18,1]{0,2,1,3:T(8,128)} %constant.159) | copy-start | bytes 69988
  11.9 29.9 %copy-start.42 = (f32[18,18]{1,0:T(8,128)S(1)}, f32[18,18]{1,0:T(8,128)}, u32[]{:S(2)}) copy-start(f32[18,18]{1,0:T(8,128)} %constant.145.clone) | copy-start | bytes 3892
  11.9 46.1 %all-to-all-start.2 = ((bf16[2,384,324]{2,0,1:T(2,128)(2,1)}), bf16[2,384,324]{2,0,1:T(2,128)(2,1)S(1)}, u32[]{:S(2)}, u32[]{:S(2)}) async-start(bf16[2,384,324]{2,0,1:T(2,128)(2,1)} %copy.414), calls=%async_computation.3 | async-start | bytes 1179648 | tf_op jit(solution)/shard_map/all_to_all | solution.py:121
  15.5 27.1 %copy-start.40 = (f32[18,18]{1,0:T(8,128)S(1)}, f32[18,18]{1,0:T(8,128)}, u32[]{:S(2)}) copy-start(f32[18,18]{1,0:T(8,128)} %constant.146.clone) | copy-start | bytes 3892
  15.5 27.0 %copy-start.73 = (f32[18]{0:T(128)}, f32[18]{0:T(128)S(1)}, u32[]{:S(2)}) copy-start(f32[18]{0:T(128)S(1)} %iota_multiply_fusion.2) | copy-start | bytes 220
  15.6 27.0 %copy-start.69 = (f32[18]{0:T(128)}, f32[18]{0:T(128)S(1)}, u32[]{:S(2)}) copy-start(f32[18]{0:T(128)S(1)} %get-tuple-element.193) | copy-start | bytes 220
  15.6 27.0 %copy-start.71 = (f32[18]{0:T(128)}, f32[18]{0:T(128)S(1)}, u32[]{:S(2)}) copy-start(f32[18]{0:T(128)S(1)} %get-tuple-element.194) | copy-start | bytes 220
  16.1 34.1 %copy-start.53 = (s32[4]{0:T(128)}, s32[4]{0:T(128)S(1)}, u32[]{:S(2)}) copy-start(s32[4]{0:T(128)S(1)} %get-tuple-element.181) | copy-start | bytes 52
  16.2 37.1 %copy-start.51 = (s32[4]{0:T(128)}, s32[4]{0:T(128)S(1)}, u32[]{:S(2)}) copy-start(s32[4]{0:T(128)S(1)} %get-tuple-element.180) | copy-start | bytes 52
  16.2 26.4 %copy-start.38 = (f32[2,192,64]{1,2,0:T(8,128)}, f32[2,192,64]{1,2,0:T(8,128)S(1)}, u32[]{:S(2)}) copy-start(f32[2,192,64]{1,2,0:T(8,128)S(1)} %neg.85) | copy-start | bytes 294916
  16.3 27.2 %copy-start.44 = (pred[192,18]{0,1:T(8,128)(4,1)}, pred[192,18]{0,1:T(8,128)(4,1)S(1)}, u32[]{:S(2)}) copy-start(pred[192,18]{0,1:T(8,128)(4,1)S(1)} %get-tuple-element.187) | copy-start | bytes 10372
  16.3 27.2 %copy-start.46 = (pred[192,18]{0,1:T(8,128)(4,1)}, pred[192,18]{0,1:T(8,128)(4,1)S(1)}, u32[]{:S(2)}) copy-start(pred[192,18]{0,1:T(8,128)(4,1)S(1)} %get-tuple-element.185) | copy-start | bytes 10372
  16.3 27.2 %copy-start.48 = (pred[192,18]{0,1:T(8,128)(4,1)}, pred[192,18]{0,1:T(8,128)(4,1)S(1)}, u32[]{:S(2)}) copy-start(pred[192,18]{0,1:T(8,128)(4,1)S(1)} %get-tuple-element.186) | copy-start | bytes 10372
  58.0 5.3 all-to-all-start
  102.9 21.1 %slice-start = ((s8[9437184]{0:T(1024)(128)(4,1)}), s8[1048576]{0:T(1024)(128)(4,1)S(1)}, s32[]{:S(2)}) async-start(s8[9437184]{0:T(1024)(128)(4,1)} %bitcast.485), calls=%async_computation.17 | async-start | bytes 2097152
  110.6 13.4 %slice-start.1 = ((s8[9437184]{0:T(1024)(128)(4,1)}), s8[4194304]{0:T(1024)(128)(4,1)S(1)}, s32[]{:S(2)}) async-start(s8[9437184]{0:T(1024)(128)(4,1)} %bitcast.485), calls=%async_computation.18 | async-start | bytes 8388608
  110.6 13.4 %slice-start.2 = ((s8[9437184]{0:T(1024)(128)(4,1)}), s8[4194304]{0:T(1024)(128)(4,1)S(1)}, s32[]{:S(2)}) async-start(s8[9437184]{0:T(1024)(128)(4,1)} %bitcast.485), calls=%async_computation.19 | async-start | bytes 8388608
  143.7 22.0 %slice-start.6 = ((s8[9437184]{0:T(1024)(128)(4,1)}), s8[1048576]{0:T(1024)(128)(4,1)S(1)}, s32[]{:S(2)}) async-start(s8[9437184]{0:T(1024)(128)(4,1)} %bitcast.489), calls=%async_computation.23 | async-start | bytes 2097152
  152.3 13.4 %slice-start.7 = ((s8[9437184]{0:T(1024)(128)(4,1)}), s8[4194304]{0:T(1024)(128)(4,1)S(1)}, s32[]{:S(2)}) async-start(s8[9437184]{0:T(1024)(128)(4,1)} %bitcast.489), calls=%async_computation.24 | async-start | bytes 8388608
  152.3 13.4 %slice-start.8 = ((s8[9437184]{0:T(1024)(128)(4,1)}), s8[4194304]{0:T(1024)(128)(4,1)S(1)}, s32[]{:S(2)}) async-start(s8[9437184]{0:T(1024)(128)(4,1)} %bitcast.489), calls=%async_computation.25 | async-start | bytes 8388608
  199.1 5.3 all-to-all-start.3
  204.4 5.3 all-to-all-start.1
  207.9 49.0 %reduce-scatter.5.cloned.1.call-start = ((), (), s32[]{:S(2)}) async-start(), calls=%async_computation.12 | async-start | bytes 1511424 | tf_op jit(solution)/shard_map/reduce_scatter | solution.py:145
  216.4 25.6 %copy-start.23 = (bf16[4,384,324]{1,2,0:T(8,128)(2,1)}, bf16[4,384,324]{1,2,0:T(8,128)(2,1)S(1)}, u32[]{:S(2)}) copy-start(bf16[4,384,324]{1,2,0:T(8,128)(2,1)S(1)} %all_gather.12) | copy-start | bytes 2985988
  221.1 20.9 %copy-start.25 = (f32[4,324,768]{2,1,0:T(8,128)}, f32[4,324,768]{2,1,0:T(8,128)S(1)}, u32[]{:S(2)}) copy-start(f32[4,324,768]{2,1,0:T(8,128)S(1)} %fusion.163) | copy-start | bytes 11943940
  221.1 22.2 %copy-start.64 = (bf16[768,384]{1,0:T(8,128)(2,1)S(1)}, bf16[768,384]{1,0:T(8,128)(2,1)}, u32[]{:S(2)}) copy-start(bf16[768,384]{1,0:T(8,128)(2,1)} %param.34) | copy-start | bytes 1769476
  245.5 23.9 %copy-start.58 = (f32[384]{0:T(512)S(1)}, f32[384]{0:T(512)}, u32[]{:S(2)}) copy-start(f32[384]{0:T(512)} %param.35) | copy-start | bytes 4612
  245.5 23.9 %copy-start.59 = (f32[384]{0:T(512)S(1)}, f32[384]{0:T(512)}, u32[]{:S(2)}) copy-start(f32[384]{0:T(512)} %param.36) | copy-start | bytes 4612
  245.5 23.9 %reduce-scatter.7.cloned.1.call-start = ((), (), s32[]{:S(2)}) async-start(), calls=%async_computation.13 | async-start | bytes 1511424 | tf_op jit(solution)/shard_map/reduce_scatter | solution.py:145
  249.4 57.7 %reduce-scatter.11.cloned.1.call-start = ((), (), s32[]{:S(2)}) async-start(), calls=%async_computation.15 | async-start | bytes 1511424 | tf_op jit(solution)/shard_map/reduce_scatter | solution.py:171
  252.4 27.8 %copy-start.18 = (bf16[1,2,384,324]{2,1,3,0:T(2,128)(2,1)}, bf16[1,2,384,324]{2,1,3,0:T(2,128)(2,1)S(1)}, u32[]{:S(2)}) copy-start(bf16[1,2,384,324]{2,1,3,0:T(2,128)(2,1)S(1)} %get-tuple-element.158) | copy-start | bytes 1492996
  283.8 23.4 %reduce-scatter.9.cloned.1.call-start = ((), (), s32[]{:S(2)}) async-start(), calls=%async_computation.14 | async-start | bytes 1511424 | tf_op jit(solution)/shard_map/reduce_scatter | solution.py:171
  295.1 377.5 %all-reduce.9.cloned.1.call-start = ((), (), s32[]{:S(2)}) async-start(), calls=%async_computation.16 | async-start | bytes 5505024 | tf_op jit(solution)/shard_map/psum | solution.py:197
  319.8 22.5 %copy-start.12 = (bf16[2,384,324]{2,1,0:T(8,128)(2,1)}, bf16[2,384,324]{2,1,0:T(8,128)(2,1)S(1)}, u32[]{:S(2)}) copy-start(bf16[2,384,324]{2,1,0:T(8,128)(2,1)S(1)} %copy.439) | copy-start | bytes 1492996
  327.0 15.3 %copy-start.2 = (bf16[4,192,18,18]{2,3,1,0:T(8,128)(2,1)S(1)}, bf16[4,192,18,18]{2,3,1,0:T(8,128)(2,1)}, u32[]{:S(2)}) copy-start(bf16[4,192,18,18]{2,3,1,0:T(8,128)(2,1)} %copy.457) | copy-start | bytes 1492996
  327.0 27.7 %slice-start.3 = ((s8[9437184]{0:T(1024)(128)(4,1)}), s8[4194304]{0:T(1024)(128)(4,1)S(1)}, s32[]{:S(2)}) async-start(s8[9437184]{0:T(1024)(128)(4,1)} %bitcast.487), calls=%async_computation.20 | async-start | bytes 8388608
  327.0 27.7 %slice-start.4 = ((s8[9437184]{0:T(1024)(128)(4,1)}), s8[4194304]{0:T(1024)(128)(4,1)S(1)}, s32[]{:S(2)}) async-start(s8[9437184]{0:T(1024)(128)(4,1)} %bitcast.487), calls=%async_computation.21 | async-start | bytes 8388608
  342.2 12.4 %slice-start.5 = ((s8[9437184]{0:T(1024)(128)(4,1)}), s8[1048576]{0:T(1024)(128)(4,1)S(1)}, s32[]{:S(2)}) async-start(s8[9437184]{0:T(1024)(128)(4,1)} %bitcast.487), calls=%async_computation.22 | async-start | bytes 2097152
  342.3 31.7 %slice-start.12 = ((s8[4718592]{0:T(1024)(128)(4,1)}), s8[4194304]{0:T(1024)(128)(4,1)S(1)}, s32[]{:S(2)}) async-start(s8[4718592]{0:T(1024)(128)(4,1)} %bitcast.493), calls=%async_computation.29 | async-start | bytes 8388608
  354.7 19.2 %slice-start.13 = ((s8[4718592]{0:T(1024)(128)(4,1)}), s8[524288]{0:T(1024)(128)(4,1)S(1)}, s32[]{:S(2)}) async-start(s8[4718592]{0:T(1024)(128)(4,1)} %bitcast.493), calls=%async_computation.30 | async-start | bytes 1048576
  416.9 20.8 %slice-start.9 = ((s8[9437184]{0:T(1024)(128)(4,1)}), s8[1048576]{0:T(1024)(128)(4,1)S(1)}, s32[]{:S(2)}) async-start(s8[9437184]{0:T(1024)(128)(4,1)} %bitcast.491), calls=%async_computation.26 | async-start | bytes 2097152
  422.5 15.2 %slice-start.10 = ((s8[9437184]{0:T(1024)(128)(4,1)}), s8[4194304]{0:T(1024)(128)(4,1)S(1)}, s32[]{:S(2)}) async-start(s8[9437184]{0:T(1024)(128)(4,1)} %bitcast.491), calls=%async_computation.27 | async-start | bytes 8388608
  422.5 15.2 %slice-start.11 = ((s8[9437184]{0:T(1024)(128)(4,1)}), s8[4194304]{0:T(1024)(128)(4,1)S(1)}, s32[]{:S(2)}) async-start(s8[9437184]{0:T(1024)(128)(4,1)} %bitcast.491), calls=%async_computation.28 | async-start | bytes 8388608
  422.5 15.2 %copy-start.3 = (bf16[4,192,18,18]{2,3,1,0:T(8,128)(2,1)S(1)}, bf16[4,192,18,18]{2,3,1,0:T(8,128)(2,1)}, u32[]{:S(2)}) copy-start(bf16[4,192,18,18]{2,3,1,0:T(8,128)(2,1)} %copy.448) | copy-start | bytes 1492996
  571.0 5.6 all-to-all-start.7
  581.7 100.3 %copy-start.1 = (bf16[384,768]{1,0:T(8,128)(2,1)S(1)}, bf16[384,768]{1,0:T(8,128)(2,1)}, u32[]{:S(2)}) copy-start(bf16[384,768]{1,0:T(8,128)(2,1)} %param.32) | copy-start | bytes 1769476
  (54 other events, 253.8 us)
Sparse Core Ops, SparseCore 0:
  245.6 11.2 reduce-scatter.4
  259.7 9.6 reduce-scatter.6
  283.9 9.6 reduce-scatter.10
  295.7 9.6 reduce-scatter.8
  529.9 142.6 all-reduce.8
where the time goes:
time: 700 us; the launch traced here: 689 us
  matrix products  264 us (38%)
  local copies, waits for them, and re-layouts  176 us (25%)
  blocking collectives  107 us (15%)
  other arithmetic  83.6 us (12%)
  waiting for transfers between devices  25.1 us (4%)
  starting transfers between devices  18.5 us (3%)
  between operations  15.7 us (2%)
    dot_general x6, matrix products, mix_channels(): jnp.einsum('ncip,ncpq->nciq', rows_op, grid_view, precision=HIGH)  93.1 us
    dot_general x6, matrix products, mix_channels(): jnp.einsum('nciq,ncjq->ncij', partial_rows, cols_op, precision=HIGH)  92 us
    psum x1, blocking collectives, on_device(): lax.psum((acc_w_in, acc_b_in, acc_w_out, acc_rate, acc_freq, acc_coef, ac...  42.9 us
    psum x1, blocking collectives, on_device(): lax.psum((acc_gain, acc_bias, acc_scale, acc_b_out), ('dp', 'mp'))  40.8 us
    dot_general x4, local copies, waits for them, and re-layouts, mix_channels(): jnp.einsum('ncip,ncpq->nciq', rows_op, grid_view, precision=HIGH)  34.1 us
    reduce_sum x1, other arithmetic, kernel_tables(): frequency[..., None] * scaled  34.1 us
    dot_general x4, local copies, waits for them, and re-layouts, mix_channels(): jnp.einsum('nciq,ncjq->ncij', partial_rows, cols_op, precision=HIGH)  33.2 us
    reduce_sum x1, other arithmetic, kernel_tables(): kernel_row = jnp.sum(coef_in[..., None] * wave_terms, axis=2)  24.5 us
  transfers between devices with their start and end apart: 10, of which 6 were waited for; matrix products, arithmetic and copies ran while one was open for 17% of the time, Pallas kernels for 0%

commit v1 on v0

v1 whole, which is shorter than its diff:
```python
import math
from functools import partial

import jax
import jax.numpy as jnp
import numpy as np
from jax import lax
from jax.experimental import pallas as pl
from jax.experimental.pallas import tpu as pltpu
from jax.sharding import PartitionSpec as P

GRID = 18
HALF = 9
SIDES = (10, 14, 18)
LAGS = 3 * GRID
F32 = jnp.float32
BF16 = jnp.bfloat16

ERF_SHIFT = 0.35 / math.sqrt(2.0)
ERF_POLY = (
    0.19396706,
    0.23864529,
    -0.01708609,
    0.69839275,
    -0.6929918,
    0.77818103,
    -0.19910822,
)
VMEM_LIMIT = 60 * 1024 * 1024


def small_sincos(angle):
    sq = angle * angle
    cos = 1.0 + sq * (
        -1 / 2 + sq * (1 / 24 + sq * (-1 / 720 + sq * (1 / 40320 + sq * (-1 / 3628800))))
    )
    sin = angle * (
        1.0
        + sq * (-1 / 6 + sq * (1 / 120 + sq * (-1 / 5040 + sq * (1 / 362880 + sq * (-1 / 39916800)))))
    )
    return sin, cos


def mode_step(rate, freq, side):
    decay = jnp.exp(rate * (-1.0 / side))
    sin, cos = small_sincos(freq * (1.0 / side))
    return decay * cos, decay * sin


def tables_kernel(extent_ref, rate_ref, freq_ref, coef_ref, out_ref):
    for axis in range(2):
        for cat, side in enumerate(SIDES):
            z_re, z_im = mode_step(rate_ref[axis], freq_ref[axis], side)
            w_re = coef_ref[axis]
            w_im = jnp.zeros_like(w_re)
            for lag in range(GRID):
                row = cat * GRID + lag
                if lag >= side:
                    out_ref[axis, row : row + 1, :] = jnp.zeros((1, w_re.shape[1]), F32)
                    continue
                total = jnp.sum(w_re, axis=0, keepdims=True)
                out_ref[axis, row : row + 1, :] = jnp.where(extent_ref[...] > lag, total, 0.0)
                if lag < side - 1:
                    w_re, w_im = w_re * z_re - w_im * z_im, w_re * z_im + w_im * z_re


def modes_grad_kernel(extent_ref, rate_ref, freq_ref, coef_ref, dk_ref, rate_out, freq_out, coef_out):
    for axis in range(2):
        coef = coef_ref[axis]
        g_rate = jnp.zeros_like(coef)
        g_freq = jnp.zeros_like(coef)
        g_coef = jnp.zeros_like(coef)
        for cat, side in enumerate(SIDES):
            z_re, z_im = mode_step(rate_ref[axis], freq_ref[axis], side)
            p_re = jnp.zeros_like(coef)
            p_im = jnp.zeros_like(coef)
            q_re = jnp.zeros_like(coef)
            q_im = jnp.zeros_like(coef)
            for lag in reversed(range(side)):
                row = cat * GRID + lag
                d = jnp.where(extent_ref[...] > lag, dk_ref[axis, row : row + 1, :], 0.0)
                p_re, p_im = p_re * z_re - p_im * z_im + d, p_re * z_im + p_im * z_re
                q_re, q_im = q_re * z_re - q_im * z_im + float(lag) * d, q_re * z_im + q_im * z_re
            g_coef = g_coef + p_re
            g_rate = g_rate - (1.0 / side) * q_re
            g_freq = g_freq - (1.0 / side) * q_im
        coef_out[axis] = g_coef
        rate_out[axis] = g_rate * coef
        freq_out[axis] = g_freq * coef


def tri(a, b):
    low, high = min(a, b), max(a, b)
    return low * HALF - low * (low - 1) // 2 + (high - low)


def rows8(index):
    if isinstance(index, int):
        return pl.ds(index * 8, 8)
    return pl.ds(pl.multiple_of(index * 8, 8), 8)


def lanes(tile):
    if isinstance(tile, int):
        return pl.ds(tile * 128, 128)
    return pl.ds(pl.multiple_of(tile * 128, 128), 128)


def swap(value):
    return pltpu.roll(value, 4, 0)


def sublane_half():
    return lax.broadcasted_iota(jnp.int32, (8, 128), 0) < 4


def side_vreg(class_ref):
    mine = lax.axis_index("mp")
    image = lax.rem(lax.broadcasted_iota(jnp.int32, (8, 128), 0), 4)
    cls = jnp.zeros((8, 128), jnp.int32)
    own = class_ref.shape[1] // 2
    for micro in range(2):
        for img in range(2):
            cls = jnp.where(image == micro * 2 + img, class_ref[micro, mine * own + img], cls)
    return 10 + 4 * cls


def build_masks(class_ref, mask_ref):
    side = side_vreg(class_ref)
    offset = jnp.where(sublane_half(), 0, 1)

    def row(i, carry):
        for pair in range(HALF):
            ok = (i < side) & (2 * pair + offset < side)
            mask_ref[rows8(i * HALF + pair), :] = jnp.where(ok, 1.0, 0.0).astype(F32)
        return carry

    lax.fori_loop(0, GRID, row, 0)


def build_operators(class_ref, table_ref, lag_ref, rowop_ref, colop_ref):
    side = side_vreg(class_ref)
    sign = jnp.where(sublane_half(), 1.0, -1.0).astype(F32)
    tiles = table_ref.shape[2] // 128

    def tile_body(tile, carry):
        at = lanes(tile)
        for axis in range(2):
            for lag in range(GRID):
                by_side = [
                    jnp.broadcast_to(table_ref[axis, cat * GRID + lag : cat * GRID + lag + 1, at], (8, 128))
                    for cat in range(3)
                ]
                lag_ref[axis * GRID + lag, :, at] = 0.5 * jnp.where(
                    side == 10, by_side[0], jnp.where(side == 14, by_side[1], by_side[2])
                )
        for a in range(HALF):
            for b in range(a, HALF):
                near = lag_ref[b - a, :, at]
                far = lag_ref[GRID - 1 - a - b, :, at]
                rowop_ref[tri(a, b), :, at] = near + far
                rowop_ref[45 + tri(a, b), :, at] = near - far
                near = lag_ref[GRID + b - a, :, at]
                far = lag_ref[GRID + GRID - 1 - a - b, :, at]
                colop_ref[tri(a, b), :, at] = near + sign * far
        return carry

    lax.fori_loop(0, tiles, tile_body, 0)


def mirror_in(source_ref, mask_ref, out_ref):
    half = sublane_half()
    sign = jnp.where(half, 1.0, -1.0).astype(F32)
    tiles = source_ref.shape[1] // 128

    def body(i, carry):
        for tile in range(tiles):
            at = lanes(tile)

            def mirrored(row, pair):
                near = source_ref[rows8(row * HALF + pair), at] * mask_ref[rows8(row * HALF + pair), :]
                if pair == 4:
                    return swap(near) + sign * near, None
                other = row * HALF + 8 - pair
                far = source_ref[rows8(other), at] * mask_ref[rows8(other), :]
                even = jnp.where(half, near, far)
                odd = jnp.where(half, far, near)
                return swap(even) + sign * even, odd + sign * swap(odd)

            for pair in range(5):
                top = mirrored(i, pair)
                bottom = mirrored(GRID - 1 - i, pair)
                for step in range(2 if pair < 4 else 1):
                    where = i * HALF + 2 * pair + step
                    out_ref[rows8(where), at] = top[step] + bottom[step]
                    out_ref[rows8(81 + where), at] = top[step] - bottom[step]
        return carry

    lax.fori_loop(0, HALF, body, 0)


def mirror_out(source_ref, mask_ref, out_ref, extra_ref, gain_ref):
    half = sublane_half()
    sign = jnp.where(half, 1.0, -1.0).astype(F32)
    tiles = source_ref.shape[1] // 128

    def body(i, carry):
        for tile in range(tiles):
            at = lanes(tile)
            gain = jnp.broadcast_to(gain_ref[:, at], (8, 128))

            def finish(index, value):
                value = value * mask_ref[rows8(index), :] + gain * extra_ref[rows8(index), at]
                out_ref[rows8(index), at] = value.astype(BF16).astype(F32)

            for pair in range(5):
                both = []
                for step in range(2 if pair < 4 else 1):
                    where = i * HALF + 2 * pair + step
                    plus = source_ref[rows8(where), at]
                    minus = source_ref[rows8(81 + where), at]
                    top, bottom = plus + minus, plus - minus
                    both.append(
                        (swap(top) + sign * top, swap(bottom) + sign * bottom)
                        if step == 0
                        else (top - sign * swap(top), bottom - sign * swap(bottom))
                    )
                for part, row in ((0, i), (1, GRID - 1 - i)):
                    if pair == 4:
                        finish(row * HALF + 4, both[0][part])
                        continue
                    if True:
                        even, odd = both[0][part], both[1][part]
                        finish(row * HALF + pair, jnp.where(half, even, odd))
                        finish(row * HALF + 8 - pair, jnp.where(half, odd, even))
        return carry

    lax.fori_loop(0, HALF, body, 0)


def apply_rows(op_ref, source_ref, out_ref):
    tiles = source_ref.shape[1] // 128

    def body(j, carry):
        for tile in range(tiles):
            at = lanes(tile)
            for rho in range(2):
                values = [source_ref[rows8(rho * 81 + p * HALF + j), at] for p in range(HALF)]
                for i in range(HALF):
                    total = None
                    for p in range(HALF):
                        term = op_ref[rho * 45 + tri(i, p), :, at] * values[p]
                        total = term if total is None else total + term
                    out_ref[rows8(rho * 81 + i * HALF + j), at] = total
        return carry

    lax.fori_loop(0, HALF, body, 0)


def apply_cols(op_ref, source_ref, out_ref):
    tiles = source_ref.shape[1] // 128

    def body(i, carry):
        for tile in range(tiles):
            at = lanes(tile)
            values = [source_ref[rows8(i * HALF + q), at] for q in range(HALF)]
            for j in range(HALF):
                total = None
                for q in range(HALF):
                    term = op_ref[tri(j, q), :, at] * values[q]
                    total = term if total is None else total + term
                out_ref[rows8(i * HALF + j), at] = total
        return carry

    lax.fori_loop(0, 2 * HALF, body, 0)


def front_kernel(
    class_ref,
    table_ref,
    x_ref,
    cot_ref,
    skip_ref,
    gain_ref,
    bias_ref,
    w_in_ref,
    b_in_ref,
    w_out_ref,
    b_out_ref,
    scale_ref,
    block_out,
    gm_out,
    u_out,
    uh_out,
    v_out,
    rowop_out,
    colop_out,
    mask_out,
    dw_in_out,
    dw_out_out,
    db_in_out,
    small_out,
    lag_ref,
    mh_ref,
    mixed_ref,
    normed_ref,
    gmlp_ref,
    act_ref,
    gpre_ref,
    mlp_ref,
    gn_ref,
    stat_ref,
):
    rows, channels = x_ref.shape
    hidden = b_in_ref.shape[1]
    build_masks(class_ref, mask_out)
    build_operators(class_ref, table_ref, lag_ref, rowop_out, colop_out)

    block = 144

    def load(t, carry):
        at = pl.ds(pl.multiple_of(t * block, block), block)
        u_out[at, :] = x_ref[at, :].astype(F32)
        mask = jnp.tile(mask_out[at, :], (1, channels // 128))
        gmlp_ref[at, :] = (cot_ref[at, :].astype(F32) * scale_ref[...] * mask).astype(BF16)
        return carry

    lax.fori_loop(0, rows // block, load, 0)
    mirror_in(u_out, mask_out, uh_out)
    apply_rows(rowop_out, uh_out, v_out)
    apply_cols(colop_out, v_out, mh_ref)
    mirror_out(mh_ref, mask_out, mixed_ref, u_out, skip_ref)

    def norm(t, carry):
        at = pl.ds(pl.multiple_of(t * block, block), block)
        value = mixed_ref[at, :]
        mean = jnp.mean(value, axis=1, keepdims=True)
        centered = value - mean
        variance = jnp.mean(centered * centered, axis=1, keepdims=True)
        rstd = lax.rsqrt(variance + 1e-06)
        hat = centered * rstd
        mixed_ref[at, :] = hat
        stat_ref[at, :] = jnp.broadcast_to(rstd, (block, 128))
        normed_ref[at, :] = (hat * gain_ref[...] + bias_ref[...]).astype(BF16)
        return carry

    lax.fori_loop(0, rows // block, norm, 0)

    chunk = 256
    tile_rows = 432
    mlp_ref[...] = jnp.broadcast_to(b_out_ref[...], mlp_ref.shape)
    gn_ref[...] = jnp.zeros_like(gn_ref)

    def feed(f, carry):
        cols = pl.ds(pl.multiple_of(f * chunk, chunk), chunk)
        w_first = w_in_ref[:, cols]
        w_second = w_out_ref[cols, :]
        bias = b_in_ref[:, cols]
        db = jnp.zeros((1, chunk), F32)
        for t in range(rows // tile_rows):
            at = pl.ds(t * tile_rows, tile_rows)
            pre = jnp.dot(normed_ref[at, :], w_first, preferred_element_type=F32) + bias
            size = jnp.abs(pre)
            inv = 1.0 / (1.0 + ERF_SHIFT * size)
            poly = jnp.full_like(inv, 0.5 * ERF_POLY[-1])
            for value in reversed(ERF_POLY[:-1]):
                poly = poly * inv + 0.5 * value
            bell = jnp.exp(-0.5 * pre * pre)
            tail = poly * inv * bell
            cdf = jnp.where(pre >= 0.0, 1.0 - tail, tail)
            act = (pre * cdf).astype(BF16)
            slope = cdf + pre * bell * (1.0 / math.sqrt(2.0 * math.pi))
            g_act = lax.dot_general(
                gmlp_ref[at, :], w_second, (((1,), (1,)), ((), ())), preferred_element_type=F32
            )
            g_pre = (g_act * slope).astype(BF16)
            db = db + jnp.sum(g_pre.astype(F32), axis=0, keepdims=True)
            act_ref[at, :] = act
            gpre_ref[at, :] = g_pre
            mlp_ref[at, :] += jnp.dot(act, w_second, preferred_element_type=F32)
            gn_ref[at, :] += lax.dot_general(
                g_pre, w_first, (((1,), (1,)), ((), ())), preferred_element_type=F32
            )
        db_in_out[:, cols] = db
        dw_in_out[:, cols] = lax.dot_general(
            normed_ref[...], gpre_ref[...], (((0,), (0,)), ((), ())), preferred_element_type=F32
        )
        dw_out_out[cols, :] = lax.dot_general(
            act_ref[...], gmlp_ref[...], (((0,), (0,)), ((), ())), preferred_element_type=F32
        )
        return carry

    lax.fori_loop(0, hidden // chunk, feed, 0)

    def back(t, carry):
        d_gain, d_bias, d_scale, d_b_out = carry
        at = pl.ds(pl.multiple_of(t * block, block), block)
        mask = jnp.tile(mask_out[at, :], (1, channels // 128))
        branch = mlp_ref[at, :] * mask
        block_out[at, :] = (u_out[at, :] + scale_ref[...] * branch).astype(BF16)
        d_scale = d_scale + jnp.sum(cot_ref[at, :].astype(F32) * branch, axis=0, keepdims=True)
        d_b_out = d_b_out + jnp.sum(gmlp_ref[at, :].astype(F32), axis=0, keepdims=True)
        grad = gn_ref[at, :]
        hat = mixed_ref[at, :]
        d_gain = d_gain + jnp.sum(grad * hat, axis=0, keepdims=True)
        d_bias = d_bias + jnp.sum(grad, axis=0, keepdims=True)
        grad = grad * gain_ref[...]
        mean_g = jnp.mean(grad, axis=1, keepdims=True)
        mean_gh = jnp.mean(grad * hat, axis=1, keepdims=True)
        rstd = jnp.tile(stat_ref[at, :], (1, channels // 128))
        gm_out[at, :] = (rstd * (grad - mean_g - hat * mean_gh)).astype(BF16).astype(F32)
        return d_gain, d_bias, d_scale, d_b_out

    zero = jnp.zeros((1, channels), F32)
    sums = lax.fori_loop(0, rows // block, back, (zero, zero, zero, zero))
    for index, value in enumerate(sums):
        small_out[index : index + 1, :] = value


def back_kernel(
    class_ref,
    gm_ref,
    cot_ref,
    u_ref,
    uh_ref,
    v_ref,
    rowop_ref,
    colop_ref,
    mask_ref,
    skip_ref,
    dx_out,
    dk_out,
    dskip_out,
    gh_ref,
    x_ref,
    row_acc,
    col_acc,
    gu_ref,
):
    rows, channels = gm_ref.shape
    tiles = channels // 128
    mirror_in(gm_ref, mask_ref, gh_ref)
    apply_cols(colop_ref, gh_ref, x_ref)
    cut = 3

    def row_corr(step, carry):
        tile = step // (2 * (HALF // cut))
        rest = lax.rem(step, 2 * (HALF // cut))
        rho = rest // (HALF // cut)
        first = lax.rem(rest, HALF // cut) * cut
        at = lanes(tile)
        sums = [[None] * HALF for _ in range(cut)]
        for j in range(HALF):
            left = [x_ref[rows8(rho * 81 + (first + k) * HALF + j), at] for k in range(cut)]
            for p in range(HALF):
                right = uh_ref[rows8(rho * 81 + p * HALF + j), at]
                for k in range(cut):
                    term = left[k] * right
                    sums[k][p] = term if sums[k][p] is None else sums[k][p] + term
        for k in range(cut):
            for p in range(HALF):
                row_acc[rows8(rho * 81 + (first + k) * HALF + p), at] = sums[k][p]
        return carry

    lax.fori_loop(0, tiles * 2 * (HALF // cut), row_corr, 0)

    def col_corr(step, carry):
        tile = step // (HALF // cut)
        first = lax.rem(step, HALF // cut) * cut
        at = lanes(tile)
        sums = [[None] * HALF for _ in range(cut)]
        for i in range(2 * HALF):
            left = [gh_ref[rows8(i * HALF + first + k), at] for k in range(cut)]
            for q in range(HALF):
                right = v_ref[rows8(i * HALF + q), at]
                for k in range(cut):
                    term = left[k] * right
                    sums[k][q] = term if sums[k][q] is None else sums[k][q] + term
        for k in range(cut):
            for q in range(HALF):
                col_acc[rows8((first + k) * HALF + q), at] = sums[k][q]
        return carry

    lax.fori_loop(0, tiles * (HALF // cut), col_corr, 0)

    side = side_vreg(class_ref)
    sign = jnp.where(sublane_half(), 1.0, -1.0).astype(F32)

    def lag_body(tile, carry):
        at = lanes(tile)
        for axis in range(2):
            near = [None] * HALF
            far = [None] * (GRID)
            for a in range(HALF):
                for b in range(HALF):
                    if axis == 0:
                        plus = row_acc[rows8(a * HALF + b), at]
                        minus = row_acc[rows8(81 + a * HALF + b), at]
                        direct, cross = plus + minus, plus - minus
                    else:
                        direct = col_acc[rows8(a * HALF + b), at]
                        cross = sign * direct
                    d, s = abs(a - b), GRID - 1 - a - b
                    near[d] = direct if near[d] is None else near[d] + direct
                    far[s] = cross if far[s] is None else far[s] + cross
            for lag in range(GRID):
                total = None
                for part in ([near[lag]] if lag < HALF else []) + ([far[lag]] if lag else []):
                    total = part if total is None else total + part
                total = 0.5 * total
                for cat, length in enumerate(SIDES):
                    row = cat * GRID + lag
                    value = jnp.where(side == length, total, 0.0)
                    dk_out[axis, row : row + 1, at] = jnp.sum(value, axis=0, keepdims=True)
        return carry

    lax.fori_loop(0, tiles, lag_body, 0)

    apply_rows(rowop_ref, x_ref, gh_ref)
    mirror_out(gh_ref, mask_ref, gu_ref, gm_ref, skip_ref)
    block = 144

    def finish(t, total):
        at = pl.ds(pl.multiple_of(t * block, block), block)
        dx_out[at, :] = (cot_ref[at, :].astype(F32) + gu_ref[at, :]).astype(BF16)
        return total + jnp.sum(gm_ref[at, :] * u_ref[at, :], axis=0, keepdims=True)

    dskip_out[...] = lax.fori_loop(0, rows // block, finish, jnp.zeros((1, channels), F32))


VM = pl.BlockSpec(memory_space=pltpu.VMEM)
SM = pl.BlockSpec(memory_space=pltpu.SMEM)


def shape(dims, kind=F32):
    return jax.ShapeDtypeStruct(dims, kind)


def call(kernel, outs, ins, scratch=(), name=None):
    return pl.pallas_call(
        kernel,
        out_shape=tuple(outs),
        in_specs=ins,
        out_specs=tuple(VM for _ in outs),
        scratch_shapes=list(scratch),
        compiler_params=pltpu.CompilerParams(vmem_limit_bytes=VMEM_LIMIT),
        name=name,
    )


def to_rows(images):
    micro, count, channels, cells = images.shape
    return images.transpose(3, 0, 1, 2).reshape(cells * micro * count, channels)


def from_rows(rows, like):
    micro, count, channels, cells = like.shape
    return rows.reshape(cells, micro, count, channels).transpose(1, 2, 3, 0)


def on_device(
    pixels,
    grid_class,
    extent,
    ssm_rate,
    ssm_freq,
    ssm_coef,
    skip_gain,
    norm_gain,
    norm_bias,
    w_in,
    b_in,
    w_out,
    b_out,
    layer_scale,
    cotangent,
):
    micro, count, channels, cells = pixels.shape
    rows = micro * count * cells
    own = ssm_rate.shape[1]
    modes = ssm_rate.shape[2]
    hidden = b_in.shape[0] * 2
    x = to_rows(pixels)
    cot = to_rows(cotangent)
    extent_row = extent.reshape(1, own)
    rate = ssm_rate.transpose(0, 2, 1)
    freq = ssm_freq.transpose(0, 2, 1)
    coef = ssm_coef.transpose(0, 2, 1)
    (table,) = call(tables_kernel, [shape((2, LAGS, own))], [VM] * 4, name="tables")(
        extent_row, rate, freq, coef
    )
    table = lax.all_gather(table, "mp", axis=2, tiled=True)
    w_in_all = lax.all_gather(w_in, "mp", axis=1, tiled=True)
    w_out_all = lax.all_gather(w_out, "mp", axis=0, tiled=True)
    vectors = lax.all_gather(jnp.concatenate([b_in, skip_gain]), "mp", axis=0)
    b_in_all = vectors[:, : b_in.shape[0]].reshape(1, hidden)
    skip_all = vectors[:, b_in.shape[0] :].reshape(1, channels)

    def row(v):
        return v.reshape(1, channels)

    field = (rows, channels)
    (
        block_out,
        gm,
        u,
        uh,
        v,
        rowop,
        colop,
        mask,
        dw_in,
        dw_out,
        db_in,
        small,
    ) = call(
        front_kernel,
        [
            shape(field, BF16),
            shape(field),
            shape(field),
            shape(field),
            shape(field),
            shape((90, 8, channels)),
            shape((45, 8, channels)),
            shape((rows, 128)),
            shape((channels, hidden)),
            shape((hidden, channels)),
            shape((1, hidden)),
            shape((4, channels)),
        ],
        [SM] + [VM] * 11,
        [
            pltpu.VMEM((2 * GRID, 8, channels), F32),
            pltpu.VMEM(field, F32),
            pltpu.VMEM(field, F32),
            pltpu.VMEM(field, BF16),
            pltpu.VMEM(field, BF16),
            pltpu.VMEM((rows, 256), BF16),
            pltpu.VMEM((rows, 256), BF16),
            pltpu.VMEM(field, F32),
            pltpu.VMEM(field, F32),
            pltpu.VMEM((rows, 128), F32),
        ],
        name="front",
    )(
        grid_class,
        table,
        x,
        cot,
        skip_all,
        row(norm_gain),
        row(norm_bias),
        w_in_all,
        b_in_all,
        w_out_all,
        row(b_out),
        row(layer_scale),
    )
    dx, dk, dskip = call(
        back_kernel,
        [shape(field, BF16), shape((2, LAGS, channels)), shape((1, channels))],
        [SM] + [VM] * 9,
        [
            pltpu.VMEM(field, F32),
            pltpu.VMEM(field, F32),
            pltpu.VMEM((162 * 8, channels), F32),
            pltpu.VMEM((81 * 8, channels), F32),
            pltpu.VMEM(field, F32),
        ],
        name="back",
    )(grid_class, gm, cot, u, uh, v, rowop, colop, mask, skip_all)

    dw_in = lax.psum(
        lax.psum_scatter(dw_in, "mp", scatter_dimension=1, tiled=True), "dp"
    )
    dw_out = lax.psum(
        lax.psum_scatter(dw_out, "mp", scatter_dimension=0, tiled=True), "dp"
    )
    mine = lax.axis_index("mp")
    db_in, dk, dskip, small = lax.psum((db_in, dk, dskip, small), ("dp", "mp"))
    db_in = lax.dynamic_slice_in_dim(db_in[0], mine * (hidden // 2), hidden // 2)
    dk = lax.dynamic_slice_in_dim(dk, mine * own, own, axis=2)
    dskip = lax.dynamic_slice_in_dim(dskip[0], mine * own, own)
    g_rate, g_freq, g_coef = call(
        modes_grad_kernel, [shape((2, modes, own))] * 3, [VM] * 5, name="modes"
    )(extent_row, rate, freq, coef, dk)
    return (
        from_rows(block_out, pixels),
        from_rows(dx, pixels),
        g_rate.transpose(0, 2, 1),
        g_freq.transpose(0, 2, 1),
        g_coef.transpose(0, 2, 1),
        dskip,
        small[0],
        small[1],
        dw_in,
        db_in,
        dw_out,
        small[3],
        small[2],
    )


def solution(mesh):
    placed = (
        P(None, ("dp", "mp"), None, None),
        P(None, "dp"),
        P("mp"),
        P(None, "mp", None),
        P(None, "mp", None),
        P(None, "mp", None),
        P("mp"),
        P(),
        P(),
        P(None, "mp"),
        P("mp"),
        P("mp", None),
        P(),
        P(),
        P(None, ("dp", "mp"), None, None),
    )
    return jax.shard_map(
        on_device,
        mesh=mesh,
        in_specs=placed,
        out_specs=(
            P(None, ("dp", "mp"), None, None),
            P(None, ("dp", "mp"), None, None),
            P(None, "mp", None),
            P(None, "mp", None),
            P(None, "mp", None),
            P("mp"),
            P(),
            P(),
            P(None, "mp"),
            P("mp"),
            P("mp", None),
            P(),
            P(),
        ),
        check_vma=False,
    )
```

time: 700 us -> 374 us (0.53); the launches traced: 689 us -> 374 us
  matrix products: 264 us -> 0 us
  waiting for transfers between devices: 25.1 us -> 228 us
  local copies, waits for them, and re-layouts: 176 us -> 22 us
  other arithmetic: 83.6 us -> 0.12 us
  Pallas kernels: 0 us -> 63.6 us
  blocking collectives: 107 us -> 45.4 us
  starting transfers between devices: 18.5 us -> 0.42 us
    dot_general x41 -> x0, matrix products: 264 us -> none  [the longest x6 93.1 us: mix_channels(): jnp.einsum('ncip,ncpq->nciq', rows_op, grid_view, precision=HIGH)]
    psum x1 -> x2, waiting for transfers between devices: 4.9 us -> 213 us  [the longest x1 133 us: on_device(): lax.psum(lax.psum_scatter(dw_in, 'mp', scatter_dimension=1, tiled=True),...]
    dot_general x16 -> x0, local copies, waits for them, and re-layouts: 99.2 us -> none  [the longest x4 34.1 us: mix_channels(): jnp.einsum('ncip,ncpq->nciq', rows_op, grid_view, precision=HIGH)]
    reduce_sum x11 -> x0, other arithmetic: 67.8 us -> none  [the longest x1 34.1 us: kernel_tables(): frequency[..., None] * scaled]
    pallas_call x0 -> x4, Pallas kernels: none -> 63.6 us  [the longest x1 38.3 us: on_device(): call(front_kernel, [shape(field, BF16), shape(field), shape(field), shape...]
    psum x2 -> x1, blocking collectives: 83.7 us -> 40.7 us  [on_device(): db_in, dk, dskip, small = lax.psum((db_in, dk, dskip, small), ('dp', 'mp'))]
    all_to_all x5 -> x0, starting transfers between devices: 17.9 us -> none  [the longest x2 7.13 us: on_device(): lax.all_to_all(field_tok, 'mp', split_axis=1, concat_axis=0, tiled=True)]
    all_to_all x12 -> x0, local copies, waits for them, and re-layouts: 17.5 us -> none  [the longest x8 14.5 us: on_device(): lax.all_to_all(grad_mixed.astype(jnp.bfloat16), 'mp', split_axis=1, conca...]
  transfers between devices with their start and end apart: 10 -> 6, of which waited for: 6 -> 4; matrix products, arithmetic and copies ran while one was open for 17% -> 5% of each run, Pallas kernels for 0% -> 7%
where the time goes in v1:
time: 374 us
  waiting for transfers between devices  228 us (61%)
  Pallas kernels  63.6 us (17%)
  blocking collectives  45.4 us (12%)
  local copies, waits for them, and re-layouts  22 us (6%)
  between operations  15 us (4%)
    psum x1, waiting for transfers between devices, on_device(): lax.psum(lax.psum_scatter(dw_in, 'mp', scatter_dimension=1, tiled=True),...  133 us
    psum x1, waiting for transfers between devices, on_device(): db_in, dk, dskip, small = lax.psum((db_in, dk, dskip, small), ('dp', 'mp'))  81 us
    psum x1, blocking collectives, on_device(): db_in, dk, dskip, small = lax.psum((db_in, dk, dskip, small), ('dp', 'mp'))  40.7 us
    pallas_call x1, Pallas kernels, on_device(): call(front_kernel, [shape(field, BF16), shape(field), shape(field), shape...  38.3 us
    pallas_call x1, Pallas kernels, on_device(): call(back_kernel, [shape(field, BF16), shape((2, LAGS, channels)), shape(...  16.9 us
  transfers between devices with their start and end apart: 6, of which 4 were waited for; matrix products, arithmetic and copies ran while one was open for 5% of the time, Pallas kernels for 7%

profile of v1, /device:TPU:0, one launch (start us, length us, event | category | flops | bytes accessed | tf_op | source)
XLA Modules:
  0.0 374.0 jit_solution(13020236398012855370)
XLA Ops:
  7.2 0.0 all-gather.4.cloned.1.call-start
  7.2 0.7 all-gather.4.cloned.1.call-update
  7.9 0.0 all-gather.6.cloned.1.call-start
  8.0 0.7 all-gather.6.cloned.1.call-update
  8.7 0.0 reduce-scatter.3.cloned.1.call-start
  8.8 3.7 tables.1
  12.4 1.0 copy.32
  13.5 2.2 all_gather.15
  15.6 0.8 copy.35.table_ref
  16.5 0.6 dynamic-slice.2
  17.7 0.1 maximum_dynamic-update-slice_fusion
  17.9 2.5 all-reduce
  20.4 0.1 reshape.72
  20.5 0.6 reshape.64.skip_ref
  21.1 0.6 copy.38
  21.7 0.7 copy.34
  22.4 1.3 reshape.63.cot_ref
  23.7 0.7 copy.33
  24.5 1.3 reshape.62.x_ref
  25.8 0.6 reshape.65.gain_ref
  26.4 0.6 reshape.66.bias_ref
  26.9 0.6 reshape.68.b_out_ref
  27.5 0.6 reshape.69.scale_ref
  28.1 5.4 %all-gather.6.cloned.1.call-done.w_out_ref = bf16[1536,384]{1,0:T(8,128)(2,1)} async-done(((bf16[768,384]{1,0:T(8,128)(2,1)}), bf16[1536,384]{1,0:T(8,128)(2,1)}) %all-gather.6.cloned.1.call-update) | async-done | bytes 1179664 | tf_op jit(solution)/shard_map/all_gather | solution.py:594
  33.5 38.3 %front.1 = (bf16[1296,384]{1,0:T(8,128)(2,1)}, f32[1296,384]{1,0:T(8,128)}, f32[1296,384]{1,0:T(8,128)}, f32[1296,384]{1,0:T(8,128)}, f32[1296,384]{1,0:T(8,128)...) custom-call(s32[2,4]{1,0:T(2,128)} %class_ref.3, ...), custom_call_target="tpu_custom_call" | custom-call | tf_op jit(solution)/shard_map/front/pallas_call | solution.py:616
  71.8 0.0 reduce-scatter.3.cloned.1.call-update
  71.9 0.0 reduce-scatter.5.cloned.1.call-start
  71.9 0.5 reduce-scatter.5.cloned.1.call-update
  72.4 0.0 all-reduce.6.cloned.1.call-start
  72.5 16.9 %back.1 = (bf16[1296,384]{1,0:T(8,128)(2,1)}, f32[2,54,384]{2,1,0:T(8,128)}, f32[1,384]{1,0:T(1,128)}) custom-call(s32[2,4]{1,0:T(2,128)} %class_ref.3, f32[1296,384]{1,0:T(8,128)} %get-tuple-element.32.gm_ref, bf16[1296,384]{1,0:T(8,128)(2,1)} %reshape.63.cot_ref, f32[1296,384]{1,0:T(8,128)} %get-tuple-element.33.u_ref, ...), custom_call_target="tpu_custom_call" | custom-call | tf_op jit(solution)/shard_map/back/pallas_call | solution.py:660
  89.4 0.2 all-reduce.8.cloned.1.call-start
  89.7 0.0 reduce-scatter.3.cloned.1.call-done
  89.7 6.7 %reduce-scatter.5.cloned.1.call-done = f32[768,384]{1,0:T(8,128)} async-done(((f32[1536,384]{1,0:T(8,128)}), f32[768,384]{1,0:T(8,128)}) %reduce-scatter.5.cloned.1.call-update) | async-done | bytes 1179664 | tf_op jit(solution)/shard_map/reduce_scatter | solution.py:678
  96.4 1.2 copy-done.4
  97.6 0.4 reshape.71
  98.0 0.4 reshape.70
  98.4 0.3 copy-done.5
  98.7 40.7 %all-reduce.1 = (f32[1,384]{1,0:T(1,128)S(1)}, f32[4,384]{1,0:T(4,128)S(1)}, f32[1,1536]{1,0:T(1,128)S(1)}) all-reduce(f32[1,384]{1,0:T(1,128)S(1)} %copy-done.12, f32[4,384]{1,0:T(4,128)S(1)} %copy-done.6, f32[1,1536]{1,0:T(1,128)S(1)} %copy-done.5), channel_id=1, replica_groups=mesh['dp'=16,'mp'=2] {'dp','mp'}, use_global_device_ids=true, to_apply=%region_1.0 | all-reduce | flops 3456 | bytes 27648 | tf_op jit(solution)/shard_map/psum | solution.py:681
  139.4 0.6 dynamic-slice_reduce_fusion
  140.0 0.6 constant_dynamic-slice_fusion
  140.7 0.6 slice_reduce_fusion
  141.3 2.6 copy_bitcast_fusion
  143.9 81.0 %all-reduce.6.cloned.1.call-done = f32[2,54,384]{2,1,0:T(8,128)} async-done(((f32[2,54,384]{2,1,0:T(8,128)}), f32[2,54,384]{2,1,0:T(8,128)}) %all-reduce.6.cloned.1.call-update) | async-done | bytes 165904 | tf_op jit(solution)/shard_map/psum | solution.py:681
  224.9 1.7 constant_dynamic-slice_fusion.1.dk_ref
  226.5 4.6 %modes.1 = (f32[2,64,192]{2,1,0:T(8,128)}, f32[2,64,192]{2,1,0:T(8,128)}, f32[2,64,192]{2,1,0:T(8,128)}) custom-call(s32[1,192]{1,0:T(1,128)} %bitcast.29, f32[2,64,192]{2,1,0:T(8,128)} %bitcast.22, f32[2,64,192]{2,1,0:T(8,128)} %bitcast.24, f32[2,64,192]{2,1,0:T(8,128)} %bitcast.26, f32[2,54,192]{2,1,0:T(8,128)} %constant_dynamic-slice_fusion.1.dk_ref), custom_call_target="tpu_custom_call" | custom-call | tf_op jit(solution)/shard_map/modes/pallas_call | solution.py:685
  231.2 132.5 %all-reduce.8.cloned.1.call-done = (f32[384,768]{1,0:T(8,128)}, f32[768,384]{1,0:T(8,128)}) async-done(((f32[384,768]{1,0:T(8,128)}, f32[768,384]{1,0:T(8,128)}), (f32[384,768]{1,0:T(8,128)}, f32[768,384]{1,0:T(8,128)})) %all-reduce.8.cloned.1.call-update) | async-done | bytes 2359312 | tf_op jit(solution)/shard_map/psum | solution.py:674
  363.7 2.5 copy.45
  366.2 1.0 copy.46
  (34 shorter events, 0.1 us)
Async XLA Ops:
  7.2 20.9 %all-gather.4.cloned.1.call-start = ((), (), s32[]{:S(2)}) async-start(), calls=%async_computation.2 | async-start | bytes 1769472 | tf_op jit(solution)/shard_map/all_gather | solution.py:593
  7.9 8.6 %copy-start.14 = (u32[32]{0:T(128)S(1)}, u32[32]{0:T(128)}, u32[]{:S(2)}) copy-start(u32[32]{0:T(128)} %constant.21) | copy-start | bytes 388
  7.9 9.8 %copy-start.7 = (f32[768]{0:T(1024)S(1)}, f32[768]{0:T(1024)}, u32[]{:S(2)}) copy-start(f32[768]{0:T(1024)} %param.25) | copy-start | bytes 9220
  7.9 9.8 %copy-start.13 = (f32[192]{0:T(256)S(1)}, f32[192]{0:T(256)}, u32[]{:S(2)}) copy-start(f32[192]{0:T(256)} %param.21) | copy-start | bytes 2308
  7.9 25.5 %all-gather.6.cloned.1.call-start = ((), (), s32[]{:S(2)}) async-start(), calls=%async_computation.3 | async-start | bytes 1769472 | tf_op jit(solution)/shard_map/all_gather | solution.py:594
  8.7 13.0 %copy-start.1 = (bf16[2,2,384,324]{2,1,3,0:T(2,128)(2,1)S(1)}, bf16[2,2,384,324]{2,1,3,0:T(2,128)(2,1)}, u32[]{:S(2)}) copy-start(bf16[2,2,384,324]{2,1,3,0:T(2,128)(2,1)} %param.29) | copy-start | bytes 2985988
  8.7 81.0 %reduce-scatter.3.cloned.1.call-start = ((), (), s32[]{:S(2)}) async-start(), calls=%async_computation.5 | async-start | bytes 3538944 | tf_op jit(solution)/shard_map/reduce_scatter | solution.py:675
  22.4 1.3 copy-start.2
  24.4 1.4 copy-start.8
  24.4 1.9 copy-start.9
  24.5 2.5 copy-start.10
  24.5 3.0 copy-start.11
  71.9 24.5 %reduce-scatter.5.cloned.1.call-start = ((), (), s32[]{:S(2)}) async-start(), calls=%async_computation.6 | async-start | bytes 3538944 | tf_op jit(solution)/shard_map/reduce_scatter | solution.py:678
  72.4 152.4 %all-reduce.6.cloned.1.call-start = ((), (), s32[]{:S(2)}) async-start(), calls=%async_computation.4 | async-start | bytes 344064 | tf_op jit(solution)/shard_map/psum | solution.py:681
  89.4 274.3 %all-reduce.8.cloned.1.call-start = ((), (), s32[]{:S(2)}) async-start(), calls=%async_computation.7 | async-start | bytes 4718592 | tf_op jit(solution)/shard_map/psum | solution.py:674
  96.4 1.2 copy-start.4
  96.4 1.6 copy-start.3
  98.0 0.7 copy-start.5
  98.0 0.7 copy-start.6
  98.0 0.7 copy-start.12
  363.7 2.5 copy-start
Sparse Core Ops, SparseCore 0:
  9.6 11.9 all-gather.3
  23.1 10.3 all-gather.5
  72.0 11.0 reduce-scatter.2
  85.3 11.0 reduce-scatter.4
  101.8 123.0 all-reduce.5
  230.4 133.2 all-reduce.7

commit v2 on v1

v2 whole, which is shorter than its diff:
```python
import math
from functools import partial

import jax
import jax.numpy as jnp
import numpy as np
from jax import lax
from jax.experimental import pallas as pl
from jax.experimental.pallas import tpu as pltpu
from jax.sharding import PartitionSpec as P

GRID = 18
HALF = 9
SIDES = (10, 14, 18)
LAGS = 3 * GRID
F32 = jnp.float32
BF16 = jnp.bfloat16

ERF_SHIFT = 0.35 / math.sqrt(2.0)
ERF_POLY = (
    0.19396706,
    0.23864529,
    -0.01708609,
    0.69839275,
    -0.6929918,
    0.77818103,
    -0.19910822,
)
VMEM_LIMIT = 60 * 1024 * 1024


def small_sincos(angle):
    sq = angle * angle
    cos = 1.0 + sq * (
        -1 / 2 + sq * (1 / 24 + sq * (-1 / 720 + sq * (1 / 40320 + sq * (-1 / 3628800))))
    )
    sin = angle * (
        1.0
        + sq * (-1 / 6 + sq * (1 / 120 + sq * (-1 / 5040 + sq * (1 / 362880 + sq * (-1 / 39916800)))))
    )
    return sin, cos


def mode_step(rate, freq, side):
    decay = jnp.exp(rate * (-1.0 / side))
    sin, cos = small_sincos(freq * (1.0 / side))
    return decay * cos, decay * sin


PACK_ROWS = 120
SMALL_ROWS = 121

def write_tables(extent_ref, rate_ref, freq_ref, coef_ref, out_ref):
    for axis in range(2):
        for cat, side in enumerate(SIDES):
            z_re, z_im = mode_step(rate_ref[axis], freq_ref[axis], side)
            w_re = coef_ref[axis]
            w_im = jnp.zeros_like(w_re)
            for lag in range(GRID):
                row = axis * LAGS + cat * GRID + lag
                if lag >= side:
                    out_ref[row : row + 1, :] = jnp.zeros((1, w_re.shape[1]), F32)
                    continue
                total = jnp.sum(w_re, axis=0, keepdims=True)
                out_ref[row : row + 1, :] = jnp.where(extent_ref[...] > lag, total, 0.0)
                if lag < side - 1:
                    w_re, w_im = w_re * z_re - w_im * z_im, w_re * z_im + w_im * z_re


def modes_grad(extent_ref, rate_ref, freq_ref, coef_ref, dk_ref, rate_out, freq_out, coef_out):
    for axis in range(2):
        coef = coef_ref[axis]
        g_rate = jnp.zeros_like(coef)
        g_freq = jnp.zeros_like(coef)
        g_coef = jnp.zeros_like(coef)
        for cat, side in enumerate(SIDES):
            z_re, z_im = mode_step(rate_ref[axis], freq_ref[axis], side)
            p_re = jnp.zeros_like(coef)
            p_im = jnp.zeros_like(coef)
            q_re = jnp.zeros_like(coef)
            q_im = jnp.zeros_like(coef)
            for lag in reversed(range(side)):
                row = axis * LAGS + cat * GRID + lag
                d = jnp.where(extent_ref[...] > lag, dk_ref[row : row + 1, :], 0.0)
                p_re, p_im = p_re * z_re - p_im * z_im + d, p_re * z_im + p_im * z_re
                q_re, q_im = q_re * z_re - q_im * z_im + float(lag) * d, q_re * z_im + q_im * z_re
            g_coef = g_coef + p_re
            g_rate = g_rate - (1.0 / side) * q_re
            g_freq = g_freq - (1.0 / side) * q_im
        coef_out[axis] = g_coef
        rate_out[axis] = g_rate * coef
        freq_out[axis] = g_freq * coef

def tri(a, b):
    low, high = min(a, b), max(a, b)
    return low * HALF - low * (low - 1) // 2 + (high - low)


def rows8(index):
    if isinstance(index, int):
        return pl.ds(index * 8, 8)
    return pl.ds(pl.multiple_of(index * 8, 8), 8)


def lanes(tile):
    if isinstance(tile, int):
        return pl.ds(tile * 128, 128)
    return pl.ds(pl.multiple_of(tile * 128, 128), 128)


def swap(value):
    return pltpu.roll(value, 4, 0)


def sublane_half():
    return lax.broadcasted_iota(jnp.int32, (8, 128), 0) < 4


def side_vreg(class_ref):
    mine = lax.axis_index("mp")
    image = lax.rem(lax.broadcasted_iota(jnp.int32, (8, 128), 0), 4)
    cls = jnp.zeros((8, 128), jnp.int32)
    own = class_ref.shape[1] // 2
    for micro in range(2):
        for img in range(2):
            cls = jnp.where(image == micro * 2 + img, class_ref[micro, mine * own + img], cls)
    return 10 + 4 * cls


def build_masks(class_ref, mask_ref):
    side = side_vreg(class_ref)
    offset = jnp.where(sublane_half(), 0, 1)

    def row(i, carry):
        for pair in range(HALF):
            ok = (i < side) & (2 * pair + offset < side)
            mask_ref[rows8(i * HALF + pair), :] = jnp.where(ok, 1.0, 0.0).astype(F32)
        return carry

    lax.fori_loop(0, GRID, row, 0)


def build_operators(class_ref, table_ref, lag_ref, rowop_ref, colop_ref):
    side = side_vreg(class_ref)
    sign = jnp.where(sublane_half(), 1.0, -1.0).astype(F32)
    tiles = table_ref.shape[1] // 128

    def tile_body(tile, carry):
        at = lanes(tile)
        for axis in range(2):
            for lag in range(GRID):
                by_side = [
                    jnp.broadcast_to(table_ref[axis * LAGS + cat * GRID + lag : axis * LAGS + cat * GRID + lag + 1, at], (8, 128))
                    for cat in range(3)
                ]
                lag_ref[axis * GRID + lag, :, at] = 0.5 * jnp.where(
                    side == 10, by_side[0], jnp.where(side == 14, by_side[1], by_side[2])
                )
        for a in range(HALF):
            for b in range(a, HALF):
                near = lag_ref[b - a, :, at]
                far = lag_ref[GRID - 1 - a - b, :, at]
                rowop_ref[tri(a, b), :, at] = near + far
                rowop_ref[45 + tri(a, b), :, at] = near - far
                near = lag_ref[GRID + b - a, :, at]
                far = lag_ref[GRID + GRID - 1 - a - b, :, at]
                colop_ref[tri(a, b), :, at] = near + sign * far
        return carry

    lax.fori_loop(0, tiles, tile_body, 0)


def mirror_in(source_ref, mask_ref, out_ref):
    half = sublane_half()
    sign = jnp.where(half, 1.0, -1.0).astype(F32)
    tiles = source_ref.shape[1] // 128

    def body(i, carry):
        for tile in range(tiles):
            at = lanes(tile)

            def mirrored(row, pair):
                near = source_ref[rows8(row * HALF + pair), at] * mask_ref[rows8(row * HALF + pair), :]
                if pair == 4:
                    return swap(near) + sign * near, None
                other = row * HALF + 8 - pair
                far = source_ref[rows8(other), at] * mask_ref[rows8(other), :]
                even = jnp.where(half, near, far)
                odd = jnp.where(half, far, near)
                return swap(even) + sign * even, odd + sign * swap(odd)

            for pair in range(5):
                top = mirrored(i, pair)
                bottom = mirrored(GRID - 1 - i, pair)
                for step in range(2 if pair < 4 else 1):
                    where = i * HALF + 2 * pair + step
                    out_ref[rows8(where), at] = top[step] + bottom[step]
                    out_ref[rows8(81 + where), at] = top[step] - bottom[step]
        return carry

    lax.fori_loop(0, HALF, body, 0)


def mirror_out(source_ref, mask_ref, out_ref, extra_ref, gain_ref):
    half = sublane_half()
    sign = jnp.where(half, 1.0, -1.0).astype(F32)
    tiles = source_ref.shape[1] // 128

    def body(i, carry):
        for tile in range(tiles):
            at = lanes(tile)
            gain = jnp.broadcast_to(gain_ref[:, at], (8, 128))

            def finish(index, value):
                value = value * mask_ref[rows8(index), :] + gain * extra_ref[rows8(index), at]
                out_ref[rows8(index), at] = value.astype(BF16).astype(F32)

            for pair in range(5):
                both = []
                for step in range(2 if pair < 4 else 1):
                    where = i * HALF + 2 * pair + step
                    plus = source_ref[rows8(where), at]
                    minus = source_ref[rows8(81 + where), at]
                    top, bottom = plus + minus, plus - minus
                    both.append(
                        (swap(top) + sign * top, swap(bottom) + sign * bottom)
                        if step == 0
                        else (top - sign * swap(top), bottom - sign * swap(bottom))
                    )
                for part, row in ((0, i), (1, GRID - 1 - i)):
                    if pair == 4:
                        finish(row * HALF + 4, both[0][part])
                        continue
                    if True:
                        even, odd = both[0][part], both[1][part]
                        finish(row * HALF + pair, jnp.where(half, even, odd))
                        finish(row * HALF + 8 - pair, jnp.where(half, odd, even))
        return carry

    lax.fori_loop(0, HALF, body, 0)


def apply_rows(op_ref, source_ref, out_ref):
    tiles = source_ref.shape[1] // 128

    def body(j, carry):
        for tile in range(tiles):
            at = lanes(tile)
            for rho in range(2):
                values = [source_ref[rows8(rho * 81 + p * HALF + j), at] for p in range(HALF)]
                for i in range(HALF):
                    total = None
                    for p in range(HALF):
                        term = op_ref[rho * 45 + tri(i, p), :, at] * values[p]
                        total = term if total is None else total + term
                    out_ref[rows8(rho * 81 + i * HALF + j), at] = total
        return carry

    lax.fori_loop(0, HALF, body, 0)


def apply_cols(op_ref, source_ref, out_ref):
    tiles = source_ref.shape[1] // 128

    def body(i, carry):
        for tile in range(tiles):
            at = lanes(tile)
            values = [source_ref[rows8(i * HALF + q), at] for q in range(HALF)]
            for j in range(HALF):
                total = None
                for q in range(HALF):
                    term = op_ref[tri(j, q), :, at] * values[q]
                    total = term if total is None else total + term
                out_ref[rows8(i * HALF + j), at] = total
        return carry

    lax.fori_loop(0, 2 * HALF, body, 0)


def row_correlate(left_ref, right_ref, acc_ref, cut=3):
    tiles = left_ref.shape[1] // 128
    blocks = HALF // cut

    def body(step, carry):
        tile = step // (2 * blocks)
        rest = lax.rem(step, 2 * blocks)
        rho = rest // blocks
        first = lax.rem(rest, blocks) * cut
        at = lanes(tile)
        sums = [[None] * HALF for _ in range(cut)]
        for j in range(HALF):
            left = [left_ref[rows8(rho * 81 + (first + k) * HALF + j), at] for k in range(cut)]
            for p in range(HALF):
                right = right_ref[rows8(rho * 81 + p * HALF + j), at]
                for k in range(cut):
                    term = left[k] * right
                    sums[k][p] = term if sums[k][p] is None else sums[k][p] + term
        for k in range(cut):
            for p in range(HALF):
                acc_ref[rows8(rho * 81 + (first + k) * HALF + p), at] = sums[k][p]
        return carry

    lax.fori_loop(0, tiles * 2 * blocks, body, 0)


def col_correlate(left_ref, right_ref, acc_ref, cut=3):
    tiles = left_ref.shape[1] // 128
    blocks = HALF // cut

    def body(step, carry):
        tile = step // blocks
        first = lax.rem(step, blocks) * cut
        at = lanes(tile)
        sums = [[None] * HALF for _ in range(cut)]
        for i in range(2 * HALF):
            left = [left_ref[rows8(i * HALF + first + k), at] for k in range(cut)]
            for q in range(HALF):
                right = right_ref[rows8(i * HALF + q), at]
                for k in range(cut):
                    term = left[k] * right
                    sums[k][q] = term if sums[k][q] is None else sums[k][q] + term
        for k in range(cut):
            for q in range(HALF):
                acc_ref[rows8((first + k) * HALF + q), at] = sums[k][q]
        return carry

    lax.fori_loop(0, tiles * blocks, body, 0)


def gather_lags(class_ref, row_acc, col_acc, dk_ref):
    side = side_vreg(class_ref)
    sign = jnp.where(sublane_half(), 1.0, -1.0).astype(F32)
    tiles = row_acc.shape[1] // 128

    def body(tile, carry):
        at = lanes(tile)
        for axis in range(2):
            near = [None] * HALF
            far = [None] * GRID
            for a in range(HALF):
                for b in range(HALF):
                    if axis == 0:
                        plus = row_acc[rows8(a * HALF + b), at]
                        minus = row_acc[rows8(81 + a * HALF + b), at]
                        direct, cross = plus + minus, plus - minus
                    else:
                        direct = col_acc[rows8(a * HALF + b), at]
                        cross = sign * direct
                    d, s = abs(a - b), GRID - 1 - a - b
                    near[d] = direct if near[d] is None else near[d] + direct
                    far[s] = cross if far[s] is None else far[s] + cross
            for lag in range(GRID):
                total = None
                for part in ([near[lag]] if lag < HALF else []) + ([far[lag]] if lag else []):
                    total = part if total is None else total + part
                total = 0.5 * total
                for cat, length in enumerate(SIDES):
                    row = axis * LAGS + cat * GRID + lag
                    value = jnp.where(side == length, total, 0.0)
                    dk_ref[row : row + 1, at] = jnp.sum(value, axis=0, keepdims=True)
        return carry

    lax.fori_loop(0, tiles, body, 0)


def bit_orders(size):
    bits = size.bit_length() - 1
    turn = min(3, max(bits, 1))
    base = list(range(bits))
    return [
        [base[(k + part) % turn] if k < turn else base[k] for k in range(bits)] for part in range(3)
    ]


def chunk_rows(total, size):
    per = -(-total // (3 * size))
    return -(-per // 16) * 16


class Ring:
    def __init__(self, size, rows, acc, send, recv, full, sems):
        self.size, self.rows = size, rows
        self.acc, self.send, self.recv, self.full = acc, send, recv, full
        self.send_sem, self.recv_sem, self.back_send, self.back_recv = sems
        self.orders = bit_orders(size)
        self.bits = size.bit_length() - 1
        self.me = lax.axis_index("dp")
        self.place = []
        for order in self.orders:
            place = 0
            for bit in order:
                place = place * 2 + lax.rem(self.me // (1 << bit), 2)
            self.place.append(place)

    def peer(self, bit):
        mine = lax.rem(self.me // (1 << bit), 2)
        return self.me + (1 - 2 * mine) * (1 << bit)

    def span(self, part, step):
        half = self.size >> (step + 1)
        index = self.place[part] // half
        mine = lax.rem(index, 2)
        base = part * self.size * self.rows
        keep = base + index * half * self.rows
        away = base + (index + 1 - 2 * mine) * half * self.rows
        return pl.multiple_of(keep, 16), pl.multiple_of(away, 16), half * self.rows

    def slot(self, part, step):
        done = self.size - (self.size >> step)
        return (part * self.size + done) * self.rows

    def reduce_copy(self, part, step):
        _, away, length = self.span(part, step)
        return pltpu.make_async_remote_copy(
            src_ref=self.send.at[pl.ds(away, length), :],
            dst_ref=self.recv.at[pl.ds(self.slot(part, step), length), :],
            send_sem=self.send_sem.at[part, step],
            recv_sem=self.recv_sem.at[part, step],
            device_id={"dp": self.peer(self.orders[part][step])},
            device_id_type=pl.DeviceIdType.MESH,
        )

    def gather_copy(self, part, step):
        keep, _, length = self.span(part, step)
        return pltpu.make_async_remote_copy(
            src_ref=self.full.at[pl.ds(keep, length), :],
            dst_ref=self.full.at[pl.ds(keep, length), :],
            send_sem=self.back_send.at[part, step],
            recv_sem=self.back_recv.at[part, step],
            device_id={"dp": self.peer(self.orders[part][step])},
            device_id_type=pl.DeviceIdType.MESH,
        )

    def reduce_start(self, step):
        for part in range(3):
            _, away, length = self.span(part, step)
            copy_rows(self.acc, away, self.send, away, length, lambda v: v.astype(BF16))
            self.reduce_copy(part, step).start()

    def reduce_finish(self, step):
        for part in range(3):
            self.reduce_copy(part, step).wait_recv()
            keep, _, length = self.span(part, step)
            slot = self.slot(part, step)

            def body(t, carry, keep=keep, slot=slot):
                at = pl.ds(pl.multiple_of(keep + t * 48, 16), 48)
                other = pl.ds(pl.multiple_of(slot + t * 48, 16), 48)
                self.acc[at, :] += self.recv[other, :].astype(F32)
                return carry

            if length % 48 == 0:
                lax.fori_loop(0, length // 48, body, 0)
            else:
                self.acc[pl.ds(keep, length), :] += self.recv[pl.ds(slot, length), :].astype(F32)

    def gather_first(self):
        for part in range(3):
            own = pl.multiple_of((part * self.size + self.place[part]) * self.rows, 16)
            copy_rows(self.acc, own, self.full, own, self.rows, lambda v: v.astype(BF16))

    def gather_start(self, step):
        for part in range(3):
            self.gather_copy(part, step).start()

    def gather_finish(self, step):
        for part in range(3):
            self.gather_copy(part, step).wait_recv()

    def close(self):
        for part in range(3):
            for step in range(self.bits):
                self.reduce_copy(part, step).wait_send()
                self.gather_copy(part, step).wait_send()


def copy_rows(source, first, target, where, length, change, block=48):
    if length % block:
        block = 16

    def body(t, carry):
        here = pl.ds(pl.multiple_of(first + t * block, 16), block)
        there = pl.ds(pl.multiple_of(where + t * block, 16), block)
        target[there, :] = change(source[here, :])
        return carry

    lax.fori_loop(0, length // block, body, 0)


def wide(ref, first, count):
    return jnp.concatenate([ref[first + k : first + k + 1, :] for k in range(count)], axis=1)


def mega_kernel(
    size,
    class_ref,
    extent_ref,
    rate_ref,
    freq_ref,
    coef_ref,
    skip_ref,
    b_in_ref,
    vec_ref,
    w_in_ref,
    w_out_ref,
    x_ref,
    cot_ref,
    block_out,
    dx_out,
    full_out,
    small_out,
    pack_own,
    pack_oth,
    w_in_oth,
    w_out_oth,
    table_ref,
    skip_all,
    mask_ref,
    lag_ref,
    rowop_ref,
    colop_ref,
    u_ref,
    uh_ref,
    v_ref,
    mh_ref,
    mixed_ref,
    normed_ref,
    gmlp_ref,
    act_ref,
    gpre_ref,
    mlp_ref,
    gn_ref,
    stat_ref,
    gm_ref,
    row_acc,
    col_acc,
    dk_ref,
    db_ref,
    sums_ref,
    acc_ref,
    away_ref,
    landed_ref,
    send_ref,
    recv_ref,
    small_keep,
    small_send,
    small_land,
    small_recv,
    pair_send,
    pair_recv,
    red_send,
    red_recv,
    gat_send,
    gat_recv,
    sc_send,
    sc_recv,
    bc_send,
    bc_recv,
):
    rows, channels = x_ref.shape
    own = pack_own.shape[1]
    half_hidden = w_in_ref.shape[1]
    me = lax.axis_index("dp")
    core = lax.axis_index("mp")
    partner = {"mp": 1 - core}

    barrier = pltpu.get_barrier_semaphore()
    pl.semaphore_signal(barrier, inc=1, device_id=partner, device_id_type=pl.DeviceIdType.MESH)
    for offset in range(1, size):
        pl.semaphore_signal(
            barrier,
            inc=1,
            device_id={"dp": lax.rem(me + offset, size)},
            device_id_type=pl.DeviceIdType.MESH,
        )

    def pair_copy(index, source, target):
        return pltpu.make_async_remote_copy(
            src_ref=source,
            dst_ref=target,
            send_sem=pair_send.at[index],
            recv_sem=pair_recv.at[index],
            device_id=partner,
            device_id_type=pl.DeviceIdType.MESH,
        )

    write_tables(extent_ref, rate_ref, freq_ref, coef_ref, pack_own)
    pack_own[108:109, :] = skip_ref[...]
    for k in range(4):
        pack_own[109 + k : 110 + k, :] = b_in_ref[:, k * own : (k + 1) * own]
    pack_own[113:PACK_ROWS, :] = jnp.zeros((PACK_ROWS - 113, own), F32)
    pl.semaphore_wait(barrier, size)
    pack_copy = pair_copy(0, pack_own, pack_oth)
    first_copy = pair_copy(1, w_in_ref, w_in_oth)
    second_copy = pair_copy(2, w_out_ref, w_out_oth)
    pack_copy.start()
    first_copy.start()
    second_copy.start()

    build_masks(class_ref, mask_ref)
    block = 144
    scale = vec_ref[3:4, :]

    def load(t, carry):
        at = pl.ds(pl.multiple_of(t * block, block), block)
        u_ref[at, :] = x_ref[at, :].astype(F32)
        mask = jnp.tile(mask_ref[at, :], (1, channels // 128))
        gmlp_ref[at, :] = (cot_ref[at, :].astype(F32) * scale * mask).astype(BF16)
        return carry

    lax.fori_loop(0, rows // block, load, 0)
    mirror_in(u_ref, mask_ref, uh_ref)

    pack_copy.wait_recv()
    first = core == 0
    low = jnp.where(first, pack_own[...], pack_oth[...])
    high = jnp.where(first, pack_oth[...], pack_own[...])
    table_ref[...] = jnp.concatenate([low, high], axis=1)
    skip_all[...] = table_ref[108:109, :]
    build_operators(class_ref, table_ref, lag_ref, rowop_ref, colop_ref)
    apply_rows(rowop_ref, uh_ref, v_ref)
    apply_cols(colop_ref, v_ref, mh_ref)
    mirror_out(mh_ref, mask_ref, mixed_ref, u_ref, skip_all)

    gain = vec_ref[0:1, :]
    shift = vec_ref[1:2, :]

    def norm(t, carry):
        at = pl.ds(pl.multiple_of(t * block, block), block)
        value = mixed_ref[at, :]
        mean = jnp.mean(value, axis=1, keepdims=True)
        centered = value - mean
        variance = jnp.mean(centered * centered, axis=1, keepdims=True)
        rstd = lax.rsqrt(variance + 1e-06)
        hat = centered * rstd
        mixed_ref[at, :] = hat
        stat_ref[at, :] = jnp.broadcast_to(rstd, (block, 128))
        normed_ref[at, :] = (hat * gain + shift).astype(BF16)
        return carry

    lax.fori_loop(0, rows // block, norm, 0)

    chunk = 256
    tile_rows = 432
    mlp_ref[...] = jnp.broadcast_to(vec_ref[2:3, :], mlp_ref.shape)
    gn_ref[...] = jnp.zeros_like(gn_ref)
    first_copy.wait_recv()
    second_copy.wait_recv()

    def feed(w_first_ref, w_second_ref, bias_row, target_ref, db_row):
        db_ref[2:3, :] = bias_row

        def body(f, carry):
            cols = pl.ds(pl.multiple_of(f * chunk, chunk), chunk)
            w_first = w_first_ref[:, cols]
            w_second = w_second_ref[cols, :]
            bias = db_ref[2:3, cols]
            db = jnp.zeros((1, chunk), F32)
            for t in range(rows // tile_rows):
                at = pl.ds(t * tile_rows, tile_rows)
                pre = jnp.dot(normed_ref[at, :], w_first, preferred_element_type=F32) + bias
                size_of = jnp.abs(pre)
                inv = 1.0 / (1.0 + ERF_SHIFT * size_of)
                poly = jnp.full_like(inv, 0.5 * ERF_POLY[-1])
                for value in reversed(ERF_POLY[:-1]):
                    poly = poly * inv + 0.5 * value
                bell = jnp.exp(-0.5 * pre * pre)
                tail = poly * inv * bell
                cdf = jnp.where(pre >= 0.0, 1.0 - tail, tail)
                act = (pre * cdf).astype(BF16)
                slope = cdf + pre * bell * (1.0 / math.sqrt(2.0 * math.pi))
                g_act = lax.dot_general(
                    gmlp_ref[at, :], w_second, (((1,), (1,)), ((), ())), preferred_element_type=F32
                )
                g_pre = (g_act * slope).astype(BF16)
                db = db + jnp.sum(g_pre.astype(F32), axis=0, keepdims=True)
                act_ref[at, :] = act
                gpre_ref[at, :] = g_pre
                mlp_ref[at, :] += jnp.dot(act, w_second, preferred_element_type=F32)
                gn_ref[at, :] += lax.dot_general(
                    g_pre, w_first, (((1,), (1,)), ((), ())), preferred_element_type=F32
                )
            db_ref[db_row : db_row + 1, cols] = db
            d_first = lax.dot_general(
                normed_ref[...], gpre_ref[...], (((0,), (0,)), ((), ())), preferred_element_type=F32
            )
            for k in range(chunk // 128):
                at = pl.ds(pl.multiple_of((f * (chunk // 128) + k) * channels, channels), channels)
                target_ref[at, :] = d_first[:, k * 128 : (k + 1) * 128].astype(target_ref.dtype)
            d_second = lax.dot_general(
                act_ref[...], gmlp_ref[...], (((0,), (0,)), ((), ())), preferred_element_type=F32
            )
            base = channels * (half_hidden // 128)
            for k in range(channels // 128):
                at = pl.ds(pl.multiple_of(base + k * half_hidden + f * chunk, chunk), chunk)
                target_ref[at, :] = d_second[:, k * 128 : (k + 1) * 128].astype(target_ref.dtype)
            return carry

        lax.fori_loop(0, half_hidden // chunk, body, 0)

    feed(w_in_oth, w_out_oth, wide(pack_oth, 109, 4), away_ref, 1)
    grads_copy = pair_copy(3, away_ref, landed_ref)
    grads_copy.start()
    feed(w_in_ref, w_out_ref, b_in_ref[...], acc_ref, 0)

    ring = Ring(size, chunk_rows(away_ref.shape[0], size), acc_ref, send_ref, recv_ref, full_out,
                (red_send, red_recv, gat_send, gat_recv))
    grads_copy.wait_recv()

    def add_pair(t, carry):
        at = pl.ds(pl.multiple_of(t * 96, 96), 96)
        acc_ref[at, :] += landed_ref[at, :].astype(F32)
        return carry

    lax.fori_loop(0, away_ref.shape[0] // 96, add_pair, 0)
    pad = acc_ref.shape[0] - away_ref.shape[0]
    if pad:
        acc_ref[away_ref.shape[0] :, :] = jnp.zeros((pad, 128), F32)

    def advance(step):
        if step > 2 * ring.bits:
            return
        if 0 < step <= ring.bits:
            ring.reduce_finish(step - 1)
        if step > ring.bits:
            ring.gather_finish(2 * ring.bits - step)
        if step < ring.bits:
            ring.reduce_start(step)
        if step == ring.bits:
            ring.gather_first()
        if ring.bits <= step < 2 * ring.bits:
            ring.gather_start(2 * ring.bits - 1 - step)

    advance(0)

    def back(t, carry):
        d_gain, d_bias, d_scale, d_b_out = carry
        at = pl.ds(pl.multiple_of(t * block, block), block)
        mask = jnp.tile(mask_ref[at, :], (1, channels // 128))
        branch = mlp_ref[at, :] * mask
        block_out[at, :] = (u_ref[at, :] + scale * branch).astype(BF16)
        d_scale = d_scale + jnp.sum(cot_ref[at, :].astype(F32) * branch, axis=0, keepdims=True)
        d_b_out = d_b_out + jnp.sum(gmlp_ref[at, :].astype(F32), axis=0, keepdims=True)
        grad = gn_ref[at, :]
        hat = mixed_ref[at, :]
        d_gain = d_gain + jnp.sum(grad * hat, axis=0, keepdims=True)
        d_bias = d_bias + jnp.sum(grad, axis=0, keepdims=True)
        grad = grad * gain
        mean_g = jnp.mean(grad, axis=1, keepdims=True)
        mean_gh = jnp.mean(grad * hat, axis=1, keepdims=True)
        rstd = jnp.tile(stat_ref[at, :], (1, channels // 128))
        gm_ref[at, :] = (rstd * (grad - mean_g - hat * mean_gh)).astype(BF16).astype(F32)
        return d_gain, d_bias, d_scale, d_b_out

    zero = jnp.zeros((1, channels), F32)
    sums = lax.fori_loop(0, rows // block, back, (zero, zero, zero, zero))
    for index, value in enumerate(sums):
        sums_ref[index : index + 1, :] = value

    gh_ref, xh_ref = mh_ref, mlp_ref
    mirror_in(gm_ref, mask_ref, gh_ref)
    advance(1)
    apply_cols(colop_ref, gh_ref, xh_ref)
    advance(2)
    row_correlate(xh_ref, uh_ref, row_acc)
    advance(3)
    col_correlate(gh_ref, v_ref, col_acc)
    advance(4)
    gather_lags(class_ref, row_acc, col_acc, dk_ref)

    def skip_sum(t, total):
        at = pl.ds(pl.multiple_of(t * block, block), block)
        return total + jnp.sum(gm_ref[at, :] * u_ref[at, :], axis=0, keepdims=True)

    dk_ref[108:109, :] = lax.fori_loop(0, rows // block, skip_sum, zero)
    dk_ref[109:112, :] = jnp.zeros((3, channels), F32)
    low = dk_ref[:, :own]
    high = dk_ref[:, own:]
    small_keep[...] = jnp.zeros_like(small_keep)
    small_keep[0:112, :] = jnp.where(first, low, high)
    small_send[0:112, :] = jnp.where(first, high, low)
    for k in range(4):
        small_keep[109 + k : 110 + k, :] = db_ref[0:1, k * own : (k + 1) * own]
        small_send[109 + k : 110 + k, :] = db_ref[1:2, k * own : (k + 1) * own]
    for k in range(8):
        value = sums_ref[k // 2 : k // 2 + 1, (k % 2) * own : (k % 2 + 1) * own]
        small_keep[113 + k : 114 + k, :] = value
        small_send[113 + k : 114 + k, :] = value
    small_send[SMALL_ROWS:128, :] = jnp.zeros((128 - SMALL_ROWS, own), F32)
    small_pair = pair_copy(4, small_send, small_land)
    small_pair.start()
    apply_rows(rowop_ref, xh_ref, gh_ref)
    small_pair.wait_recv()
    small_keep[0:128, :] += small_land[...]

    per = small_keep.shape[0] // size
    mine = pl.ds(pl.multiple_of(me * per, 8), per)

    def scatter_copy(offset):
        target = lax.rem(me + offset, size)
        return pltpu.make_async_remote_copy(
            src_ref=small_keep.at[pl.ds(pl.multiple_of(target * per, 8), per), :],
            dst_ref=small_recv.at[offset - 1],
            send_sem=sc_send.at[offset - 1],
            recv_sem=sc_recv.at[offset - 1],
            device_id={"dp": target},
            device_id_type=pl.DeviceIdType.MESH,
        )

    def spread_copy(offset):
        target = lax.rem(me + offset, size)
        return pltpu.make_async_remote_copy(
            src_ref=small_out.at[mine, :],
            dst_ref=small_out.at[mine, :],
            send_sem=bc_send.at[offset - 1],
            recv_sem=bc_recv.at[offset - 1],
            device_id={"dp": target},
            device_id_type=pl.DeviceIdType.MESH,
        )

    for offset in range(1, size):
        scatter_copy(offset).start()
    mirror_out(gh_ref, mask_ref, gn_ref, gm_ref, skip_all)
    total = small_keep[mine, :]
    for offset in range(1, size):
        scatter_copy(offset).wait_recv()
        total = total + small_recv[offset - 1]
    small_out[mine, :] = total
    for offset in range(1, size):
        spread_copy(offset).start()

    def finish(t, carry):
        at = pl.ds(pl.multiple_of(t * block, block), block)
        dx_out[at, :] = (cot_ref[at, :].astype(F32) + gn_ref[at, :]).astype(BF16)
        return carry

    lax.fori_loop(0, rows // block, finish, 0)
    for step in range(5, 2 * ring.bits + 1):
        advance(step)
    if ring.bits == 0:
        pass
    for offset in range(1, size):
        spread_copy(offset).wait_recv()
    for offset in range(1, size):
        scatter_copy(offset).wait_send()
        spread_copy(offset).wait_send()
    ring.close()
    for copy in (pack_copy, first_copy, second_copy, grads_copy, small_pair):
        copy.wait_send()


def final_kernel(
    extent_ref, rate_ref, freq_ref, coef_ref, full_ref, small_ref, rate_out, freq_out, coef_out,
    skip_out, vec_out, dw_in_out, db_in_out, dw_out_out,
):
    channels, half_hidden = dw_in_out.shape
    for k in range(half_hidden // 128):
        dw_in_out[:, k * 128 : (k + 1) * 128] = full_ref[k * channels : (k + 1) * channels, :].astype(F32)
    base = channels * (half_hidden // 128)
    for k in range(channels // 128):
        dw_out_out[:, k * 128 : (k + 1) * 128] = full_ref[
            base + k * half_hidden : base + (k + 1) * half_hidden, :
        ].astype(F32)
    modes_grad(extent_ref, rate_ref, freq_ref, coef_ref, small_ref, rate_out, freq_out, coef_out)
    skip_out[...] = small_ref[108:109, :]
    db_in_out[...] = wide(small_ref, 109, 4)
    for k in range(4):
        vec_out[k : k + 1, :] = wide(small_ref, 113 + 2 * k, 2)


VM = pl.BlockSpec(memory_space=pltpu.VMEM)
SM = pl.BlockSpec(memory_space=pltpu.SMEM)


def shape(dims, kind=F32):
    return jax.ShapeDtypeStruct(dims, kind)


def to_rows(images):
    micro, count, channels, cells = images.shape
    return images.transpose(3, 0, 1, 2).reshape(cells * micro * count, channels)


def from_rows(rows, like):
    micro, count, channels, cells = like.shape
    return rows.reshape(cells, micro, count, channels).transpose(1, 2, 3, 0)


def on_device(
    size,
    pixels,
    grid_class,
    extent,
    ssm_rate,
    ssm_freq,
    ssm_coef,
    skip_gain,
    norm_gain,
    norm_bias,
    w_in,
    b_in,
    w_out,
    b_out,
    layer_scale,
    cotangent,
):
    micro, count, channels, cells = pixels.shape
    rows = micro * count * cells
    own = ssm_rate.shape[1]
    modes = ssm_rate.shape[2]
    half_hidden = b_in.shape[0]
    x = to_rows(pixels)
    cot = to_rows(cotangent)
    extent_row = extent.reshape(1, own)
    rate = ssm_rate.transpose(0, 2, 1)
    freq = ssm_freq.transpose(0, 2, 1)
    coef = ssm_coef.transpose(0, 2, 1)
    vec = jnp.stack([norm_gain, norm_bias, b_out, layer_scale])
    field = (rows, channels)
    grad_rows = 2 * channels * half_hidden // 128
    all_rows = 3 * size * chunk_rows(grad_rows, size)
    small_rows = max(128, 8 * size)
    bits = max(size.bit_length() - 1, 1)
    peers = max(size - 1, 1)
    DMA = pltpu.SemaphoreType.DMA
    block_out, dx, full, small = pl.pallas_call(
        partial(mega_kernel, size),
        out_shape=(
            shape(field, BF16),
            shape(field, BF16),
            shape((all_rows, 128), BF16),
            shape((small_rows, own)),
        ),
        in_specs=[SM] + [VM] * 11,
        out_specs=(VM,) * 4,
        scratch_shapes=[
            pltpu.VMEM((PACK_ROWS, own), F32),
            pltpu.VMEM((PACK_ROWS, own), F32),
            pltpu.VMEM(w_in.shape, BF16),
            pltpu.VMEM(w_out.shape, BF16),
            pltpu.VMEM((PACK_ROWS, channels), F32),
            pltpu.VMEM((1, channels), F32),
            pltpu.VMEM((rows, 128), F32),
            pltpu.VMEM((2 * GRID, 8, channels), F32),
            pltpu.VMEM((90, 8, channels), F32),
            pltpu.VMEM((45, 8, channels), F32),
            pltpu.VMEM(field, F32),
            pltpu.VMEM(field, F32),
            pltpu.VMEM(field, F32),
            pltpu.VMEM(field, F32),
            pltpu.VMEM(field, F32),
            pltpu.VMEM(field, BF16),
            pltpu.VMEM(field, BF16),
            pltpu.VMEM((rows, 256), BF16),
            pltpu.VMEM((rows, 256), BF16),
            pltpu.VMEM(field, F32),
            pltpu.VMEM(field, F32),
            pltpu.VMEM((rows, 128), F32),
            pltpu.VMEM(field, F32),
            pltpu.VMEM((162 * 8, channels), F32),
            pltpu.VMEM((81 * 8, channels), F32),
            pltpu.VMEM((112, channels), F32),
            pltpu.VMEM((3, half_hidden), F32),
            pltpu.VMEM((4, channels), F32),
            pltpu.VMEM((all_rows, 128), F32),
            pltpu.VMEM((grad_rows, 128), BF16),
            pltpu.VMEM((grad_rows, 128), BF16),
            pltpu.VMEM((all_rows, 128), BF16),
            pltpu.VMEM((all_rows, 128), BF16),
            pltpu.VMEM((small_rows, own), F32),
            pltpu.VMEM((128, own), F32),
            pltpu.VMEM((128, own), F32),
            pltpu.VMEM((peers, small_rows // size, own), F32),
            DMA((5,)),
            DMA((5,)),
            DMA((3, bits)),
            DMA((3, bits)),
            DMA((3, bits)),
            DMA((3, bits)),
            DMA((peers,)),
            DMA((peers,)),
            DMA((peers,)),
            DMA((peers,)),
        ],
        compiler_params=pltpu.CompilerParams(
            vmem_limit_bytes=VMEM_LIMIT, collective_id=0, has_side_effects=True
        ),
        name="block",
    )(
        grid_class,
        extent_row,
        rate,
        freq,
        coef,
        skip_gain.reshape(1, own),
        b_in.reshape(1, half_hidden),
        vec,
        w_in,
        w_out,
        x,
        cot,
    )
    g_rate, g_freq, g_coef, g_skip, g_vec, dw_in, db_in, dw_out = pl.pallas_call(
        final_kernel,
        out_shape=(
            shape((2, modes, own)),
            shape((2, modes, own)),
            shape((2, modes, own)),
            shape((1, own)),
            shape((4, channels)),
            shape(w_in.shape),
            shape((1, half_hidden)),
            shape(w_out.shape),
        ),
        in_specs=[VM] * 6,
        out_specs=(VM,) * 8,
        compiler_params=pltpu.CompilerParams(vmem_limit_bytes=VMEM_LIMIT),
        name="final",
    )(extent_row, rate, freq, coef, full, small)
    return (
        from_rows(block_out, pixels),
        from_rows(dx, pixels),
        g_rate.transpose(0, 2, 1),
        g_freq.transpose(0, 2, 1),
        g_coef.transpose(0, 2, 1),
        g_skip[0],
        g_vec[0],
        g_vec[1],
        dw_in,
        db_in[0],
        dw_out,
        g_vec[3],
        g_vec[2],
    )


def solution(mesh):
    placed = (
        P(None, ("dp", "mp"), None, None),
        P(None, "dp"),
        P("mp"),
        P(None, "mp", None),
        P(None, "mp", None),
        P(None, "mp", None),
        P("mp"),
        P(),
        P(),
        P(None, "mp"),
        P("mp"),
        P("mp", None),
        P(),
        P(),
        P(None, ("dp", "mp"), None, None),
    )
    return jax.shard_map(
        partial(on_device, mesh.shape["dp"]),
        mesh=mesh,
        in_specs=placed,
        out_specs=(
            P(None, ("dp", "mp"), None, None),
            P(None, ("dp", "mp"), None, None),
            P(None, "mp", None),
            P(None, "mp", None),
            P(None, "mp", None),
            P("mp"),
            P(),
            P(),
            P(None, "mp"),
            P("mp"),
            P("mp", None),
            P(),
            P(),
        ),
        check_vma=False,
    )
```

time: 374 us -> 109 us (0.29)
  waiting for transfers between devices: 228 us -> 0 us
  blocking collectives: 45.4 us -> 0 us
  Pallas kernels: 63.6 us -> 89.1 us
  between operations: 15 us -> 0.71 us
  local copies, waits for them, and re-layouts: 22 us -> 16.4 us
    psum x2 -> x0, waiting for transfers between devices: 213 us -> none  [the longest x1 133 us: on_device(): lax.psum(lax.psum_scatter(dw_in, 'mp', scatter_dimension=1, tiled=True),...]
    psum x1 -> x0, blocking collectives: 40.7 us -> none  [on_device(): db_in, dk, dskip, small = lax.psum((db_in, dk, dskip, small), ('dp', 'mp'))]
    pallas_call x4 -> x2, Pallas kernels: 63.6 us -> 89.1 us  [the longest x1 83.4 us: on_device(): pl.pallas_call(partial(mega_kernel, size), out_shape=(shape(field, BF16),...]
    reduce_scatter x2 -> x0, waiting for transfers between devices: 6.72 us -> none  [the longest x1 6.7 us: on_device(): lax.psum_scatter(dw_out, 'mp', scatter_dimension=0, tiled=True)]
    unnamed x36 -> x4, local copies, waits for them, and re-layouts: 6.18 us -> 0.01 us
    all_gather x2 -> x0, waiting for transfers between devices: 5.42 us -> none  [the longest x1 5.42 us: on_device(): w_out_all = lax.all_gather(w_out, 'mp', axis=0, tiled=True)]
  transfers between devices with their start and end apart: 6 -> 0, of which waited for: 4 -> 0; matrix products, arithmetic and copies ran while one was open for 5% -> 0% of each run, Pallas kernels for 7% -> 0%
where the time goes in v2:
time: 109 us; the launch traced here: 108 us
  Pallas kernels  89.1 us (82%)
  local copies, waits for them, and re-layouts  16.4 us (15%)
  other arithmetic  1.88 us (2%)
    pallas_call x1, Pallas kernels, on_device(): pl.pallas_call(partial(mega_kernel, size), out_shape=(shape(field, BF16),...  83.4 us
    pallas_call x1, Pallas kernels, on_device(): pl.pallas_call(final_kernel, out_shape=(shape((2, modes, own)), shape((2,...  5.69 us
    reshape x2, local copies, waits for them, and re-layouts, from_rows(): return rows.reshape(cells, micro, count, channels).transpose(1, 2, 3, 0)  3.11 us
    another operation x4, local copies, waits for them, and re-layouts, on_device(): vec = jnp.stack([norm_gain, norm_bias, b_out, layer_scale])  2.73 us
    transpose x1, local copies, waits for them, and re-layouts, from_rows(): return rows.reshape(cells, micro, count, channels).transpose(1, 2, 3, 0)  2.64 us
    reshape x2, local copies, waits for them, and re-layouts, to_rows(): return images.transpose(3, 0, 1, 2).reshape(cells * micro * count, channels)  2.64 us
    transpose x2, local copies, waits for them, and re-layouts, to_rows(): return images.transpose(3, 0, 1, 2).reshape(cells * micro * count, channels)  2.57 us

profile of v2, /device:TPU:0, one launch (start us, length us, event | category | flops | bytes accessed | tf_op | source)
XLA Modules:
  0.0 108.2 jit_solution(16768317429753669388)
XLA Ops:
  0.6 0.7 stack.15
  1.3 0.7 stack.16
  2.0 0.7 stack.17
  2.7 0.7 stack.18
  3.4 0.6 pad_maximum_fusion.vec_ref
  4.0 1.3 %reshape.49.b_in_ref = f32[1,768]{1,0:T(1,128)} reshape(f32[768]{0:T(1024)} %param.25) | data formatting | bytes 6144 | tf_op jit(solution)/shard_map/reshape | solution.py:996
  5.2 1.9 %copy.28 = bf16[324,2,2,384]{3,2,1,0:T(2,128)(2,1)S(1)} copy(bf16[324,2,2,384]{3,2,0,1:T(2,128)(2,1)} %bitcast.15) | data formatting | bytes 1990656 | tf_op jit(solution)/shard_map/transpose | solution.py:881
  7.1 0.0 copy-start
  7.2 1.3 %reshape.50.x_ref = bf16[1296,384]{1,0:T(8,128)(2,1)} reshape(bf16[324,2,2,384]{3,2,1,0:T(2,128)(2,1)S(1)} %copy.28) | data formatting | bytes 1990656 | tf_op jit(solution)/shard_map/reshape | solution.py:881
  8.5 0.0 copy-done
  8.5 0.7 copy.29
  9.2 1.3 %reshape.51.cot_ref = bf16[1296,384]{1,0:T(8,128)(2,1)} reshape(bf16[324,2,2,384]{3,2,1,0:T(2,128)(2,1)S(1)} %copy.29) | data formatting | bytes 1990656 | tf_op jit(solution)/shard_map/reshape | solution.py:881
  10.5 83.4 %block.1 = (bf16[1296,384]{1,0:T(8,128)(2,1)}, bf16[1296,384]{1,0:T(8,128)(2,1)}, bf16[4608,128]{1,0:T(8,128)(2,1)}, f32[128,192]{1,0:T(8,128)}) custom-call(s32[2,4]{1,0:T(2,128)} %class_ref.1, s32[1,192]{1,0:T(1,128)} %bitcast.23, f32[2,64,192]{2,1,0:T(8,128)} %bitcast.17, f32[2,64,192]{2,1,0:T(8,128)} %bitcast.19, f32[2,64,192]{2,1,0:T(8,128)} %bitcast.21, ...), custom_call_target="tpu_custom_call" | custom-call | tf_op jit(solution)/shard_map/block/pallas_call | solution.py:926
  93.9 0.0 copy-start.1
  93.9 2.7 %reshape.52 = bf16[324,2,2,384]{3,2,1,0:T(2,128)(2,1)S(1)} reshape(bf16[1296,384]{1,0:T(8,128)(2,1)} %get-tuple-element.25) | data formatting | bytes 1990656 | tf_op jit(solution)/shard_map/reshape | solution.py:886
  96.7 0.0 copy-done.1
  96.7 0.4 reshape.53
  97.1 2.6 %copy_bitcast_fusion = (bf16[2,2,384,324]{2,1,3,0:T(2,128)(2,1)}, bf16[2,2,384,324]{2,1,3,0:T(2,128)(2,1)}) fusion(bf16[324,2,2,384]{3,2,1,0:T(2,128)(2,1)S(1)} %reshape.53, bf16[324,2,2,384]{3,2,1,0:T(2,128)(2,1)S(1)} %reshape.52), kind=kLoop, calls=%fused_computation | loop fusion | bytes 3981312 | tf_op jit(solution)/shard_map/transpose | solution.py:886
  99.7 5.7 %final.1 = (f32[2,64,192]{2,1,0:T(8,128)}, f32[2,64,192]{2,1,0:T(8,128)}, f32[2,64,192]{2,1,0:T(8,128)}, f32[1,192]{1,0:T(1,128)}, f32[4,384]{1,0:T(4,128)}, /*i...) custom-call(s32[1,192]{1,0:T(1,128)} %bitcast.24, f32[2,64,192]{2,1,0:T(8,128)} %bitcast.18, ...), custom_call_target="tpu_custom_call" | custom-call | tf_op jit(solution)/shard_map/final/pallas_call | solution.py:1003
  105.4 1.3 %reduce.2 = f32[768]{0:T(1024)} reduce(f32[1,768]{1,0:T(1,128)} %get-tuple-element.35, f32[]{:T(128)} %constant.3), dimensions={0}, to_apply=%get-tuple-element.35.reduce_sub_computation | reduce | bytes 6148 | tf_op jit(solution)/shard_map/final/pallas_call | solution.py:1003
  106.7 1.4 %slice_reduce_fusion = (f32[384]{0:T(512)}, f32[384]{0:T(512)}, f32[384]{0:T(512)}, f32[384]{0:T(512)}) fusion(f32[4,384]{1,0:T(4,128)} %get-tuple-element.33), kind=kLoop, calls=%fused_computation.3 | loop fusion | bytes 12288 | tf_op jit(solution)/shard_map/slice | solution.py:1033
Async XLA Ops:
  7.1 1.3 %copy-start = (bf16[2,2,384,324]{2,1,3,0:T(2,128)(2,1)S(1)}, bf16[2,2,384,324]{2,1,3,0:T(2,128)(2,1)}, u32[]{:S(2)}) copy-start(bf16[2,2,384,324]{2,1,3,0:T(2,128)(2,1)} %param.29) | copy-start | bytes 2985988
  93.9 2.8 %copy-start.1 = (bf16[1296,384]{1,0:T(8,128)(2,1)S(1)}, bf16[1296,384]{1,0:T(8,128)(2,1)}, u32[]{:S(2)}) copy-start(bf16[1296,384]{1,0:T(8,128)(2,1)} %get-tuple-element.26) | copy-start | bytes 2985988

commit v3 on v2

--- a/solution.py
+++ b/solution.py
@@ -26,6 +26,7 @@
     0.77818103,
     -0.19910822,
 )
+CHUNK = 256
 VMEM_LIMIT = 60 * 1024 * 1024
 
 
@@ -51,6 +52,7 @@
 SMALL_ROWS = 121
 
 def write_tables(extent_ref, rate_ref, freq_ref, coef_ref, out_ref):
+    extent = extent_ref[...].reshape(1, extent_ref.shape[0])
     for axis in range(2):
         for cat, side in enumerate(SIDES):
             z_re, z_im = mode_step(rate_ref[axis], freq_ref[axis], side)
@@ -62,12 +64,13 @@
                     out_ref[row : row + 1, :] = jnp.zeros((1, w_re.shape[1]), F32)
                     continue
                 total = jnp.sum(w_re, axis=0, keepdims=True)
-                out_ref[row : row + 1, :] = jnp.where(extent_ref[...] > lag, total, 0.0)
+                out_ref[row : row + 1, :] = jnp.where(extent > lag, total, 0.0)
                 if lag < side - 1:
                     w_re, w_im = w_re * z_re - w_im * z_im, w_re * z_im + w_im * z_re
 
 
 def modes_grad(extent_ref, rate_ref, freq_ref, coef_ref, dk_ref, rate_out, freq_out, coef_out):
+    extent = extent_ref[...].reshape(1, extent_ref.shape[0])
     for axis in range(2):
         coef = coef_ref[axis]
         g_rate = jnp.zeros_like(coef)
@@ -81,7 +84,7 @@
             q_im = jnp.zeros_like(coef)
             for lag in reversed(range(side)):
                 row = axis * LAGS + cat * GRID + lag
-                d = jnp.where(extent_ref[...] > lag, dk_ref[row : row + 1, :], 0.0)
+                d = jnp.where(extent > lag, dk_ref[row : row + 1, :], 0.0)
                 p_re, p_im = p_re * z_re - p_im * z_im + d, p_re * z_im + p_im * z_re
                 q_re, q_im = q_re * z_re - q_im * z_im + float(lag) * d, q_re * z_im + q_im * z_re
             g_coef = g_coef + p_re
@@ -278,53 +281,48 @@
 
 
 def row_correlate(left_ref, right_ref, acc_ref, cut=3):
-    tiles = left_ref.shape[1] // 128
-    blocks = HALF // cut
-
-    def body(step, carry):
-        tile = step // (2 * blocks)
-        rest = lax.rem(step, 2 * blocks)
-        rho = rest // blocks
-        first = lax.rem(rest, blocks) * cut
-        at = lanes(tile)
-        sums = [[None] * HALF for _ in range(cut)]
-        for j in range(HALF):
-            left = [left_ref[rows8(rho * 81 + (first + k) * HALF + j), at] for k in range(cut)]
-            for p in range(HALF):
-                right = right_ref[rows8(rho * 81 + p * HALF + j), at]
+    for tile in range(left_ref.shape[1] // 128):
+        for rho in range(2):
+
+            def body(step, carry, at=lanes(tile), rho=rho):
+                first = step * cut
+                sums = [[None] * HALF for _ in range(cut)]
+                for j in range(HALF):
+                    left = [
+                        left_ref[rows8(rho * 81 + (first + k) * HALF + j), at] for k in range(cut)
+                    ]
+                    for p in range(HALF):
+                        right = right_ref[rows8(rho * 81 + p * HALF + j), at]
+                        for k in range(cut):
+                            term = left[k] * right
+                            sums[k][p] = term if sums[k][p] is None else sums[k][p] + term
                 for k in range(cut):
-                    term = left[k] * right
-                    sums[k][p] = term if sums[k][p] is None else sums[k][p] + term
-        for k in range(cut):
-            for p in range(HALF):
-                acc_ref[rows8(rho * 81 + (first + k) * HALF + p), at] = sums[k][p]
-        return carry
-
-    lax.fori_loop(0, tiles * 2 * blocks, body, 0)
+                    for p in range(HALF):
+                        acc_ref[rows8(rho * 81 + (first + k) * HALF + p), at] = sums[k][p]
+                return carry
+
+            lax.fori_loop(0, HALF // cut, body, 0)
 
 
 def col_correlate(left_ref, right_ref, acc_ref, cut=3):
-    tiles = left_ref.shape[1] // 128
-    blocks = HALF // cut
-
-    def body(step, carry):
-        tile = step // blocks
-        first = lax.rem(step, blocks) * cut
-        at = lanes(tile)
-        sums = [[None] * HALF for _ in range(cut)]
-        for i in range(2 * HALF):
-            left = [left_ref[rows8(i * HALF + first + k), at] for k in range(cut)]
-            for q in range(HALF):
-                right = right_ref[rows8(i * HALF + q), at]
-                for k in range(cut):
-                    term = left[k] * right
-                    sums[k][q] = term if sums[k][q] is None else sums[k][q] + term
-        for k in range(cut):
-            for q in range(HALF):
-                acc_ref[rows8((first + k) * HALF + q), at] = sums[k][q]
-        return carry
-
-    lax.fori_loop(0, tiles * blocks, body, 0)
+    for tile in range(left_ref.shape[1] // 128):
+
+        def body(step, carry, at=lanes(tile)):
+            first = step * cut
+            sums = [[None] * HALF for _ in range(cut)]
+            for i in range(2 * HALF):
+                left = [left_ref[rows8(i * HALF + first + k), at] for k in range(cut)]
+                for q in range(HALF):
+                    right = right_ref[rows8(i * HALF + q), at]
+                    for k in range(cut):
+                        term = left[k] * right
+                        sums[k][q] = term if sums[k][q] is None else sums[k][q] + term
+            for k in range(cut):
+                for q in range(HALF):
+                    acc_ref[rows8((first + k) * HALF + q), at] = sums[k][q]
+            return carry
+
+        lax.fori_loop(0, HALF // cut, body, 0)
 
 
 def gather_lags(class_ref, row_acc, col_acc, dk_ref):
@@ -363,26 +361,29 @@
     lax.fori_loop(0, tiles, body, 0)
 
 
-def bit_orders(size):
+def bit_orders(size, parts):
     bits = size.bit_length() - 1
     turn = min(3, max(bits, 1))
     base = list(range(bits))
     return [
-        [base[(k + part) % turn] if k < turn else base[k] for k in range(bits)] for part in range(3)
+        [base[(k + part) % turn] if k < turn else base[k] for k in range(bits)]
+        for part in range(parts)
     ]
 
 
-def chunk_rows(total, size):
-    per = -(-total // (3 * size))
-    return -(-per // 16) * 16
+def ring_plan(rows, size):
+    parts = 3 if rows % (48 * size) == 0 else 1
+    per = -(-rows // (parts * size))
+    return parts, -(-per // 16) * 16
 
 
 class Ring:
-    def __init__(self, size, rows, acc, send, recv, full, sems):
-        self.size, self.rows = size, rows
+    def __init__(self, group, size, plan, acc, send, recv, full, sems):
+        self.group, self.size = group, size
+        self.parts, self.rows = plan
         self.acc, self.send, self.recv, self.full = acc, send, recv, full
         self.send_sem, self.recv_sem, self.back_send, self.back_recv = sems
-        self.orders = bit_orders(size)
+        self.orders = bit_orders(size, self.parts)
         self.bits = size.bit_length() - 1
         self.me = lax.axis_index("dp")
         self.place = []
@@ -392,6 +393,9 @@
                 place = place * 2 + lax.rem(self.me // (1 << bit), 2)
             self.place.append(place)
 
+    def base(self, part):
+        return (self.group * self.parts + part) * self.size * self.rows
+
     def peer(self, bit):
         mine = lax.rem(self.me // (1 << bit), 2)
         return self.me + (1 - 2 * mine) * (1 << bit)
@@ -400,22 +404,24 @@
         half = self.size >> (step + 1)
         index = self.place[part] // half
         mine = lax.rem(index, 2)
-        base = part * self.size * self.rows
-        keep = base + index * half * self.rows
-        away = base + (index + 1 - 2 * mine) * half * self.rows
+        keep = self.base(part) + index * half * self.rows
+        away = self.base(part) + (index + 1 - 2 * mine) * half * self.rows
         return pl.multiple_of(keep, 16), pl.multiple_of(away, 16), half * self.rows
 
     def slot(self, part, step):
         done = self.size - (self.size >> step)
-        return (part * self.size + done) * self.rows
+        return self.base(part) + done * self.rows
+
+    def sem(self, sems, part, step):
+        return sems.at[self.group * self.parts + part, step]
 
     def reduce_copy(self, part, step):
         _, away, length = self.span(part, step)
         return pltpu.make_async_remote_copy(
             src_ref=self.send.at[pl.ds(away, length), :],
             dst_ref=self.recv.at[pl.ds(self.slot(part, step), length), :],
-            send_sem=self.send_sem.at[part, step],
-            recv_sem=self.recv_sem.at[part, step],
+            send_sem=self.sem(self.send_sem, part, step),
+            recv_sem=self.sem(self.recv_sem, part, step),
             device_id={"dp": self.peer(self.orders[part][step])},
             device_id_type=pl.DeviceIdType.MESH,
         )
@@ -425,58 +431,77 @@
         return pltpu.make_async_remote_copy(
             src_ref=self.full.at[pl.ds(keep, length), :],
             dst_ref=self.full.at[pl.ds(keep, length), :],
-            send_sem=self.back_send.at[part, step],
-            recv_sem=self.back_recv.at[part, step],
+            send_sem=self.sem(self.back_send, part, step),
+            recv_sem=self.sem(self.back_recv, part, step),
             device_id={"dp": self.peer(self.orders[part][step])},
             device_id_type=pl.DeviceIdType.MESH,
         )
 
     def reduce_start(self, step):
-        for part in range(3):
+        for part in range(self.parts):
             _, away, length = self.span(part, step)
             copy_rows(self.acc, away, self.send, away, length, lambda v: v.astype(BF16))
             self.reduce_copy(part, step).start()
 
     def reduce_finish(self, step):
-        for part in range(3):
+        for part in range(self.parts):
             self.reduce_copy(part, step).wait_recv()
             keep, _, length = self.span(part, step)
-            slot = self.slot(part, step)
-
-            def body(t, carry, keep=keep, slot=slot):
-                at = pl.ds(pl.multiple_of(keep + t * 48, 16), 48)
-                other = pl.ds(pl.multiple_of(slot + t * 48, 16), 48)
-                self.acc[at, :] += self.recv[other, :].astype(F32)
-                return carry
-
-            if length % 48 == 0:
-                lax.fori_loop(0, length // 48, body, 0)
-            else:
-                self.acc[pl.ds(keep, length), :] += self.recv[pl.ds(slot, length), :].astype(F32)
+            add_rows(self.recv, self.slot(part, step), self.acc, keep, length)
 
     def gather_first(self):
-        for part in range(3):
-            own = pl.multiple_of((part * self.size + self.place[part]) * self.rows, 16)
+        for part in range(self.parts):
+            own = pl.multiple_of(self.base(part) + self.place[part] * self.rows, 16)
             copy_rows(self.acc, own, self.full, own, self.rows, lambda v: v.astype(BF16))
 
     def gather_start(self, step):
-        for part in range(3):
+        for part in range(self.parts):
             self.gather_copy(part, step).start()
 
     def gather_finish(self, step):
-        for part in range(3):
+        for part in range(self.parts):
             self.gather_copy(part, step).wait_recv()
 
+    def advance(self, step):
+        bits = self.bits
+        if step > 2 * bits:
+            return
+        if 0 < step <= bits:
+            self.reduce_finish(step - 1)
+        if step > bits:
+            self.gather_finish(2 * bits - step)
+        if step < bits:
+            self.reduce_start(step)
+        if step == bits:
+            self.gather_first()
+        if bits <= step < 2 * bits:
+            self.gather_start(2 * bits - 1 - step)
+
     def close(self):
-        for part in range(3):
+        for part in range(self.parts):
             for step in range(self.bits):
                 self.reduce_copy(part, step).wait_send()
                 self.gather_copy(part, step).wait_send()
 
 
-def copy_rows(source, first, target, where, length, change, block=48):
-    if length % block:
-        block = 16
+def row_block(length):
+    return next(block for block in (128, 96, 64, 48, 32, 16) if length % block == 0)
+
+
+def add_rows(source, first, target, where, length):
+    block = row_block(length)
+
+    def body(t, carry):
+        here = pl.ds(pl.multiple_of(first + t * block, 16), block)
+        there = pl.ds(pl.multiple_of(where + t * block, 16), block)
+        target[there, :] += source[here, :].astype(F32)
+        return carry
+
+    lax.fori_loop(0, length // block, body, 0)
+
+
+def copy_rows(source, first, target, where, length, change):
+    block = row_block(length)
 
     def body(t, carry):
         here = pl.ds(pl.multiple_of(first + t * block, 16), block)
@@ -489,6 +514,17 @@
 
 def wide(ref, first, count):
     return jnp.concatenate([ref[first + k : first + k + 1, :] for k in range(count)], axis=1)
+
+
+def images_in(ref, first, count):
+    parts = [ref[micro, pl.ds(first, count), :, :].astype(F32) for micro in range(2)]
+    return jnp.concatenate(parts, axis=1).reshape(4 * count, ref.shape[3])
+
+
+def images_out(ref, first, count, value):
+    value = value.reshape(count, 4, ref.shape[3])
+    for micro in range(2):
+        ref[micro, pl.ds(first, count)] = value[:, 2 * micro : 2 * micro + 2, :].astype(BF16)
 
 
 def mega_kernel(
@@ -500,7 +536,10 @@
     coef_ref,
     skip_ref,
     b_in_ref,
-    vec_ref,
+    gain_ref,
+    shift_ref,
+    b_out_ref,
+    scale_ref,
     w_in_ref,
     w_out_ref,
     x_ref,
@@ -557,7 +596,8 @@
     bc_send,
     bc_recv,
 ):
-    rows, channels = x_ref.shape
+    cells, channels = x_ref.shape[1], x_ref.shape[3]
+    rows = 4 * cells
     own = pack_own.shape[1]
     half_hidden = w_in_ref.shape[1]
     me = lax.axis_index("dp")
@@ -585,9 +625,10 @@
         )
 
     write_tables(extent_ref, rate_ref, freq_ref, coef_ref, pack_own)
-    pack_own[108:109, :] = skip_ref[...]
+    pack_own[108:109, :] = skip_ref[...].reshape(1, own)
+    b_in = b_in_ref[...].reshape(1, half_hidden)
     for k in range(4):
-        pack_own[109 + k : 110 + k, :] = b_in_ref[:, k * own : (k + 1) * own]
+        pack_own[109 + k : 110 + k, :] = b_in[:, k * own : (k + 1) * own]
     pack_own[113:PACK_ROWS, :] = jnp.zeros((PACK_ROWS - 113, own), F32)
     pl.semaphore_wait(barrier, size)
     pack_copy = pair_copy(0, pack_own, pack_oth)
@@ -599,16 +640,16 @@
 
     build_masks(class_ref, mask_ref)
     block = 144
-    scale = vec_ref[3:4, :]
+    scale = scale_ref[...].reshape(1, channels)
 
     def load(t, carry):
-        at = pl.ds(pl.multiple_of(t * block, block), block)
-        u_ref[at, :] = x_ref[at, :].astype(F32)
+        at = pl.ds(pl.multiple_of(t * 48, 16), 48)
+        u_ref[at, :] = images_in(x_ref, t * 12, 12)
         mask = jnp.tile(mask_ref[at, :], (1, channels // 128))
-        gmlp_ref[at, :] = (cot_ref[at, :].astype(F32) * scale * mask).astype(BF16)
-        return carry
-
-    lax.fori_loop(0, rows // block, load, 0)
+        gmlp_ref[at, :] = (images_in(cot_ref, t * 12, 12) * scale * mask).astype(BF16)
+        return carry
+
+    lax.fori_loop(0, rows // 48, load, 0)
     mirror_in(u_ref, mask_ref, uh_ref)
 
     pack_copy.wait_recv()
@@ -622,8 +663,8 @@
     apply_cols(colop_ref, v_ref, mh_ref)
     mirror_out(mh_ref, mask_ref, mixed_ref, u_ref, skip_all)
 
-    gain = vec_ref[0:1, :]
-    shift = vec_ref[1:2, :]
+    gain = gain_ref[...].reshape(1, channels)
+    shift = shift_ref[...].reshape(1, channels)
 
     def norm(t, carry):
         at = pl.ds(pl.multiple_of(t * block, block), block)
@@ -640,106 +681,115 @@
 
     lax.fori_loop(0, rows // block, norm, 0)
 
-    chunk = 256
+    chunk = CHUNK
     tile_rows = 432
-    mlp_ref[...] = jnp.broadcast_to(vec_ref[2:3, :], mlp_ref.shape)
+    mlp_ref[...] = jnp.broadcast_to(b_out_ref[...].reshape(1, channels), mlp_ref.shape)
     gn_ref[...] = jnp.zeros_like(gn_ref)
     first_copy.wait_recv()
     second_copy.wait_recv()
 
-    def feed(w_first_ref, w_second_ref, bias_row, target_ref, db_row):
-        db_ref[2:3, :] = bias_row
-
-        def body(f, carry):
-            cols = pl.ds(pl.multiple_of(f * chunk, chunk), chunk)
-            w_first = w_first_ref[:, cols]
-            w_second = w_second_ref[cols, :]
-            bias = db_ref[2:3, cols]
-            db = jnp.zeros((1, chunk), F32)
-            for t in range(rows // tile_rows):
-                at = pl.ds(t * tile_rows, tile_rows)
-                pre = jnp.dot(normed_ref[at, :], w_first, preferred_element_type=F32) + bias
-                size_of = jnp.abs(pre)
-                inv = 1.0 / (1.0 + ERF_SHIFT * size_of)
-                poly = jnp.full_like(inv, 0.5 * ERF_POLY[-1])
-                for value in reversed(ERF_POLY[:-1]):
-                    poly = poly * inv + 0.5 * value
-                bell = jnp.exp(-0.5 * pre * pre)
-                tail = poly * inv * bell
-                cdf = jnp.where(pre >= 0.0, 1.0 - tail, tail)
-                act = (pre * cdf).astype(BF16)
-                slope = cdf + pre * bell * (1.0 / math.sqrt(2.0 * math.pi))
-                g_act = lax.dot_general(
-                    gmlp_ref[at, :], w_second, (((1,), (1,)), ((), ())), preferred_element_type=F32
-                )
-                g_pre = (g_act * slope).astype(BF16)
-                db = db + jnp.sum(g_pre.astype(F32), axis=0, keepdims=True)
-                act_ref[at, :] = act
-                gpre_ref[at, :] = g_pre
-                mlp_ref[at, :] += jnp.dot(act, w_second, preferred_element_type=F32)
-                gn_ref[at, :] += lax.dot_general(
-                    g_pre, w_first, (((1,), (1,)), ((), ())), preferred_element_type=F32
-                )
-            db_ref[db_row : db_row + 1, cols] = db
-            d_first = lax.dot_general(
-                normed_ref[...], gpre_ref[...], (((0,), (0,)), ((), ())), preferred_element_type=F32
+    group_rows = 2 * channels * chunk // 128
+    plan = ring_plan(group_rows, size)
+    stride = plan[0] * plan[1] * size
+    groups = half_hidden // chunk
+    rings = [
+        Ring(group, size, plan, acc_ref, send_ref, recv_ref, full_out,
+             (red_send, red_recv, gat_send, gat_recv))
+        for group in range(groups)
+    ]
+    db_ref[2:3, :] = wide(pack_oth, 109, 4)
+    db_ref[3:4, :] = b_in
+
+    def feed(f, w_first_ref, w_second_ref, bias_row, target_ref, target_base, db_row):
+        cols = pl.ds(pl.multiple_of(f * chunk, chunk), chunk)
+        w_first = w_first_ref[:, cols]
+        w_second = w_second_ref[cols, :]
+        bias = db_ref[bias_row : bias_row + 1, cols]
+        db = jnp.zeros((1, chunk), F32)
+        for t in range(rows // tile_rows):
+            at = pl.ds(t * tile_rows, tile_rows)
+            pre = jnp.dot(normed_ref[at, :], w_first, preferred_element_type=F32) + bias
+            inv = 1.0 / (1.0 + ERF_SHIFT * jnp.abs(pre))
+            poly = jnp.full_like(inv, 0.5 * ERF_POLY[-1])
+            for value in reversed(ERF_POLY[:-1]):
+                poly = poly * inv + 0.5 * value
+            bell = jnp.exp(-0.5 * pre * pre)
+            tail = poly * inv * bell
+            cdf = jnp.where(pre >= 0.0, 1.0 - tail, tail)
+            act = (pre * cdf).astype(BF16)
+            slope = cdf + pre * bell * (1.0 / math.sqrt(2.0 * math.pi))
+            g_act = lax.dot_general(
+                gmlp_ref[at, :], w_second, (((1,), (1,)), ((), ())), preferred_element_type=F32
             )
-            for k in range(chunk // 128):
-                at = pl.ds(pl.multiple_of((f * (chunk // 128) + k) * channels, channels), channels)
-                target_ref[at, :] = d_first[:, k * 128 : (k + 1) * 128].astype(target_ref.dtype)
-            d_second = lax.dot_general(
-                act_ref[...], gmlp_ref[...], (((0,), (0,)), ((), ())), preferred_element_type=F32
+            g_pre = (g_act * slope).astype(BF16)
+            db = db + jnp.sum(g_pre.astype(F32), axis=0, keepdims=True)
+            act_ref[at, :] = act
+            gpre_ref[at, :] = g_pre
+            mlp_ref[at, :] += jnp.dot(act, w_second, preferred_element_type=F32)
+            gn_ref[at, :] += lax.dot_general(
+                g_pre, w_first, (((1,), (1,)), ((), ())), preferred_element_type=F32
             )
-            base = channels * (half_hidden // 128)
-            for k in range(channels // 128):
-                at = pl.ds(pl.multiple_of(base + k * half_hidden + f * chunk, chunk), chunk)
-                target_ref[at, :] = d_second[:, k * 128 : (k + 1) * 128].astype(target_ref.dtype)
-            return carry
-
-        lax.fori_loop(0, half_hidden // chunk, body, 0)
-
-    feed(w_in_oth, w_out_oth, wide(pack_oth, 109, 4), away_ref, 1)
-    grads_copy = pair_copy(3, away_ref, landed_ref)
-    grads_copy.start()
-    feed(w_in_ref, w_out_ref, b_in_ref[...], acc_ref, 0)
-
-    ring = Ring(size, chunk_rows(away_ref.shape[0], size), acc_ref, send_ref, recv_ref, full_out,
-                (red_send, red_recv, gat_send, gat_recv))
-    grads_copy.wait_recv()
-
-    def add_pair(t, carry):
-        at = pl.ds(pl.multiple_of(t * 96, 96), 96)
-        acc_ref[at, :] += landed_ref[at, :].astype(F32)
-        return carry
-
-    lax.fori_loop(0, away_ref.shape[0] // 96, add_pair, 0)
-    pad = acc_ref.shape[0] - away_ref.shape[0]
-    if pad:
-        acc_ref[away_ref.shape[0] :, :] = jnp.zeros((pad, 128), F32)
-
-    def advance(step):
-        if step > 2 * ring.bits:
-            return
-        if 0 < step <= ring.bits:
-            ring.reduce_finish(step - 1)
-        if step > ring.bits:
-            ring.gather_finish(2 * ring.bits - step)
-        if step < ring.bits:
-            ring.reduce_start(step)
-        if step == ring.bits:
-            ring.gather_first()
-        if ring.bits <= step < 2 * ring.bits:
-            ring.gather_start(2 * ring.bits - 1 - step)
-
-    advance(0)
+        db_ref[db_row : db_row + 1, cols] = db
+        d_first = lax.dot_general(
+            normed_ref[...], gpre_ref[...], (((0,), (0,)), ((), ())), preferred_element_type=F32
+        )
+        for k in range(chunk // 128):
+            at = pl.ds(pl.multiple_of(target_base + k * channels, 128), channels)
+            target_ref[at, :] = d_first[:, k * 128 : (k + 1) * 128].astype(target_ref.dtype)
+        d_second = lax.dot_general(
+            act_ref[...], gmlp_ref[...], (((0,), (0,)), ((), ())), preferred_element_type=F32
+        )
+        base = target_base + channels * (chunk // 128)
+        for k in range(channels // 128):
+            at = pl.ds(pl.multiple_of(base + k * chunk, 128), chunk)
+            target_ref[at, :] = d_second[:, k * 128 : (k + 1) * 128].astype(target_ref.dtype)
+
+    def grads_copy(group):
+        at = pl.ds(pl.multiple_of(group * group_rows, 16), group_rows)
+        return pair_copy(4 + group, away_ref.at[at, :], landed_ref.at[at, :])
+
+    def join(group):
+        grads_copy(group).wait_recv()
+        add_rows(landed_ref, pl.multiple_of(group * group_rows, 16), acc_ref,
+                 pl.multiple_of(group * stride, 16), group_rows)
+        if stride > group_rows:
+            acc_ref[pl.ds(pl.multiple_of(group * stride + group_rows, 16), stride - group_rows), :] = (
+                jnp.zeros((stride - group_rows, 128), F32)
+            )
+
+    def tick(count):
+        for group in reversed(range(groups)):
+            step = count - 2 * group
+            if 0 <= step <= 2 * rings[group].bits:
+                rings[group].advance(step)
+
+    def pair_of_chunks(f, carry):
+        feed(f, w_in_oth, w_out_oth, 2, away_ref, f * group_rows, 1)
+        grads_copy(f).start()
+        for count in range(1, groups):
+            pl.when(f == count)(partial(tick, 2 * count - 1))
+        feed(f, w_in_ref, w_out_ref, 3, acc_ref, f * stride, 0)
+        join(f)
+        for count in range(groups):
+            pl.when(f == count)(partial(tick, 2 * count))
+        return carry
+
+    lax.fori_loop(0, groups, pair_of_chunks, 0)
+    last = 2 * rings[0].bits + 2 * (groups - 1)
+    ticks = iter(range(2 * groups - 1, last + 1))
+
+    def advance():
+        count = next(ticks, None)
+        if count is not None:
+            tick(count)
 
     def back(t, carry):
         d_gain, d_bias, d_scale, d_b_out = carry
-        at = pl.ds(pl.multiple_of(t * block, block), block)
+        at = pl.ds(pl.multiple_of(t * 48, 16), 48)
         mask = jnp.tile(mask_ref[at, :], (1, channels // 128))
         branch = mlp_ref[at, :] * mask
-        block_out[at, :] = (u_ref[at, :] + scale * branch).astype(BF16)
-        d_scale = d_scale + jnp.sum(cot_ref[at, :].astype(F32) * branch, axis=0, keepdims=True)
+        images_out(block_out, t * 12, 12, u_ref[at, :] + scale * branch)
+        d_scale = d_scale + jnp.sum(images_in(cot_ref, t * 12, 12) * branch, axis=0, keepdims=True)
         d_b_out = d_b_out + jnp.sum(gmlp_ref[at, :].astype(F32), axis=0, keepdims=True)
         grad = gn_ref[at, :]
         hat = mixed_ref[at, :]
@@ -753,19 +803,19 @@
         return d_gain, d_bias, d_scale, d_b_out
 
     zero = jnp.zeros((1, channels), F32)
-    sums = lax.fori_loop(0, rows // block, back, (zero, zero, zero, zero))
+    sums = lax.fori_loop(0, rows // 48, back, (zero, zero, zero, zero))
     for index, value in enumerate(sums):
         sums_ref[index : index + 1, :] = value
 
     gh_ref, xh_ref = mh_ref, mlp_ref
+    advance()
     mirror_in(gm_ref, mask_ref, gh_ref)
-    advance(1)
     apply_cols(colop_ref, gh_ref, xh_ref)
-    advance(2)
+    advance()
     row_correlate(xh_ref, uh_ref, row_acc)
-    advance(3)
+    advance()
     col_correlate(gh_ref, v_ref, col_acc)
-    advance(4)
+    advance()
     gather_lags(class_ref, row_acc, col_acc, dk_ref)
 
     def skip_sum(t, total):
@@ -787,9 +837,10 @@
         small_keep[113 + k : 114 + k, :] = value
         small_send[113 + k : 114 + k, :] = value
     small_send[SMALL_ROWS:128, :] = jnp.zeros((128 - SMALL_ROWS, own), F32)
-    small_pair = pair_copy(4, small_send, small_land)
+    small_pair = pair_copy(3, small_send, small_land)
     small_pair.start()
     apply_rows(rowop_ref, xh_ref, gh_ref)
+    advance()
     small_pair.wait_recv()
     small_keep[0:128, :] += small_land[...]
 
@@ -821,6 +872,7 @@
     for offset in range(1, size):
         scatter_copy(offset).start()
     mirror_out(gh_ref, mask_ref, gn_ref, gm_ref, skip_all)
+    advance()
     total = small_keep[mine, :]
     for offset in range(1, size):
         scatter_copy(offset).wait_recv()
@@ -830,42 +882,48 @@
         spread_copy(offset).start()
 
     def finish(t, carry):
-        at = pl.ds(pl.multiple_of(t * block, block), block)
-        dx_out[at, :] = (cot_ref[at, :].astype(F32) + gn_ref[at, :]).astype(BF16)
-        return carry
-
-    lax.fori_loop(0, rows // block, finish, 0)
-    for step in range(5, 2 * ring.bits + 1):
-        advance(step)
-    if ring.bits == 0:
-        pass
+        at = pl.ds(pl.multiple_of(t * 48, 16), 48)
+        images_out(dx_out, t * 12, 12, images_in(cot_ref, t * 12, 12) + gn_ref[at, :])
+        return carry
+
+    lax.fori_loop(0, rows // 48, finish, 0)
+    for _ in range(last + 1):
+        advance()
     for offset in range(1, size):
         spread_copy(offset).wait_recv()
     for offset in range(1, size):
         scatter_copy(offset).wait_send()
         spread_copy(offset).wait_send()
-    ring.close()
-    for copy in (pack_copy, first_copy, second_copy, grads_copy, small_pair):
+    for group in range(groups):
+        rings[group].close()
+        grads_copy(group).wait_send()
+    for copy in (pack_copy, first_copy, second_copy, small_pair):
         copy.wait_send()
 
 
 def final_kernel(
     extent_ref, rate_ref, freq_ref, coef_ref, full_ref, small_ref, rate_out, freq_out, coef_out,
-    skip_out, vec_out, dw_in_out, db_in_out, dw_out_out,
+    skip_out, gain_out, bias_out, dw_in_out, db_in_out, dw_out_out, b_out_out, scale_out,
 ):
     channels, half_hidden = dw_in_out.shape
-    for k in range(half_hidden // 128):
-        dw_in_out[:, k * 128 : (k + 1) * 128] = full_ref[k * channels : (k + 1) * channels, :].astype(F32)
-    base = channels * (half_hidden // 128)
-    for k in range(channels // 128):
-        dw_out_out[:, k * 128 : (k + 1) * 128] = full_ref[
-            base + k * half_hidden : base + (k + 1) * half_hidden, :
-        ].astype(F32)
+    groups = half_hidden // CHUNK
+    stride = full_ref.shape[0] // groups
+    for group in range(groups):
+        base = group * stride
+        for k in range(CHUNK // 128):
+            at = group * CHUNK + k * 128
+            dw_in_out[:, at : at + 128] = full_ref[base : base + channels, :].astype(F32)
+            base += channels
+        for k in range(channels // 128):
+            dw_out_out[group * CHUNK : (group + 1) * CHUNK, k * 128 : (k + 1) * 128] = full_ref[
+                base : base + CHUNK, :
+            ].astype(F32)
+            base += CHUNK
     modes_grad(extent_ref, rate_ref, freq_ref, coef_ref, small_ref, rate_out, freq_out, coef_out)
-    skip_out[...] = small_ref[108:109, :]
-    db_in_out[...] = wide(small_ref, 109, 4)
-    for k in range(4):
-        vec_out[k : k + 1, :] = wide(small_ref, 113 + 2 * k, 2)
+    skip_out[...] = small_ref[108:109, :].reshape(skip_out.shape)
+    db_in_out[...] = wide(small_ref, 109, 4).reshape(db_in_out.shape)
+    for k, ref in enumerate((gain_out, bias_out, scale_out, b_out_out)):
+        ref[...] = wide(small_ref, 113 + 2 * k, 2).reshape(ref.shape)
 
 
 VM = pl.BlockSpec(memory_space=pltpu.VMEM)
@@ -874,16 +932,6 @@
 
 def shape(dims, kind=F32):
     return jax.ShapeDtypeStruct(dims, kind)
-
-
-def to_rows(images):
-    micro, count, channels, cells = images.shape
-    return images.transpose(3, 0, 1, 2).reshape(cells * micro * count, channels)
-
-
-def from_rows(rows, like):
-    micro, count, channels, cells = like.shape
-    return rows.reshape(cells, micro, count, channels).transpose(1, 2, 3, 0)
 
 
 def on_device(
@@ -909,16 +957,16 @@
     own = ssm_rate.shape[1]
     modes = ssm_rate.shape[2]
     half_hidden = b_in.shape[0]
-    x = to_rows(pixels)
-    cot = to_rows(cotangent)
-    extent_row = extent.reshape(1, own)
+    x = pixels.transpose(0, 3, 1, 2)
+    cot = cotangent.transpose(0, 3, 1, 2)
     rate = ssm_rate.transpose(0, 2, 1)
     freq = ssm_freq.transpose(0, 2, 1)
     coef = ssm_coef.transpose(0, 2, 1)
-    vec = jnp.stack([norm_gain, norm_bias, b_out, layer_scale])
     field = (rows, channels)
     grad_rows = 2 * channels * half_hidden // 128
-    all_rows = 3 * size * chunk_rows(grad_rows, size)
+    groups = half_hidden // CHUNK
+    parts, per = ring_plan(grad_rows // groups, size)
+    all_rows = groups * parts * per * size
     small_rows = max(128, 8 * size)
     bits = max(size.bit_length() - 1, 1)
     peers = max(size - 1, 1)
@@ -926,12 +974,12 @@
     block_out, dx, full, small = pl.pallas_call(
         partial(mega_kernel, size),
         out_shape=(
-            shape(field, BF16),
-            shape(field, BF16),
+            shape(x.shape, BF16),
+            shape(x.shape, BF16),
             shape((all_rows, 128), BF16),
             shape((small_rows, own)),
         ),
-        in_specs=[SM] + [VM] * 11,
+        in_specs=[SM] + [VM] * 14,
         out_specs=(VM,) * 4,
         scratch_shapes=[
             pltpu.VMEM((PACK_ROWS, own), F32),
@@ -960,7 +1008,7 @@
             pltpu.VMEM((162 * 8, channels), F32),
             pltpu.VMEM((81 * 8, channels), F32),
             pltpu.VMEM((112, channels), F32),
-            pltpu.VMEM((3, half_hidden), F32),
+            pltpu.VMEM((4, half_hidden), F32),
             pltpu.VMEM((4, channels), F32),
             pltpu.VMEM((all_rows, 128), F32),
             pltpu.VMEM((grad_rows, 128), BF16),
@@ -971,12 +1019,12 @@
             pltpu.VMEM((128, own), F32),
             pltpu.VMEM((128, own), F32),
             pltpu.VMEM((peers, small_rows // size, own), F32),
-            DMA((5,)),
-            DMA((5,)),
-            DMA((3, bits)),
-            DMA((3, bits)),
-            DMA((3, bits)),
-            DMA((3, bits)),
+            DMA((4 + groups,)),
+            DMA((4 + groups,)),
+            DMA((groups * parts, bits)),
+            DMA((groups * parts, bits)),
+            DMA((groups * parts, bits)),
+            DMA((groups * parts, bits)),
             DMA((peers,)),
             DMA((peers,)),
             DMA((peers,)),
@@ -988,49 +1036,55 @@
         name="block",
     )(
         grid_class,
-        extent_row,
+        extent,
         rate,
         freq,
         coef,
-        skip_gain.reshape(1, own),
-        b_in.reshape(1, half_hidden),
-        vec,
+        skip_gain,
+        b_in,
+        norm_gain,
+        norm_bias,
+        b_out,
+        layer_scale,
         w_in,
         w_out,
         x,
         cot,
     )
-    g_rate, g_freq, g_coef, g_skip, g_vec, dw_in, db_in, dw_out = pl.pallas_call(
+    g_rate, g_freq, g_coef, g_skip, g_gain, g_bias, dw_in, db_in, dw_out, g_b_out, g_scale = pl.pallas_call(
         final_kernel,
         out_shape=(
             shape((2, modes, own)),
             shape((2, modes, own)),
             shape((2, modes, own)),
-            shape((1, own)),
-            shape((4, channels)),
+            shape((own,)),
+            shape((channels,)),
+            shape((channels,)),
             shape(w_in.shape),
-            shape((1, half_hidden)),
+            shape((half_hidden,)),
             shape(w_out.shape),
+            shape((channels,)),
+            shape((channels,)),
         ),
         in_specs=[VM] * 6,
-        out_specs=(VM,) * 8,
+        out_specs=(VM,) * 11,
         compiler_params=pltpu.CompilerParams(vmem_limit_bytes=VMEM_LIMIT),
         name="final",
-    )(extent_row, rate, freq, coef, full, small)
+    )(extent, rate, freq, coef, full, small)
     return (
-        from_rows(block_out, pixels),
-        from_rows(dx, pixels),
+        block_out.transpose(0, 2, 3, 1),
+        dx.transpose(0, 2, 3, 1),
         g_rate.transpose(0, 2, 1),
         g_freq.transpose(0, 2, 1),
         g_coef.transpose(0, 2, 1),
-        g_skip[0],
-        g_vec[0],
-        g_vec[1],
+        g_skip,
+        g_gain,
+        g_bias,
         dw_in,
-        db_in[0],
+        db_in,
         dw_out,
-        g_vec[3],
-        g_vec[2],
+        g_b_out,
+        g_scale,
     )
 
 

time: 109 us -> 82.7 us (0.76)
  local copies, waits for them, and re-layouts: 16.4 us -> 2.5 us
  Pallas kernels: 89.1 us -> 79.3 us
  other arithmetic: 1.88 us -> 0 us
    pallas_call x1, Pallas kernels: 83.4 us -> 73.5 us  [on_device(): pl.pallas_call(partial(mega_kernel, size), out_shape=(shape(x.shape, BF16...]
    reshape x5 -> x0, local copies, waits for them, and re-layouts: 7.02 us -> none  [the longest x2 3.11 us: from_rows(): return rows.reshape(cells, micro, count, channels).transpose(1, 2, 3, 0)]
    transpose x3 -> x0, local copies, waits for them, and re-layouts: 5.22 us -> none  [the longest x1 2.64 us: from_rows(): return rows.reshape(cells, micro, count, channels).transpose(1, 2, 3, 0)]
    another operation x4 -> x0, local copies, waits for them, and re-layouts: 2.73 us -> none  [on_device(): vec = jnp.stack([norm_gain, norm_bias, b_out, layer_scale])]
    unnamed x4 -> x6, local copies, waits for them, and re-layouts: 0.01 us -> 2.5 us
    slice x1 -> x0, local copies, waits for them, and re-layouts: 1.45 us -> none  [on_device(): g_vec[2]]
    pallas_call x1 -> x0, other arithmetic: 1.28 us -> none  [on_device(): pl.pallas_call(final_kernel, out_shape=(shape((2, modes, own)), shape((2,...]
where the time goes in v3:
time: 82.7 us; the launch traced here: 82.4 us
  Pallas kernels  79.3 us (96%)
  local copies, waits for them, and re-layouts  2.5 us (3%)
    pallas_call x1, Pallas kernels, on_device(): pl.pallas_call(partial(mega_kernel, size), out_shape=(shape(x.shape, BF16...  73.5 us
    pallas_call x1, Pallas kernels, on_device(): pl.pallas_call(final_kernel, out_shape=(shape((2, modes, own)), shape((2,...  5.77 us
    unnamed x6, local copies, waits for them, and re-layouts  2.5 us

profile of v3, /device:TPU:0, one launch (start us, length us, event | category | flops | bytes accessed | tf_op | source)
XLA Modules:
  0.0 82.4 jit_solution(7570885465844315330)
XLA Ops:
  0.6 73.5 %block.1 = (bf16[2,324,2,384]{3,2,1,0:T(2,128)(2,1)}, bf16[2,324,2,384]{3,2,1,0:T(2,128)(2,1)}, bf16[4608,128]{1,0:T(8,128)(2,1)}, f32[128,192]{1,0:T(8,128)}) custom-call(s32[2,4]{1,0:T(2,128)} %class_ref.1, s32[192]{0:T(256)} %extent_ref.3, f32[2,64,192]{2,1,0:T(8,128)} %bitcast.14, f32[2,64,192]{2,1,0:T(8,128)} %bitcast.16, f32[2,64,192]{2,1,0:T(8,128)} %bitcast.18, ...), custom_call_target="tpu_custom_call" | custom-call | tf_op jit(solution)/shard_map/block/pallas_call | solution.py:974
  74.2 0.0 copy-start.1
  74.2 5.8 %final.1 = (f32[2,64,192]{2,1,0:T(8,128)}, f32[2,64,192]{2,1,0:T(8,128)}, f32[2,64,192]{2,1,0:T(8,128)}, f32[192]{0:T(256)}, f32[384]{0:T(512)}, /*index=5*/f32[...) custom-call(s32[192]{0:T(256)} %extent_ref.3, ...), custom_call_target="tpu_custom_call" | custom-call | tf_op jit(solution)/shard_map/final/pallas_call | solution.py:1054
  79.9 0.0 copy-start
  79.9 0.0 copy-done.1
  80.0 1.0 %copy.30 = bf16[2,2,384,324]{2,1,3,0:T(2,128)(2,1)} copy(bf16[2,2,384,324]{2,1,3,0:T(2,128)(2,1)S(1)} %bitcast.13) | data formatting | bytes 1990656
  80.9 0.6 copy-done
  81.5 0.9 %copy.31 = bf16[2,2,384,324]{2,1,3,0:T(2,128)(2,1)} copy(bf16[2,2,384,324]{2,1,3,0:T(2,128)(2,1)S(1)} %bitcast.12) | data formatting | bytes 1990656
Async XLA Ops:
  74.2 5.8 %copy-start.1 = (bf16[2,324,2,384]{3,2,1,0:T(2,128)(2,1)S(1)}, bf16[2,324,2,384]{3,2,1,0:T(2,128)(2,1)}, u32[]{:S(2)}) copy-start(bf16[2,324,2,384]{3,2,1,0:T(2,128)(2,1)} %get-tuple-element.28) | copy-start | bytes 2985988
  79.9 1.6 %copy-start = (bf16[2,324,2,384]{3,2,1,0:T(2,128)(2,1)S(1)}, bf16[2,324,2,384]{3,2,1,0:T(2,128)(2,1)}, u32[]{:S(2)}) copy-start(bf16[2,324,2,384]{3,2,1,0:T(2,128)(2,1)} %get-tuple-element.29) | copy-start | bytes 2985988

commit v4 on v3

--- a/solution.py
+++ b/solution.py
@@ -48,8 +48,10 @@
     return decay * cos, decay * sin
 
 
-PACK_ROWS = 120
-SMALL_ROWS = 121
+PACK_ROWS = 112
+SUM_ROWS = 128
+WIDE = 512
+
 
 def write_tables(extent_ref, rate_ref, freq_ref, coef_ref, out_ref):
     extent = extent_ref[...].reshape(1, extent_ref.shape[0])
@@ -69,9 +71,9 @@
                     w_re, w_im = w_re * z_re - w_im * z_im, w_re * z_im + w_im * z_re
 
 
-def modes_grad(extent_ref, rate_ref, freq_ref, coef_ref, dk_ref, rate_out, freq_out, coef_out):
+def modes_grad(axis, extent_ref, rate_ref, freq_ref, coef_ref, dk_ref, rate_out, freq_out, coef_out):
     extent = extent_ref[...].reshape(1, extent_ref.shape[0])
-    for axis in range(2):
+    if True:
         coef = coef_ref[axis]
         g_rate = jnp.zeros_like(coef)
         g_freq = jnp.zeros_like(coef)
@@ -361,140 +363,142 @@
     lax.fori_loop(0, tiles, body, 0)
 
 
-def bit_orders(size, parts):
+def stages_of(size):
     bits = size.bit_length() - 1
-    turn = min(3, max(bits, 1))
-    base = list(range(bits))
-    return [
-        [base[(k + part) % turn] if k < turn else base[k] for k in range(bits)]
-        for part in range(parts)
-    ]
-
-
-def ring_plan(rows, size):
-    parts = 3 if rows % (48 * size) == 0 else 1
-    per = -(-rows // (parts * size))
-    return parts, -(-per // 16) * 16
+    stages, stride = [], 1
+    while bits:
+        take = bits if bits <= 3 and bits != 2 else 2
+        stages.append((stride, 1 << take))
+        stride <<= take
+        bits -= take
+    return stages
+
+
+def chunk_rows(rows, size):
+    return -(-rows // (16 * size)) * 16
 
 
 class Ring:
-    def __init__(self, group, size, plan, acc, send, recv, full, sems):
-        self.group, self.size = group, size
-        self.parts, self.rows = plan
+    def __init__(self, group, size, rows, acc, send, recv, full, sems):
+        self.group, self.size, self.rows = group, size, rows
         self.acc, self.send, self.recv, self.full = acc, send, recv, full
         self.send_sem, self.recv_sem, self.back_send, self.back_recv = sems
-        self.orders = bit_orders(size, self.parts)
-        self.bits = size.bit_length() - 1
+        self.stages = stages_of(size)
         self.me = lax.axis_index("dp")
-        self.place = []
-        for order in self.orders:
-            place = 0
-            for bit in order:
-                place = place * 2 + lax.rem(self.me // (1 << bit), 2)
-            self.place.append(place)
-
-    def base(self, part):
-        return (self.group * self.parts + part) * self.size * self.rows
-
-    def peer(self, bit):
-        mine = lax.rem(self.me // (1 << bit), 2)
-        return self.me + (1 - 2 * mine) * (1 << bit)
-
-    def span(self, part, step):
-        half = self.size >> (step + 1)
-        index = self.place[part] // half
-        mine = lax.rem(index, 2)
-        keep = self.base(part) + index * half * self.rows
-        away = self.base(part) + (index + 1 - 2 * mine) * half * self.rows
-        return pl.multiple_of(keep, 16), pl.multiple_of(away, 16), half * self.rows
-
-    def slot(self, part, step):
-        done = self.size - (self.size >> step)
-        return self.base(part) + done * self.rows
-
-    def sem(self, sems, part, step):
-        return sems.at[self.group * self.parts + part, step]
-
-    def reduce_copy(self, part, step):
-        _, away, length = self.span(part, step)
+        self.base = group * size * rows
+        self.digit, self.start, self.length = [], [], []
+        start, length = 0, size
+        for stride, members in self.stages:
+            digit = lax.rem(self.me // stride, members)
+            self.digit.append(digit)
+            self.start.append(start)
+            self.length.append(length)
+            length //= members
+            start = start + digit * length
+        self.mine = start
+
+    def at(self, chunk, count):
+        return pl.ds(pl.multiple_of(self.base + chunk * self.rows, 16), count * self.rows)
+
+    def hop(self, stage, offset):
+        stride, members = self.stages[stage]
+        digit = self.digit[stage]
+        other = lax.rem(digit + offset, members)
+        length = self.length[stage] // members
+        start = self.start[stage]
+        return self.me + (other - digit) * stride, start + other * length, start + digit * length, length
+
+    def slot(self, stage, offset):
+        length = self.length[stage] // self.stages[stage][1]
+        return self.at(self.size - self.length[stage] + (offset - 1) * length, length)
+
+    def sem(self, sems, stage, offset):
+        return sems.at[self.group, stage, offset - 1]
+
+    def reduce_copy(self, stage, offset):
+        peer, theirs, _, length = self.hop(stage, offset)
         return pltpu.make_async_remote_copy(
-            src_ref=self.send.at[pl.ds(away, length), :],
-            dst_ref=self.recv.at[pl.ds(self.slot(part, step), length), :],
-            send_sem=self.sem(self.send_sem, part, step),
-            recv_sem=self.sem(self.recv_sem, part, step),
-            device_id={"dp": self.peer(self.orders[part][step])},
+            src_ref=self.send.at[self.at(theirs, length), :],
+            dst_ref=self.recv.at[self.slot(stage, offset), :],
+            send_sem=self.sem(self.send_sem, stage, offset),
+            recv_sem=self.sem(self.recv_sem, stage, offset),
+            device_id={"dp": peer},
             device_id_type=pl.DeviceIdType.MESH,
         )
 
-    def gather_copy(self, part, step):
-        keep, _, length = self.span(part, step)
+    def gather_copy(self, stage, offset):
+        peer, _, ours, length = self.hop(stage, offset)
         return pltpu.make_async_remote_copy(
-            src_ref=self.full.at[pl.ds(keep, length), :],
-            dst_ref=self.full.at[pl.ds(keep, length), :],
-            send_sem=self.sem(self.back_send, part, step),
-            recv_sem=self.sem(self.back_recv, part, step),
-            device_id={"dp": self.peer(self.orders[part][step])},
+            src_ref=self.full.at[self.at(ours, length), :],
+            dst_ref=self.full.at[self.at(ours, length), :],
+            send_sem=self.sem(self.back_send, stage, offset),
+            recv_sem=self.sem(self.back_recv, stage, offset),
+            device_id={"dp": peer},
             device_id_type=pl.DeviceIdType.MESH,
         )
 
-    def reduce_start(self, step):
-        for part in range(self.parts):
-            _, away, length = self.span(part, step)
-            copy_rows(self.acc, away, self.send, away, length, lambda v: v.astype(BF16))
-            self.reduce_copy(part, step).start()
-
-    def reduce_finish(self, step):
-        for part in range(self.parts):
-            self.reduce_copy(part, step).wait_recv()
-            keep, _, length = self.span(part, step)
-            add_rows(self.recv, self.slot(part, step), self.acc, keep, length)
-
-    def gather_first(self):
-        for part in range(self.parts):
-            own = pl.multiple_of(self.base(part) + self.place[part] * self.rows, 16)
+    def offsets(self, stage):
+        return range(1, self.stages[stage][1])
+
+    def reduce_start(self, stage):
+        for offset in self.offsets(stage):
+            _, theirs, _, length = self.hop(stage, offset)
+            first = pl.multiple_of(self.base + theirs * self.rows, 16)
+            copy_rows(self.acc, first, self.send, first, length * self.rows, lambda v: v.astype(BF16))
+            self.reduce_copy(stage, offset).start()
+
+    def reduce_finish(self, stage):
+        for offset in self.offsets(stage):
+            self.reduce_copy(stage, offset).wait_recv()
+        _, _, ours, length = self.hop(stage, 0)
+        shift = length * self.rows
+        slot = self.base + (self.size - self.length[stage]) * self.rows
+        add_rows(self.recv, slot, shift, self.stages[stage][1] - 1, self.acc,
+                 pl.multiple_of(self.base + ours * self.rows, 16), shift)
+
+    def gather_start(self, stage):
+        for offset in self.offsets(stage):
+            self.gather_copy(stage, offset).start()
+
+    def gather_finish(self, stage):
+        for offset in self.offsets(stage):
+            self.gather_copy(stage, offset).wait_recv()
+
+    def advance(self, step):
+        count = len(self.stages)
+        if 0 < step <= count:
+            self.reduce_finish(step - 1)
+        if step > count:
+            self.gather_finish(2 * count - step)
+        if step < count:
+            self.reduce_start(step)
+        if step == count:
+            own = pl.multiple_of(self.base + self.mine * self.rows, 16)
             copy_rows(self.acc, own, self.full, own, self.rows, lambda v: v.astype(BF16))
-
-    def gather_start(self, step):
-        for part in range(self.parts):
-            self.gather_copy(part, step).start()
-
-    def gather_finish(self, step):
-        for part in range(self.parts):
-            self.gather_copy(part, step).wait_recv()
-
-    def advance(self, step):
-        bits = self.bits
-        if step > 2 * bits:
-            return
-        if 0 < step <= bits:
-            self.reduce_finish(step - 1)
-        if step > bits:
-            self.gather_finish(2 * bits - step)
-        if step < bits:
-            self.reduce_start(step)
-        if step == bits:
-            self.gather_first()
-        if bits <= step < 2 * bits:
-            self.gather_start(2 * bits - 1 - step)
+        if count <= step < 2 * count:
+            self.gather_start(2 * count - 1 - step)
 
     def close(self):
-        for part in range(self.parts):
-            for step in range(self.bits):
-                self.reduce_copy(part, step).wait_send()
-                self.gather_copy(part, step).wait_send()
+        for stage in range(len(self.stages)):
+            for offset in self.offsets(stage):
+                self.reduce_copy(stage, offset).wait_send()
+                self.gather_copy(stage, offset).wait_send()
 
 
 def row_block(length):
     return next(block for block in (128, 96, 64, 48, 32, 16) if length % block == 0)
 
 
-def add_rows(source, first, target, where, length):
+def add_rows(source, first, shift, count, target, where, length):
     block = row_block(length)
 
     def body(t, carry):
-        here = pl.ds(pl.multiple_of(first + t * block, 16), block)
         there = pl.ds(pl.multiple_of(where + t * block, 16), block)
-        target[there, :] += source[here, :].astype(F32)
+        total = target[there, :]
+        for n in range(count):
+            here = pl.ds(pl.multiple_of(first + n * shift + t * block, 16), block)
+            total = total + source[here, :].astype(F32)
+        target[there, :] = total
         return carry
 
     lax.fori_loop(0, length // block, body, 0)
@@ -512,10 +516,6 @@
     lax.fori_loop(0, length // block, body, 0)
 
 
-def wide(ref, first, count):
-    return jnp.concatenate([ref[first + k : first + k + 1, :] for k in range(count)], axis=1)
-
-
 def images_in(ref, first, count):
     parts = [ref[micro, pl.ds(first, count), :, :].astype(F32) for micro in range(2)]
     return jnp.concatenate(parts, axis=1).reshape(4 * count, ref.shape[3])
@@ -525,6 +525,30 @@
     value = value.reshape(count, 4, ref.shape[3])
     for micro in range(2):
         ref[micro, pl.ds(first, count)] = value[:, 2 * micro : 2 * micro + 2, :].astype(BF16)
+
+
+def gelu_and_slope(pre):
+    size = 1.0 + ERF_SHIFT * jnp.abs(pre)
+    inv = pltpu.reciprocal(size, approx=True)
+    inv = inv * (2.0 - size * inv)
+    poly = (0.5 * ERF_POLY[-1]) * inv + 0.5 * ERF_POLY[-2]
+    for value in reversed(ERF_POLY[:-2]):
+        poly = poly * inv + 0.5 * value
+    bell = jnp.exp2(pre * pre * (-0.5 * math.log2(math.e)))
+    tail = poly * inv * bell
+    cdf = jnp.where(pre >= 0.0, 1.0 - tail, tail)
+    return (pre * cdf).astype(BF16), cdf + pre * bell * (1.0 / math.sqrt(2.0 * math.pi))
+
+
+STEPS = (
+    ((), (), (), ()),
+    ((), (), (), (0,)),
+    ((), (), (), ()),
+    ((), (), (), (0, 1)),
+    ((), (), (), ()),
+    ((), (0,), (), (1, 2)),
+)
+LATER = ((), (), (0, 1), (), (2,), (), (1,), (2, 0), (1, 2))
 
 
 def mega_kernel(
@@ -540,14 +564,19 @@
     shift_ref,
     b_out_ref,
     scale_ref,
+    w_in_hbm,
+    w_out_hbm,
+    x_hbm,
+    cot_hbm,
+    block_out,
+    dx_out,
+    dw_in_out,
+    dw_out_out,
+    small_out,
+    x_ref,
+    cot_ref,
     w_in_ref,
     w_out_ref,
-    x_ref,
-    cot_ref,
-    block_out,
-    dx_out,
-    full_out,
-    small_out,
     pack_own,
     pack_oth,
     w_in_oth,
@@ -573,7 +602,6 @@
     gm_ref,
     row_acc,
     col_acc,
-    dk_ref,
     db_ref,
     sums_ref,
     acc_ref,
@@ -581,8 +609,12 @@
     landed_ref,
     send_ref,
     recv_ref,
+    full_ref,
+    dw_in_ref,
+    dw_out_ref,
+    block_ref,
+    dx_ref,
     small_keep,
-    small_send,
     small_land,
     small_recv,
     pair_send,
@@ -595,6 +627,8 @@
     sc_recv,
     bc_send,
     bc_recv,
+    out_sem,
+    in_sem,
 ):
     cells, channels = x_ref.shape[1], x_ref.shape[3]
     rows = 4 * cells
@@ -613,6 +647,19 @@
             device_id={"dp": lax.rem(me + offset, size)},
             device_id_type=pl.DeviceIdType.MESH,
         )
+    reads = [
+        pltpu.make_async_copy(source, target, in_sem.at[index])
+        for index, (source, target) in enumerate(
+            (
+                (w_in_hbm, w_in_ref.at[pl.ds(0, channels), :]),
+                (w_out_hbm, w_out_ref),
+                (x_hbm, x_ref),
+                (cot_hbm, cot_ref),
+            )
+        )
+    ]
+    for copy in reads:
+        copy.start()
 
     def pair_copy(index, source, target):
         return pltpu.make_async_remote_copy(
@@ -626,21 +673,40 @@
 
     write_tables(extent_ref, rate_ref, freq_ref, coef_ref, pack_own)
     pack_own[108:109, :] = skip_ref[...].reshape(1, own)
+    pack_own[109:PACK_ROWS, :] = jnp.zeros((PACK_ROWS - 109, own), F32)
     b_in = b_in_ref[...].reshape(1, half_hidden)
-    for k in range(4):
-        pack_own[109 + k : 110 + k, :] = b_in[:, k * own : (k + 1) * own]
-    pack_own[113:PACK_ROWS, :] = jnp.zeros((PACK_ROWS - 113, own), F32)
+    b_high = b_in.astype(BF16).astype(F32)
+    b_mid = (b_in - b_high).astype(BF16).astype(F32)
+    b_low = b_in - b_high - b_mid
+    line = lax.broadcasted_iota(jnp.int32, (16, half_hidden), 0)
+    w_in_ref[channels : channels + 16, :] = jnp.where(
+        line == 0, b_high, jnp.where(line == 1, b_mid, jnp.where(line == 2, b_low, 0.0))
+    ).astype(BF16)
+    rest = WIDE - channels - 16
+    w_in_ref[channels + 16 : WIDE, :] = jnp.zeros((rest, half_hidden), BF16)
+    w_in_oth[channels + 16 : WIDE, :] = jnp.zeros((rest, half_hidden), BF16)
     pl.semaphore_wait(barrier, size)
     pack_copy = pair_copy(0, pack_own, pack_oth)
-    first_copy = pair_copy(1, w_in_ref, w_in_oth)
+    first_copy = pair_copy(
+        1, w_in_ref.at[pl.ds(0, channels + 16), :], w_in_oth.at[pl.ds(0, channels + 16), :]
+    )
     second_copy = pair_copy(2, w_out_ref, w_out_oth)
     pack_copy.start()
+    reads[0].wait()
     first_copy.start()
+    reads[1].wait()
     second_copy.start()
 
     build_masks(class_ref, mask_ref)
     block = 144
     scale = scale_ref[...].reshape(1, channels)
+    normed_ref[:, channels:] = jnp.where(
+        lax.broadcasted_iota(jnp.int32, (rows, WIDE - channels), 1) < 3, 1.0, 0.0
+    ).astype(BF16)
+    mlp_ref[...] = jnp.broadcast_to(b_out_ref[...].reshape(1, channels), mlp_ref.shape)
+    gn_ref[...] = jnp.zeros_like(gn_ref)
+    reads[2].wait()
+    reads[3].wait()
 
     def load(t, carry):
         at = pl.ds(pl.multiple_of(t * 48, 16), 48)
@@ -676,119 +742,127 @@
         hat = centered * rstd
         mixed_ref[at, :] = hat
         stat_ref[at, :] = jnp.broadcast_to(rstd, (block, 128))
-        normed_ref[at, :] = (hat * gain + shift).astype(BF16)
+        normed_ref[at, :channels] = (hat * gain + shift).astype(BF16)
         return carry
 
     lax.fori_loop(0, rows // block, norm, 0)
 
     chunk = CHUNK
     tile_rows = 432
-    mlp_ref[...] = jnp.broadcast_to(b_out_ref[...].reshape(1, channels), mlp_ref.shape)
-    gn_ref[...] = jnp.zeros_like(gn_ref)
     first_copy.wait_recv()
     second_copy.wait_recv()
 
     group_rows = 2 * channels * chunk // 128
-    plan = ring_plan(group_rows, size)
-    stride = plan[0] * plan[1] * size
+    per_chunk = chunk_rows(group_rows, size)
+    stride = per_chunk * size
     groups = half_hidden // chunk
     rings = [
-        Ring(group, size, plan, acc_ref, send_ref, recv_ref, full_out,
+        Ring(group, size, per_chunk, acc_ref, send_ref, recv_ref, full_ref,
              (red_send, red_recv, gat_send, gat_recv))
         for group in range(groups)
     ]
-    db_ref[2:3, :] = wide(pack_oth, 109, 4)
-    db_ref[3:4, :] = b_in
-
-    def feed(f, w_first_ref, w_second_ref, bias_row, target_ref, target_base, db_row):
-        cols = pl.ds(pl.multiple_of(f * chunk, chunk), chunk)
-        w_first = w_first_ref[:, cols]
-        w_second = w_second_ref[cols, :]
-        bias = db_ref[bias_row : bias_row + 1, cols]
-        db = jnp.zeros((1, chunk), F32)
-        for t in range(rows // tile_rows):
+    done = [0] * groups
+
+    def advance(*which):
+        last = 2 * len(stages_of(size))
+        for group in which:
+            if done[group] > last:
+                continue
+            rings[group].advance(done[group])
+            if done[group] == last:
+                unpack(group)
+            done[group] += 1
+
+    def unpack(group):
+        base = group * stride
+        for k in range(chunk // 128):
+            at = group * chunk + k * 128
+            dw_in_ref[:, at : at + 128] = full_ref[base : base + channels, :].astype(F32)
+            base += channels
+        for k in range(channels // 128):
+            dw_out_ref[group * chunk : (group + 1) * chunk, k * 128 : (k + 1) * 128] = full_ref[
+                base : base + chunk, :
+            ].astype(F32)
+            base += chunk
+        at = pl.ds(group * chunk, chunk)
+        first = pltpu.make_async_copy(dw_in_ref.at[:, at], dw_in_out.at[:, at], out_sem.at[2 * group])
+        second = pltpu.make_async_copy(dw_out_ref.at[at, :], dw_out_out.at[at, :], out_sem.at[2 * group + 1])
+        first.start()
+        second.start()
+        writes.extend((first, second))
+
+    writes = []
+    tiles = rows // tile_rows
+
+    def feed(f, w_first_ref, w_second_ref, target_ref, target_base, db_row, steps):
+        cols = pl.ds(f * chunk, chunk)
+
+        def ahead(t):
             at = pl.ds(t * tile_rows, tile_rows)
-            pre = jnp.dot(normed_ref[at, :], w_first, preferred_element_type=F32) + bias
-            inv = 1.0 / (1.0 + ERF_SHIFT * jnp.abs(pre))
-            poly = jnp.full_like(inv, 0.5 * ERF_POLY[-1])
-            for value in reversed(ERF_POLY[:-1]):
-                poly = poly * inv + 0.5 * value
-            bell = jnp.exp(-0.5 * pre * pre)
-            tail = poly * inv * bell
-            cdf = jnp.where(pre >= 0.0, 1.0 - tail, tail)
-            act = (pre * cdf).astype(BF16)
-            slope = cdf + pre * bell * (1.0 / math.sqrt(2.0 * math.pi))
+            pre = jnp.dot(normed_ref[at, :], w_first_ref[:, cols], preferred_element_type=F32)
             g_act = lax.dot_general(
-                gmlp_ref[at, :], w_second, (((1,), (1,)), ((), ())), preferred_element_type=F32
+                gmlp_ref[at, :],
+                w_second_ref[cols, :],
+                (((1,), (1,)), ((), ())),
+                preferred_element_type=F32,
             )
+            return pre, g_act
+
+        waiting = ahead(0)
+        for t in range(tiles):
+            pre, g_act = waiting
+            if t + 1 < tiles:
+                waiting = ahead(t + 1)
+            at = pl.ds(t * tile_rows, tile_rows)
+            act, slope = gelu_and_slope(pre)
             g_pre = (g_act * slope).astype(BF16)
-            db = db + jnp.sum(g_pre.astype(F32), axis=0, keepdims=True)
             act_ref[at, :] = act
             gpre_ref[at, :] = g_pre
-            mlp_ref[at, :] += jnp.dot(act, w_second, preferred_element_type=F32)
+            mlp_ref[at, :] += jnp.dot(act, w_second_ref[cols, :], preferred_element_type=F32)
             gn_ref[at, :] += lax.dot_general(
-                g_pre, w_first, (((1,), (1,)), ((), ())), preferred_element_type=F32
+                g_pre,
+                w_first_ref[:channels, cols],
+                (((1,), (1,)), ((), ())),
+                preferred_element_type=F32,
             )
-        db_ref[db_row : db_row + 1, cols] = db
+            advance(*steps[t])
         d_first = lax.dot_general(
             normed_ref[...], gpre_ref[...], (((0,), (0,)), ((), ())), preferred_element_type=F32
         )
         for k in range(chunk // 128):
-            at = pl.ds(pl.multiple_of(target_base + k * channels, 128), channels)
-            target_ref[at, :] = d_first[:, k * 128 : (k + 1) * 128].astype(target_ref.dtype)
+            at = pl.ds(target_base + k * channels, channels)
+            target_ref[at, :] = d_first[:channels, k * 128 : (k + 1) * 128].astype(target_ref.dtype)
+        db_ref[db_row : db_row + 1, cols] = d_first[channels : channels + 1, :]
         d_second = lax.dot_general(
             act_ref[...], gmlp_ref[...], (((0,), (0,)), ((), ())), preferred_element_type=F32
         )
         base = target_base + channels * (chunk // 128)
         for k in range(channels // 128):
-            at = pl.ds(pl.multiple_of(base + k * chunk, 128), chunk)
+            at = pl.ds(base + k * chunk, chunk)
             target_ref[at, :] = d_second[:, k * 128 : (k + 1) * 128].astype(target_ref.dtype)
 
     def grads_copy(group):
-        at = pl.ds(pl.multiple_of(group * group_rows, 16), group_rows)
+        at = pl.ds(group * group_rows, group_rows)
         return pair_copy(4 + group, away_ref.at[at, :], landed_ref.at[at, :])
 
-    def join(group):
+    for group in range(groups):
+        feed(group, w_in_oth, w_out_oth, away_ref, group * group_rows, 1, STEPS[2 * group])
+        grads_copy(group).start()
+        advance(*STEPS[2 * group][3])
+        feed(group, w_in_ref, w_out_ref, acc_ref, group * stride, 0, STEPS[2 * group + 1])
         grads_copy(group).wait_recv()
-        add_rows(landed_ref, pl.multiple_of(group * group_rows, 16), acc_ref,
-                 pl.multiple_of(group * stride, 16), group_rows)
+        add_rows(landed_ref, group * group_rows, 0, 1, acc_ref, group * stride, group_rows)
         if stride > group_rows:
-            acc_ref[pl.ds(pl.multiple_of(group * stride + group_rows, 16), stride - group_rows), :] = (
-                jnp.zeros((stride - group_rows, 128), F32)
+            acc_ref[group * stride + group_rows : (group + 1) * stride, :] = jnp.zeros(
+                (stride - group_rows, 128), F32
             )
-
-    def tick(count):
-        for group in reversed(range(groups)):
-            step = count - 2 * group
-            if 0 <= step <= 2 * rings[group].bits:
-                rings[group].advance(step)
-
-    def pair_of_chunks(f, carry):
-        feed(f, w_in_oth, w_out_oth, 2, away_ref, f * group_rows, 1)
-        grads_copy(f).start()
-        for count in range(1, groups):
-            pl.when(f == count)(partial(tick, 2 * count - 1))
-        feed(f, w_in_ref, w_out_ref, 3, acc_ref, f * stride, 0)
-        join(f)
-        for count in range(groups):
-            pl.when(f == count)(partial(tick, 2 * count))
-        return carry
-
-    lax.fori_loop(0, groups, pair_of_chunks, 0)
-    last = 2 * rings[0].bits + 2 * (groups - 1)
-    ticks = iter(range(2 * groups - 1, last + 1))
-
-    def advance():
-        count = next(ticks, None)
-        if count is not None:
-            tick(count)
+        advance(*STEPS[2 * group + 1][3])
 
     def back(t, carry):
         d_gain, d_bias, d_scale, d_b_out = carry
         at = pl.ds(pl.multiple_of(t * 48, 16), 48)
         mask = jnp.tile(mask_ref[at, :], (1, channels // 128))
         branch = mlp_ref[at, :] * mask
-        images_out(block_out, t * 12, 12, u_ref[at, :] + scale * branch)
         d_scale = d_scale + jnp.sum(images_in(cot_ref, t * 12, 12) * branch, axis=0, keepdims=True)
         d_b_out = d_b_out + jnp.sum(gmlp_ref[at, :].astype(F32), axis=0, keepdims=True)
         grad = gn_ref[at, :]
@@ -804,45 +878,46 @@
 
     zero = jnp.zeros((1, channels), F32)
     sums = lax.fori_loop(0, rows // 48, back, (zero, zero, zero, zero))
+    mine_only = pl.ds(pl.multiple_of(core * 256, 128), 128)
+    theirs_only = pl.ds(pl.multiple_of((1 - core) * 256, 128), 128)
     for index, value in enumerate(sums):
-        sums_ref[index : index + 1, :] = value
-
-    gh_ref, xh_ref = mh_ref, mlp_ref
-    advance()
+        for k in range(channels // 128):
+            row = 115 + index * (channels // 128) + k
+            tile = value[:, k * 128 : (k + 1) * 128]
+            sums_ref[row : row + 1, mine_only] = tile
+            sums_ref[row : row + 1, theirs_only] = tile
+    for k in range(half_hidden // 128):
+        at = slice(k * 128, (k + 1) * 128)
+        sums_ref[109 + k : 110 + k, mine_only] = db_ref[0:1, at]
+        sums_ref[109 + k : 110 + k, theirs_only] = db_ref[1:2, at]
+    sums_ref[109:127, 128:256] = jnp.zeros((18, 128), F32)
+    sums_ref[127:128, :] = zero
+    advance(*LATER[0])
+    gh_ref, xh_ref = mh_ref, row_acc
     mirror_in(gm_ref, mask_ref, gh_ref)
+    col_correlate(gh_ref, v_ref, col_acc)
+    advance(*LATER[1])
     apply_cols(colop_ref, gh_ref, xh_ref)
-    advance()
-    row_correlate(xh_ref, uh_ref, row_acc)
-    advance()
-    col_correlate(gh_ref, v_ref, col_acc)
-    advance()
-    gather_lags(class_ref, row_acc, col_acc, dk_ref)
+    advance(*LATER[2])
+    row_correlate(xh_ref, uh_ref, v_ref)
+    advance(*LATER[3])
+    gather_lags(class_ref, v_ref, col_acc, sums_ref)
 
     def skip_sum(t, total):
         at = pl.ds(pl.multiple_of(t * block, block), block)
         return total + jnp.sum(gm_ref[at, :] * u_ref[at, :], axis=0, keepdims=True)
 
-    dk_ref[108:109, :] = lax.fori_loop(0, rows // block, skip_sum, zero)
-    dk_ref[109:112, :] = jnp.zeros((3, channels), F32)
-    low = dk_ref[:, :own]
-    high = dk_ref[:, own:]
-    small_keep[...] = jnp.zeros_like(small_keep)
-    small_keep[0:112, :] = jnp.where(first, low, high)
-    small_send[0:112, :] = jnp.where(first, high, low)
-    for k in range(4):
-        small_keep[109 + k : 110 + k, :] = db_ref[0:1, k * own : (k + 1) * own]
-        small_send[109 + k : 110 + k, :] = db_ref[1:2, k * own : (k + 1) * own]
-    for k in range(8):
-        value = sums_ref[k // 2 : k // 2 + 1, (k % 2) * own : (k % 2 + 1) * own]
-        small_keep[113 + k : 114 + k, :] = value
-        small_send[113 + k : 114 + k, :] = value
-    small_send[SMALL_ROWS:128, :] = jnp.zeros((128 - SMALL_ROWS, own), F32)
-    small_pair = pair_copy(3, small_send, small_land)
+    sums_ref[108:109, :] = lax.fori_loop(0, rows // block, skip_sum, zero)
+    mine_slice = pl.ds(pl.multiple_of(core * 128, 128), 256)
+    theirs_slice = pl.ds(pl.multiple_of((1 - core) * 128, 128), 256)
+    small_pair = pair_copy(3, sums_ref.at[:, theirs_slice], small_land)
     small_pair.start()
     apply_rows(rowop_ref, xh_ref, gh_ref)
-    advance()
+    advance(*LATER[4])
     small_pair.wait_recv()
-    small_keep[0:128, :] += small_land[...]
+    small_keep[0:SUM_ROWS, :] = sums_ref[:, mine_slice] + small_land[...]
+    if small_keep.shape[0] > SUM_ROWS:
+        small_keep[SUM_ROWS:, :] = jnp.zeros((small_keep.shape[0] - SUM_ROWS, 256), F32)
 
     per = small_keep.shape[0] // size
     mine = pl.ds(pl.multiple_of(me * per, 8), per)
@@ -872,7 +947,21 @@
     for offset in range(1, size):
         scatter_copy(offset).start()
     mirror_out(gh_ref, mask_ref, gn_ref, gm_ref, skip_all)
-    advance()
+    advance(*LATER[5])
+
+    def finish(t, carry):
+        at = pl.ds(pl.multiple_of(t * 48, 16), 48)
+        images_out(dx_ref, t * 12, 12, images_in(cot_ref, t * 12, 12) + gn_ref[at, :])
+        branch = mlp_ref[at, :] * jnp.tile(mask_ref[at, :], (1, channels // 128))
+        images_out(block_ref, t * 12, 12, u_ref[at, :] + scale * branch)
+        return carry
+
+    lax.fori_loop(0, rows // 48, finish, 0)
+    for index, (source, target) in enumerate(((dx_ref, dx_out), (block_ref, block_out))):
+        copy = pltpu.make_async_copy(source, target, out_sem.at[2 * groups + index])
+        copy.start()
+        writes.append(copy)
+    advance(*LATER[6])
     total = small_keep[mine, :]
     for offset in range(1, size):
         scatter_copy(offset).wait_recv()
@@ -881,14 +970,9 @@
     for offset in range(1, size):
         spread_copy(offset).start()
 
-    def finish(t, carry):
-        at = pl.ds(pl.multiple_of(t * 48, 16), 48)
-        images_out(dx_out, t * 12, 12, images_in(cot_ref, t * 12, 12) + gn_ref[at, :])
-        return carry
-
-    lax.fori_loop(0, rows // 48, finish, 0)
-    for _ in range(last + 1):
-        advance()
+    advance(*LATER[7])
+    for _ in range(2 * len(stages_of(size)) + 1):
+        advance(*range(groups))
     for offset in range(1, size):
         spread_copy(offset).wait_recv()
     for offset in range(1, size):
@@ -899,33 +983,46 @@
         grads_copy(group).wait_send()
     for copy in (pack_copy, first_copy, second_copy, small_pair):
         copy.wait_send()
+    for copy in writes:
+        copy.wait()
 
 
 def final_kernel(
-    extent_ref, rate_ref, freq_ref, coef_ref, full_ref, small_ref, rate_out, freq_out, coef_out,
-    skip_out, gain_out, bias_out, dw_in_out, db_in_out, dw_out_out, b_out_out, scale_out,
+    extent_ref, rate_ref, freq_ref, coef_ref, small_ref, block_ref, dx_ref, dw_in_ref, dw_out_ref,
+    block_out, dx_out, rate_out, freq_out, coef_out, skip_out, gain_out, bias_out, dw_in_out,
+    db_in_out, dw_out_out, b_out_out, scale_out,
+    mine_ref, block_hold, dx_hold, dw_in_hold, dw_out_hold, sems,
 ):
-    channels, half_hidden = dw_in_out.shape
-    groups = half_hidden // CHUNK
-    stride = full_ref.shape[0] // groups
-    for group in range(groups):
-        base = group * stride
-        for k in range(CHUNK // 128):
-            at = group * CHUNK + k * 128
-            dw_in_out[:, at : at + 128] = full_ref[base : base + channels, :].astype(F32)
-            base += channels
-        for k in range(channels // 128):
-            dw_out_out[group * CHUNK : (group + 1) * CHUNK, k * 128 : (k + 1) * 128] = full_ref[
-                base : base + CHUNK, :
-            ].astype(F32)
-            base += CHUNK
-    modes_grad(extent_ref, rate_ref, freq_ref, coef_ref, small_ref, rate_out, freq_out, coef_out)
-    skip_out[...] = small_ref[108:109, :].reshape(skip_out.shape)
-    db_in_out[...] = wide(small_ref, 109, 4).reshape(db_in_out.shape)
+    held = (block_ref, dx_ref, dw_in_ref, dw_out_ref)
+    stage = (block_hold, dx_hold, dw_in_hold, dw_out_hold)
+    outs = (block_out, dx_out, dw_in_out, dw_out_out)
+    into = [pltpu.make_async_copy(held[k], stage[k], sems.at[k]) for k in range(4)]
+    away = [pltpu.make_async_copy(stage[k], outs[k], sems.at[4 + k]) for k in range(4)]
+    for copy in into:
+        copy.start()
+    core = lax.axis_index("mp")
+    own = mine_ref.shape[1]
+    mine_ref[...] = jnp.where(core == 0, small_ref[0:112, :own], small_ref[0:112, 256 - own :])
+    only = pl.ds(pl.multiple_of(core * 128, 128), 128)
+
+    def line(first, count):
+        return jnp.concatenate([small_ref[first + k : first + k + 1, only] for k in range(count)], axis=1)
+
+    args = (extent_ref, rate_ref, freq_ref, coef_ref, mine_ref, rate_out, freq_out, coef_out)
+    modes_grad(0, *args)
+    for k in range(4):
+        into[k].wait()
+        away[k].start()
+    modes_grad(1, *args)
+    skip_out[...] = mine_ref[108:109, :].reshape(skip_out.shape)
+    db_in_out[...] = line(109, db_in_out.shape[0] // 128).reshape(db_in_out.shape)
     for k, ref in enumerate((gain_out, bias_out, scale_out, b_out_out)):
-        ref[...] = wide(small_ref, 113 + 2 * k, 2).reshape(ref.shape)
-
-
+        ref[...] = line(115 + 3 * k, 3).reshape(ref.shape)
+    for copy in away:
+        copy.wait()
+
+
+ANY = pl.BlockSpec(memory_space=pl.ANY)
 VM = pl.BlockSpec(memory_space=pltpu.VMEM)
 SM = pl.BlockSpec(memory_space=pltpu.SMEM)
 
@@ -965,26 +1062,31 @@
     field = (rows, channels)
     grad_rows = 2 * channels * half_hidden // 128
     groups = half_hidden // CHUNK
-    parts, per = ring_plan(grad_rows // groups, size)
-    all_rows = groups * parts * per * size
+    all_rows = groups * chunk_rows(grad_rows // groups, size) * size
+    stages = stages_of(size)
+    hops = (groups, max(len(stages), 1), max([members - 1 for _, members in stages] + [1]))
     small_rows = max(128, 8 * size)
-    bits = max(size.bit_length() - 1, 1)
     peers = max(size - 1, 1)
     DMA = pltpu.SemaphoreType.DMA
-    block_out, dx, full, small = pl.pallas_call(
+    block_out, dx, dw_in, dw_out, small = pl.pallas_call(
         partial(mega_kernel, size),
         out_shape=(
             shape(x.shape, BF16),
             shape(x.shape, BF16),
-            shape((all_rows, 128), BF16),
-            shape((small_rows, own)),
+            shape(w_in.shape),
+            shape(w_out.shape),
+            shape((small_rows, 256)),
         ),
-        in_specs=[SM] + [VM] * 14,
-        out_specs=(VM,) * 4,
+        in_specs=[SM] + [VM] * 10 + [ANY] * 4,
+        out_specs=(ANY,) * 4 + (VM,),
         scratch_shapes=[
+            pltpu.VMEM(x.shape, BF16),
+            pltpu.VMEM(x.shape, BF16),
+            pltpu.VMEM((WIDE, half_hidden), BF16),
+            pltpu.VMEM(w_out.shape, BF16),
             pltpu.VMEM((PACK_ROWS, own), F32),
             pltpu.VMEM((PACK_ROWS, own), F32),
-            pltpu.VMEM(w_in.shape, BF16),
+            pltpu.VMEM((WIDE, half_hidden), BF16),
             pltpu.VMEM(w_out.shape, BF16),
             pltpu.VMEM((PACK_ROWS, channels), F32),
             pltpu.VMEM((1, channels), F32),
@@ -997,7 +1099,7 @@
             pltpu.VMEM(field, F32),
             pltpu.VMEM(field, F32),
             pltpu.VMEM(field, F32),
-            pltpu.VMEM(field, BF16),
+            pltpu.VMEM((rows, WIDE), BF16),
             pltpu.VMEM(field, BF16),
             pltpu.VMEM((rows, 256), BF16),
             pltpu.VMEM((rows, 256), BF16),
@@ -1007,28 +1109,33 @@
             pltpu.VMEM(field, F32),
             pltpu.VMEM((162 * 8, channels), F32),
             pltpu.VMEM((81 * 8, channels), F32),
-            pltpu.VMEM((112, channels), F32),
-            pltpu.VMEM((4, half_hidden), F32),
-            pltpu.VMEM((4, channels), F32),
+            pltpu.VMEM((2, half_hidden), F32),
+            pltpu.VMEM((SUM_ROWS, channels), F32),
             pltpu.VMEM((all_rows, 128), F32),
             pltpu.VMEM((grad_rows, 128), BF16),
             pltpu.VMEM((grad_rows, 128), BF16),
             pltpu.VMEM((all_rows, 128), BF16),
             pltpu.VMEM((all_rows, 128), BF16),
-            pltpu.VMEM((small_rows, own), F32),
-            pltpu.VMEM((128, own), F32),
-            pltpu.VMEM((128, own), F32),
-            pltpu.VMEM((peers, small_rows // size, own), F32),
+            pltpu.VMEM((all_rows, 128), BF16),
+            pltpu.VMEM(w_in.shape, F32),
+            pltpu.VMEM(w_out.shape, F32),
+            pltpu.VMEM(x.shape, BF16),
+            pltpu.VMEM(x.shape, BF16),
+            pltpu.VMEM((small_rows, 256), F32),
+            pltpu.VMEM((SUM_ROWS, 256), F32),
+            pltpu.VMEM((peers, small_rows // size, 256), F32),
             DMA((4 + groups,)),
             DMA((4 + groups,)),
-            DMA((groups * parts, bits)),
-            DMA((groups * parts, bits)),
-            DMA((groups * parts, bits)),
-            DMA((groups * parts, bits)),
+            DMA(hops),
+            DMA(hops),
+            DMA(hops),
+            DMA(hops),
             DMA((peers,)),
             DMA((peers,)),
             DMA((peers,)),
             DMA((peers,)),
+            DMA((2 * groups + 2,)),
+            DMA((4,)),
         ],
         compiler_params=pltpu.CompilerParams(
             vmem_limit_bytes=VMEM_LIMIT, collective_id=0, has_side_effects=True
@@ -1051,9 +1158,13 @@
         x,
         cot,
     )
-    g_rate, g_freq, g_coef, g_skip, g_gain, g_bias, dw_in, db_in, dw_out, g_b_out, g_scale = pl.pallas_call(
+    (
+        block_out, dx, g_rate, g_freq, g_coef, g_skip, g_gain, g_bias, dw_in, db_in, dw_out, g_b_out, g_scale,
+    ) = pl.pallas_call(
         final_kernel,
         out_shape=(
+            shape(x.shape, BF16),
+            shape(x.shape, BF16),
             shape((2, modes, own)),
             shape((2, modes, own)),
             shape((2, modes, own)),
@@ -1066,11 +1177,19 @@
             shape((channels,)),
             shape((channels,)),
         ),
-        in_specs=[VM] * 6,
-        out_specs=(VM,) * 11,
+        in_specs=[VM] * 5 + [ANY] * 4,
+        out_specs=(ANY, ANY) + (VM,) * 6 + (ANY, VM, ANY, VM, VM),
+        scratch_shapes=[
+            pltpu.VMEM((112, own), F32),
+            pltpu.VMEM(x.shape, BF16),
+            pltpu.VMEM(x.shape, BF16),
+            pltpu.VMEM(w_in.shape, F32),
+            pltpu.VMEM(w_out.shape, F32),
+            DMA((8,)),
+        ],
         compiler_params=pltpu.CompilerParams(vmem_limit_bytes=VMEM_LIMIT),
         name="final",
-    )(extent, rate, freq, coef, full, small)
+    )(extent, rate, freq, coef, small, block_out, dx, dw_in, dw_out)
     return (
         block_out.transpose(0, 2, 3, 1),
         dx.transpose(0, 2, 3, 1),

time: 82.7 us -> 76.4 us (0.924)
  Pallas kernels: 79.3 us -> 75.4 us
  local copies, waits for them, and re-layouts: 2.5 us -> 0 us
    pallas_call x1, Pallas kernels: 73.5 us -> 69.5 us  [on_device(): pl.pallas_call(partial(mega_kernel, size), out_shape=(shape(x.shape, BF16...]
    unnamed x6 -> x0, local copies, waits for them, and re-layouts: 2.5 us -> none
where the time goes in v4:
time: 76.4 us; the launch traced here: 76.2 us
  Pallas kernels  75.4 us (99%)
  between operations  0.86 us (1%)
    pallas_call x1, Pallas kernels, on_device(): pl.pallas_call(partial(mega_kernel, size), out_shape=(shape(x.shape, BF16...  69.5 us
    pallas_call x1, Pallas kernels, on_device(): pl.pallas_call(final_kernel, out_shape=(shape(x.shape, BF16), shape(x.sha...  5.81 us

profile of v4, /device:TPU:0, one launch (start us, length us, event | category | flops | bytes accessed | tf_op | source)
XLA Modules:
  0.0 76.2 jit_solution(3065658702871584363)
XLA Ops:
  0.6 69.5 %block.1 = (bf16[2,324,2,384]{3,2,1,0:T(2,128)(2,1)}, bf16[2,324,2,384]{3,2,1,0:T(2,128)(2,1)}, f32[384,768]{1,0:T(8,128)}, f32[768,384]{1,0:T(8,128)}, f32[128,256]{1,0:T(8,128)}) custom-call(s32[2,4]{1,0:T(2,128)} %class_ref.1, s32[192]{0:T(256)} %extent_ref.3, f32[2,64,192]{2,1,0:T(8,128)} %bitcast.12, f32[2,64,192]{2,1,0:T(8,128)} %bitcast.14, ...), custom_call_target="tpu_custom_call" | custom-call | tf_op jit(solution)/shard_map/block/pallas_call | solution.py:1071
  70.2 5.8 %final.1 = (bf16[2,324,2,384]{3,2,1,0:T(2,128)(2,1)}, bf16[2,324,2,384]{3,2,1,0:T(2,128)(2,1)}, f32[2,64,192]{2,1,0:T(8,128)}, f32[2,64,192]{2,1,0:T(8,128)}, f3...) custom-call(s32[192]{0:T(256)} %extent_ref.3, ...), custom_call_target="tpu_custom_call" | custom-call | tf_op jit(solution)/shard_map/final/pallas_call | solution.py:1163

commit v5 on v4

--- a/solution.py
+++ b/solution.py
@@ -548,7 +548,7 @@
     ((), (), (), ()),
     ((), (0,), (), (1, 2)),
 )
-LATER = ((), (), (0, 1), (), (2,), (), (1,), (2, 0), (1, 2))
+LATER = ((), (), (0, 1), (2,), (), (1,), (2,), (0, 2, 1))
 
 
 def mega_kernel(
@@ -568,10 +568,9 @@
     w_out_hbm,
     x_hbm,
     cot_hbm,
-    block_out,
-    dx_out,
-    dw_in_out,
-    dw_out_out,
+    block_ref,
+    dx_ref,
+    full_ref,
     small_out,
     x_ref,
     cot_ref,
@@ -609,11 +608,6 @@
     landed_ref,
     send_ref,
     recv_ref,
-    full_ref,
-    dw_in_ref,
-    dw_out_ref,
-    block_ref,
-    dx_ref,
     small_keep,
     small_land,
     small_recv,
@@ -627,7 +621,6 @@
     sc_recv,
     bc_send,
     bc_recv,
-    out_sem,
     in_sem,
 ):
     cells, channels = x_ref.shape[1], x_ref.shape[3]
@@ -703,7 +696,6 @@
     normed_ref[:, channels:] = jnp.where(
         lax.broadcasted_iota(jnp.int32, (rows, WIDE - channels), 1) < 3, 1.0, 0.0
     ).astype(BF16)
-    mlp_ref[...] = jnp.broadcast_to(b_out_ref[...].reshape(1, channels), mlp_ref.shape)
     gn_ref[...] = jnp.zeros_like(gn_ref)
     reads[2].wait()
     reads[3].wait()
@@ -769,33 +761,14 @@
             if done[group] > last:
                 continue
             rings[group].advance(done[group])
-            if done[group] == last:
-                unpack(group)
             done[group] += 1
 
-    def unpack(group):
-        base = group * stride
-        for k in range(chunk // 128):
-            at = group * chunk + k * 128
-            dw_in_ref[:, at : at + 128] = full_ref[base : base + channels, :].astype(F32)
-            base += channels
-        for k in range(channels // 128):
-            dw_out_ref[group * chunk : (group + 1) * chunk, k * 128 : (k + 1) * 128] = full_ref[
-                base : base + chunk, :
-            ].astype(F32)
-            base += chunk
-        at = pl.ds(group * chunk, chunk)
-        first = pltpu.make_async_copy(dw_in_ref.at[:, at], dw_in_out.at[:, at], out_sem.at[2 * group])
-        second = pltpu.make_async_copy(dw_out_ref.at[at, :], dw_out_out.at[at, :], out_sem.at[2 * group + 1])
-        first.start()
-        second.start()
-        writes.extend((first, second))
-
-    writes = []
     tiles = rows // tile_rows
-
-    def feed(f, w_first_ref, w_second_ref, target_ref, target_base, db_row, steps):
+    shares = []
+
+    def feed(f, w_first_ref, w_second_ref, target_ref, target_base, db_row, steps, ready):
         cols = pl.ds(f * chunk, chunk)
+        act_cols = pl.ds((1 - db_row) * half_hidden + f * chunk, chunk)
 
         def ahead(t):
             at = pl.ds(t * tile_rows, tile_rows)
@@ -808,6 +781,16 @@
             )
             return pre, g_act
 
+        def outward(t, g_pre):
+            at = pl.ds(t * tile_rows, tile_rows)
+            gn_ref[at, :] += lax.dot_general(
+                g_pre,
+                w_first_ref[:channels, cols],
+                (((1,), (1,)), ((), ())),
+                preferred_element_type=F32,
+            )
+
+        late = f == groups - 1 and db_row == 0
         waiting = ahead(0)
         for t in range(tiles):
             pre, g_act = waiting
@@ -816,54 +799,58 @@
             at = pl.ds(t * tile_rows, tile_rows)
             act, slope = gelu_and_slope(pre)
             g_pre = (g_act * slope).astype(BF16)
-            act_ref[at, :] = act
+            act_ref[at, act_cols] = act
             gpre_ref[at, :] = g_pre
-            mlp_ref[at, :] += jnp.dot(act, w_second_ref[cols, :], preferred_element_type=F32)
-            gn_ref[at, :] += lax.dot_general(
-                g_pre,
-                w_first_ref[:channels, cols],
-                (((1,), (1,)), ((), ())),
-                preferred_element_type=F32,
-            )
+            if not late:
+                outward(t, g_pre)
             advance(*steps[t])
         d_first = lax.dot_general(
-            normed_ref[...], gpre_ref[...], (((0,), (0,)), ((), ())), preferred_element_type=F32
+            normed_ref[:, : channels + 16],
+            gpre_ref[...],
+            (((0,), (0,)), ((), ())),
+            preferred_element_type=F32,
         )
         for k in range(chunk // 128):
             at = pl.ds(target_base + k * channels, channels)
             target_ref[at, :] = d_first[:channels, k * 128 : (k + 1) * 128].astype(target_ref.dtype)
         db_ref[db_row : db_row + 1, cols] = d_first[channels : channels + 1, :]
         d_second = lax.dot_general(
-            act_ref[...], gmlp_ref[...], (((0,), (0,)), ((), ())), preferred_element_type=F32
+            act_ref[:, act_cols], gmlp_ref[...], (((0,), (0,)), ((), ())), preferred_element_type=F32
         )
         base = target_base + channels * (chunk // 128)
         for k in range(channels // 128):
             at = pl.ds(base + k * chunk, chunk)
             target_ref[at, :] = d_second[:, k * 128 : (k + 1) * 128].astype(target_ref.dtype)
+        shares.append(
+            jnp.sum(d_second * w_second_ref[cols, :].astype(F32), axis=0, keepdims=True)
+        )
+        ready(f)
+        advance(*steps[3])
+        if late:
+            for t in range(tiles):
+                at = pl.ds(t * tile_rows, tile_rows)
+                outward(t, gpre_ref[at, :])
 
     def grads_copy(group):
         at = pl.ds(group * group_rows, group_rows)
         return pair_copy(4 + group, away_ref.at[at, :], landed_ref.at[at, :])
 
-    for group in range(groups):
-        feed(group, w_in_oth, w_out_oth, away_ref, group * group_rows, 1, STEPS[2 * group])
-        grads_copy(group).start()
-        advance(*STEPS[2 * group][3])
-        feed(group, w_in_ref, w_out_ref, acc_ref, group * stride, 0, STEPS[2 * group + 1])
+    def join(group):
         grads_copy(group).wait_recv()
         add_rows(landed_ref, group * group_rows, 0, 1, acc_ref, group * stride, group_rows)
         if stride > group_rows:
             acc_ref[group * stride + group_rows : (group + 1) * stride, :] = jnp.zeros(
                 (stride - group_rows, 128), F32
             )
-        advance(*STEPS[2 * group + 1][3])
+
+    for group in range(groups):
+        feed(group, w_in_oth, w_out_oth, away_ref, group * group_rows, 1, STEPS[2 * group],
+             lambda g: grads_copy(g).start())
+        feed(group, w_in_ref, w_out_ref, acc_ref, group * stride, 0, STEPS[2 * group + 1], join)
 
     def back(t, carry):
-        d_gain, d_bias, d_scale, d_b_out = carry
+        d_gain, d_bias, d_b_out = carry
         at = pl.ds(pl.multiple_of(t * 48, 16), 48)
-        mask = jnp.tile(mask_ref[at, :], (1, channels // 128))
-        branch = mlp_ref[at, :] * mask
-        d_scale = d_scale + jnp.sum(images_in(cot_ref, t * 12, 12) * branch, axis=0, keepdims=True)
         d_b_out = d_b_out + jnp.sum(gmlp_ref[at, :].astype(F32), axis=0, keepdims=True)
         grad = gn_ref[at, :]
         hat = mixed_ref[at, :]
@@ -874,10 +861,13 @@
         mean_gh = jnp.mean(grad * hat, axis=1, keepdims=True)
         rstd = jnp.tile(stat_ref[at, :], (1, channels // 128))
         gm_ref[at, :] = (rstd * (grad - mean_g - hat * mean_gh)).astype(BF16).astype(F32)
-        return d_gain, d_bias, d_scale, d_b_out
+        return d_gain, d_bias, d_b_out
 
     zero = jnp.zeros((1, channels), F32)
-    sums = lax.fori_loop(0, rows // 48, back, (zero, zero, zero, zero))
+    d_gain, d_bias, d_b_out = lax.fori_loop(0, rows // 48, back, (zero, zero, zero))
+    b_out = b_out_ref[...].reshape(1, channels)
+    d_scale = (sum(shares) + b_out * d_b_out) / scale
+    sums = (d_gain, d_bias, d_scale, d_b_out)
     mine_only = pl.ds(pl.multiple_of(core * 256, 128), 128)
     theirs_only = pl.ds(pl.multiple_of((1 - core) * 256, 128), 128)
     for index, value in enumerate(sums):
@@ -948,6 +938,13 @@
         scatter_copy(offset).start()
     mirror_out(gh_ref, mask_ref, gn_ref, gm_ref, skip_all)
     advance(*LATER[5])
+    for t in range(tiles):
+        at = pl.ds(t * tile_rows, tile_rows)
+        mlp_ref[at, :] = (
+            jnp.dot(act_ref[at, :half_hidden], w_out_oth[...], preferred_element_type=F32)
+            + jnp.dot(act_ref[at, half_hidden:], w_out_ref[...], preferred_element_type=F32)
+            + b_out
+        )
 
     def finish(t, carry):
         at = pl.ds(pl.multiple_of(t * 48, 16), 48)
@@ -957,10 +954,6 @@
         return carry
 
     lax.fori_loop(0, rows // 48, finish, 0)
-    for index, (source, target) in enumerate(((dx_ref, dx_out), (block_ref, block_out))):
-        copy = pltpu.make_async_copy(source, target, out_sem.at[2 * groups + index])
-        copy.start()
-        writes.append(copy)
     advance(*LATER[6])
     total = small_keep[mine, :]
     for offset in range(1, size):
@@ -983,22 +976,27 @@
         grads_copy(group).wait_send()
     for copy in (pack_copy, first_copy, second_copy, small_pair):
         copy.wait_send()
-    for copy in writes:
-        copy.wait()
 
 
 def final_kernel(
-    extent_ref, rate_ref, freq_ref, coef_ref, small_ref, block_ref, dx_ref, dw_in_ref, dw_out_ref,
+    extent_ref, rate_ref, freq_ref, coef_ref, small_ref, block_hbm, dx_hbm, full_hbm,
     block_out, dx_out, rate_out, freq_out, coef_out, skip_out, gain_out, bias_out, dw_in_out,
     db_in_out, dw_out_out, b_out_out, scale_out,
-    mine_ref, block_hold, dx_hold, dw_in_hold, dw_out_hold, sems,
+    mine_ref, dw_in_ref, dw_out_ref, full_ref, block_ref, dx_ref, sems,
 ):
-    held = (block_ref, dx_ref, dw_in_ref, dw_out_ref)
-    stage = (block_hold, dx_hold, dw_in_hold, dw_out_hold)
-    outs = (block_out, dx_out, dw_in_out, dw_out_out)
-    into = [pltpu.make_async_copy(held[k], stage[k], sems.at[k]) for k in range(4)]
-    away = [pltpu.make_async_copy(stage[k], outs[k], sems.at[4 + k]) for k in range(4)]
-    for copy in into:
+    channels, half_hidden = dw_in_ref.shape
+    groups = half_hidden // CHUNK
+    stride = full_ref.shape[0] // groups
+
+    def moves(first, *pairs):
+        return [
+            pltpu.make_async_copy(source, target, sems.at[first + k])
+            for k, (source, target) in enumerate(pairs)
+        ]
+
+    reads = moves(0, (full_hbm, full_ref), (block_hbm, block_ref), (dx_hbm, dx_ref))
+    writes = moves(3, (dw_in_ref, dw_in_out), (dw_out_ref, dw_out_out), (block_ref, block_out), (dx_ref, dx_out))
+    for copy in reads:
         copy.start()
     core = lax.axis_index("mp")
     own = mine_ref.shape[1]
@@ -1010,15 +1008,30 @@
 
     args = (extent_ref, rate_ref, freq_ref, coef_ref, mine_ref, rate_out, freq_out, coef_out)
     modes_grad(0, *args)
-    for k in range(4):
-        into[k].wait()
-        away[k].start()
+    reads[0].wait()
+    for group in range(groups):
+        base = group * stride
+        for k in range(CHUNK // 128):
+            at = group * CHUNK + k * 128
+            dw_in_ref[:, at : at + 128] = full_ref[base : base + channels, :].astype(F32)
+            base += channels
+        for k in range(channels // 128):
+            dw_out_ref[group * CHUNK : (group + 1) * CHUNK, k * 128 : (k + 1) * 128] = full_ref[
+                base : base + CHUNK, :
+            ].astype(F32)
+            base += CHUNK
+    writes[0].start()
+    writes[1].start()
+    reads[1].wait()
+    writes[2].start()
+    reads[2].wait()
+    writes[3].start()
     modes_grad(1, *args)
     skip_out[...] = mine_ref[108:109, :].reshape(skip_out.shape)
     db_in_out[...] = line(109, db_in_out.shape[0] // 128).reshape(db_in_out.shape)
     for k, ref in enumerate((gain_out, bias_out, scale_out, b_out_out)):
         ref[...] = line(115 + 3 * k, 3).reshape(ref.shape)
-    for copy in away:
+    for copy in writes:
         copy.wait()
 
 
@@ -1068,17 +1081,16 @@
     small_rows = max(128, 8 * size)
     peers = max(size - 1, 1)
     DMA = pltpu.SemaphoreType.DMA
-    block_out, dx, dw_in, dw_out, small = pl.pallas_call(
+    block_out, dx, full, small = pl.pallas_call(
         partial(mega_kernel, size),
         out_shape=(
             shape(x.shape, BF16),
             shape(x.shape, BF16),
-            shape(w_in.shape),
-            shape(w_out.shape),
+            shape((all_rows, 128), BF16),
             shape((small_rows, 256)),
         ),
         in_specs=[SM] + [VM] * 10 + [ANY] * 4,
-        out_specs=(ANY,) * 4 + (VM,),
+        out_specs=(VM,) * 4,
         scratch_shapes=[
             pltpu.VMEM(x.shape, BF16),
             pltpu.VMEM(x.shape, BF16),
@@ -1101,8 +1113,8 @@
             pltpu.VMEM(field, F32),
             pltpu.VMEM((rows, WIDE), BF16),
             pltpu.VMEM(field, BF16),
-            pltpu.VMEM((rows, 256), BF16),
-            pltpu.VMEM((rows, 256), BF16),
+            pltpu.VMEM((rows, 2 * half_hidden), BF16),
+            pltpu.VMEM((rows, CHUNK), BF16),
             pltpu.VMEM(field, F32),
             pltpu.VMEM(field, F32),
             pltpu.VMEM((rows, 128), F32),
@@ -1116,11 +1128,6 @@
             pltpu.VMEM((grad_rows, 128), BF16),
             pltpu.VMEM((all_rows, 128), BF16),
             pltpu.VMEM((all_rows, 128), BF16),
-            pltpu.VMEM((all_rows, 128), BF16),
-            pltpu.VMEM(w_in.shape, F32),
-            pltpu.VMEM(w_out.shape, F32),
-            pltpu.VMEM(x.shape, BF16),
-            pltpu.VMEM(x.shape, BF16),
             pltpu.VMEM((small_rows, 256), F32),
             pltpu.VMEM((SUM_ROWS, 256), F32),
             pltpu.VMEM((peers, small_rows // size, 256), F32),
@@ -1134,7 +1141,6 @@
             DMA((peers,)),
             DMA((peers,)),
             DMA((peers,)),
-            DMA((2 * groups + 2,)),
             DMA((4,)),
         ],
         compiler_params=pltpu.CompilerParams(
@@ -1177,19 +1183,20 @@
             shape((channels,)),
             shape((channels,)),
         ),
-        in_specs=[VM] * 5 + [ANY] * 4,
+        in_specs=[VM] * 5 + [ANY] * 3,
         out_specs=(ANY, ANY) + (VM,) * 6 + (ANY, VM, ANY, VM, VM),
         scratch_shapes=[
             pltpu.VMEM((112, own), F32),
+            pltpu.VMEM(w_in.shape, F32),
+            pltpu.VMEM(w_out.shape, F32),
+            pltpu.VMEM(full.shape, BF16),
             pltpu.VMEM(x.shape, BF16),
             pltpu.VMEM(x.shape, BF16),
-            pltpu.VMEM(w_in.shape, F32),
-            pltpu.VMEM(w_out.shape, F32),
-            DMA((8,)),
+            DMA((7,)),
         ],
         compiler_params=pltpu.CompilerParams(vmem_limit_bytes=VMEM_LIMIT),
         name="final",
-    )(extent, rate, freq, coef, small, block_out, dx, dw_in, dw_out)
+    )(extent, rate, freq, coef, small, block_out, dx, full)
     return (
         block_out.transpose(0, 2, 3, 1),
         dx.transpose(0, 2, 3, 1),

time: 76.4 us -> 69.9 us (0.915)
  Pallas kernels: 75.4 us -> 68.9 us
    pallas_call x1, Pallas kernels: 69.5 us -> 63.1 us  [on_device(): pl.pallas_call(partial(mega_kernel, size), out_shape=(shape(x.shape, BF16...]
where the time goes in v5:
time: 69.9 us; the launch traced here: 69.8 us
  Pallas kernels  68.9 us (99%)
  between operations  0.84 us (1%)
    pallas_call x1, Pallas kernels, on_device(): pl.pallas_call(partial(mega_kernel, size), out_shape=(shape(x.shape, BF16...  63.1 us
    pallas_call x1, Pallas kernels, on_device(): pl.pallas_call(final_kernel, out_shape=(shape(x.shape, BF16), shape(x.sha...  5.87 us

profile of v5, /device:TPU:0, one launch (start us, length us, event | category | flops | bytes accessed | tf_op | source)
XLA Modules:
  0.0 69.8 jit_solution(3595466867438163895)
XLA Ops:
  0.6 63.1 %block.1 = (bf16[2,324,2,384]{3,2,1,0:T(2,128)(2,1)}, bf16[2,324,2,384]{3,2,1,0:T(2,128)(2,1)}, bf16[4608,128]{1,0:T(8,128)(2,1)}, f32[128,256]{1,0:T(8,128)}) custom-call(s32[2,4]{1,0:T(2,128)} %class_ref.1, s32[192]{0:T(256)} %extent_ref.3, f32[2,64,192]{2,1,0:T(8,128)} %bitcast.12, f32[2,64,192]{2,1,0:T(8,128)} %bitcast.14, f32[2,64,192]{2,1,0:T(8,128)} %bitcast.16, ...), custom_call_target="tpu_custom_call" | custom-call | tf_op jit(solution)/shard_map/block/pallas_call | solution.py:1084
  63.7 5.9 %final.1 = (bf16[2,324,2,384]{3,2,1,0:T(2,128)(2,1)}, bf16[2,324,2,384]{3,2,1,0:T(2,128)(2,1)}, f32[2,64,192]{2,1,0:T(8,128)}, f32[2,64,192]{2,1,0:T(8,128)}, f3...) custom-call(s32[192]{0:T(256)} %extent_ref.3, ...), custom_call_target="tpu_custom_call" | custom-call | tf_op jit(solution)/shard_map/final/pallas_call | solution.py:1169

commit v6 on v5

--- a/solution.py
+++ b/solution.py
@@ -548,7 +548,7 @@
     ((), (), (), ()),
     ((), (0,), (), (1, 2)),
 )
-LATER = ((), (), (0, 1), (2,), (), (1,), (2,), (0, 2, 1))
+LATER = ((), (0,), (1, 2), (), (), (1, 2), (), (), (2, 0, 1))
 
 
 def mega_kernel(
@@ -691,7 +691,7 @@
     second_copy.start()
 
     build_masks(class_ref, mask_ref)
-    block = 144
+    block = 432
     scale = scale_ref[...].reshape(1, channels)
     normed_ref[:, channels:] = jnp.where(
         lax.broadcasted_iota(jnp.int32, (rows, WIDE - channels), 1) < 3, 1.0, 0.0
@@ -768,6 +768,7 @@
 
     def feed(f, w_first_ref, w_second_ref, target_ref, target_base, db_row, steps, ready):
         cols = pl.ds(f * chunk, chunk)
+        pre_cols = pl.ds((1 - db_row) * chunk, chunk)
         act_cols = pl.ds((1 - db_row) * half_hidden + f * chunk, chunk)
 
         def ahead(t):
@@ -800,13 +801,13 @@
             act, slope = gelu_and_slope(pre)
             g_pre = (g_act * slope).astype(BF16)
             act_ref[at, act_cols] = act
-            gpre_ref[at, :] = g_pre
+            gpre_ref[at, pre_cols] = g_pre
             if not late:
                 outward(t, g_pre)
             advance(*steps[t])
         d_first = lax.dot_general(
             normed_ref[:, : channels + 16],
-            gpre_ref[...],
+            gpre_ref[:, pre_cols],
             (((0,), (0,)), ((), ())),
             preferred_element_type=F32,
         )
@@ -829,7 +830,7 @@
         if late:
             for t in range(tiles):
                 at = pl.ds(t * tile_rows, tile_rows)
-                outward(t, gpre_ref[at, :])
+                outward(t, gpre_ref[at, pre_cols])
 
     def grads_copy(group):
         at = pl.ds(group * group_rows, group_rows)
@@ -945,6 +946,7 @@
             + jnp.dot(act_ref[at, half_hidden:], w_out_ref[...], preferred_element_type=F32)
             + b_out
         )
+    advance(*LATER[6])
 
     def finish(t, carry):
         at = pl.ds(pl.multiple_of(t * 48, 16), 48)
@@ -954,7 +956,7 @@
         return carry
 
     lax.fori_loop(0, rows // 48, finish, 0)
-    advance(*LATER[6])
+    advance(*LATER[7])
     total = small_keep[mine, :]
     for offset in range(1, size):
         scatter_copy(offset).wait_recv()
@@ -963,7 +965,7 @@
     for offset in range(1, size):
         spread_copy(offset).start()
 
-    advance(*LATER[7])
+    advance(*LATER[8])
     for _ in range(2 * len(stages_of(size)) + 1):
         advance(*range(groups))
     for offset in range(1, size):
@@ -1008,6 +1010,10 @@
 
     args = (extent_ref, rate_ref, freq_ref, coef_ref, mine_ref, rate_out, freq_out, coef_out)
     modes_grad(0, *args)
+    reads[1].wait()
+    writes[2].start()
+    reads[2].wait()
+    writes[3].start()
     reads[0].wait()
     for group in range(groups):
         base = group * stride
@@ -1022,10 +1028,6 @@
             base += CHUNK
     writes[0].start()
     writes[1].start()
-    reads[1].wait()
-    writes[2].start()
-    reads[2].wait()
-    writes[3].start()
     modes_grad(1, *args)
     skip_out[...] = mine_ref[108:109, :].reshape(skip_out.shape)
     db_in_out[...] = line(109, db_in_out.shape[0] // 128).reshape(db_in_out.shape)
@@ -1114,7 +1116,7 @@
             pltpu.VMEM((rows, WIDE), BF16),
             pltpu.VMEM(field, BF16),
             pltpu.VMEM((rows, 2 * half_hidden), BF16),
-            pltpu.VMEM((rows, CHUNK), BF16),
+            pltpu.VMEM((rows, 2 * CHUNK), BF16),
             pltpu.VMEM(field, F32),
             pltpu.VMEM(field, F32),
             pltpu.VMEM((rows, 128), F32),

time: 69.9 us -> 68.4 us (0.979)
  Pallas kernels: 68.9 us -> 67.4 us
    pallas_call x1, Pallas kernels: 63.1 us -> 61.6 us  [on_device(): pl.pallas_call(partial(mega_kernel, size), out_shape=(shape(x.shape, BF16...]
where the time goes in v6:
time: 68.4 us; the launch traced here: 68.2 us
  Pallas kernels  67.4 us (99%)
  between operations  0.84 us (1%)
    pallas_call x1, Pallas kernels, on_device(): pl.pallas_call(partial(mega_kernel, size), out_shape=(shape(x.shape, BF16...  61.6 us
    pallas_call x1, Pallas kernels, on_device(): pl.pallas_call(final_kernel, out_shape=(shape(x.shape, BF16), shape(x.sha...  5.8 us

profile of v6, /device:TPU:0, one launch (start us, length us, event | category | flops | bytes accessed | tf_op | source)
XLA Modules:
  0.0 68.2 jit_solution(14703136898759359649)
XLA Ops:
  0.6 61.6 %block.1 = (bf16[2,324,2,384]{3,2,1,0:T(2,128)(2,1)}, bf16[2,324,2,384]{3,2,1,0:T(2,128)(2,1)}, bf16[4608,128]{1,0:T(8,128)(2,1)}, f32[128,256]{1,0:T(8,128)}) custom-call(s32[2,4]{1,0:T(2,128)} %class_ref.1, s32[192]{0:T(256)} %extent_ref.3, f32[2,64,192]{2,1,0:T(8,128)} %bitcast.12, f32[2,64,192]{2,1,0:T(8,128)} %bitcast.14, f32[2,64,192]{2,1,0:T(8,128)} %bitcast.16, ...), custom_call_target="tpu_custom_call" | custom-call | tf_op jit(solution)/shard_map/block/pallas_call | solution.py:1086
  62.2 5.8 %final.1 = (bf16[2,324,2,384]{3,2,1,0:T(2,128)(2,1)}, bf16[2,324,2,384]{3,2,1,0:T(2,128)(2,1)}, f32[2,64,192]{2,1,0:T(8,128)}, f32[2,64,192]{2,1,0:T(8,128)}, f3...) custom-call(s32[192]{0:T(256)} %extent_ref.3, ...), custom_call_target="tpu_custom_call" | custom-call | tf_op jit(solution)/shard_map/final/pallas_call | solution.py:1171

commit v7 on v6

--- a/solution.py
+++ b/solution.py
@@ -701,13 +701,13 @@
     reads[3].wait()
 
     def load(t, carry):
-        at = pl.ds(pl.multiple_of(t * 48, 16), 48)
-        u_ref[at, :] = images_in(x_ref, t * 12, 12)
+        at = pl.ds(pl.multiple_of(t * 144, 16), 144)
+        u_ref[at, :] = images_in(x_ref, t * 36, 36)
         mask = jnp.tile(mask_ref[at, :], (1, channels // 128))
-        gmlp_ref[at, :] = (images_in(cot_ref, t * 12, 12) * scale * mask).astype(BF16)
+        gmlp_ref[at, :] = (images_in(cot_ref, t * 36, 36) * scale * mask).astype(BF16)
         return carry
 
-    lax.fori_loop(0, rows // 48, load, 0)
+    lax.fori_loop(0, rows // 144, load, 0)
     mirror_in(u_ref, mask_ref, uh_ref)
 
     pack_copy.wait_recv()
@@ -851,7 +851,7 @@
 
     def back(t, carry):
         d_gain, d_bias, d_b_out = carry
-        at = pl.ds(pl.multiple_of(t * 48, 16), 48)
+        at = pl.ds(pl.multiple_of(t * 144, 16), 144)
         d_b_out = d_b_out + jnp.sum(gmlp_ref[at, :].astype(F32), axis=0, keepdims=True)
         grad = gn_ref[at, :]
         hat = mixed_ref[at, :]
@@ -865,7 +865,7 @@
         return d_gain, d_bias, d_b_out
 
     zero = jnp.zeros((1, channels), F32)
-    d_gain, d_bias, d_b_out = lax.fori_loop(0, rows // 48, back, (zero, zero, zero))
+    d_gain, d_bias, d_b_out = lax.fori_loop(0, rows // 144, back, (zero, zero, zero))
     b_out = b_out_ref[...].reshape(1, channels)
     d_scale = (sum(shares) + b_out * d_b_out) / scale
     sums = (d_gain, d_bias, d_scale, d_b_out)
@@ -949,13 +949,13 @@
     advance(*LATER[6])
 
     def finish(t, carry):
-        at = pl.ds(pl.multiple_of(t * 48, 16), 48)
-        images_out(dx_ref, t * 12, 12, images_in(cot_ref, t * 12, 12) + gn_ref[at, :])
+        at = pl.ds(pl.multiple_of(t * 144, 16), 144)
+        images_out(dx_ref, t * 36, 36, images_in(cot_ref, t * 36, 36) + gn_ref[at, :])
         branch = mlp_ref[at, :] * jnp.tile(mask_ref[at, :], (1, channels // 128))
-        images_out(block_ref, t * 12, 12, u_ref[at, :] + scale * branch)
+        images_out(block_ref, t * 36, 36, u_ref[at, :] + scale * branch)
         return carry
 
-    lax.fori_loop(0, rows // 48, finish, 0)
+    lax.fori_loop(0, rows // 144, finish, 0)
     advance(*LATER[7])
     total = small_keep[mine, :]
     for offset in range(1, size):

time: 68.4 us -> 67.1 us (0.981)
  Pallas kernels: 67.4 us -> 66.1 us
    pallas_call x1, Pallas kernels: 61.6 us -> 60.3 us  [on_device(): pl.pallas_call(partial(mega_kernel, size), out_shape=(shape(x.shape, BF16...]
where the time goes in v7:
time: 67.1 us; the launch traced here: 67 us
  Pallas kernels  66.1 us (99%)
  between operations  0.84 us (1%)
    pallas_call x1, Pallas kernels, on_device(): pl.pallas_call(partial(mega_kernel, size), out_shape=(shape(x.shape, BF16...  60.3 us
    pallas_call x1, Pallas kernels, on_device(): pl.pallas_call(final_kernel, out_shape=(shape(x.shape, BF16), shape(x.sha...  5.8 us

profile of v7, /device:TPU:0, one launch (start us, length us, event | category | flops | bytes accessed | tf_op | source)
XLA Modules:
  0.0 67.0 jit_solution(3121331918744059835)
XLA Ops:
  0.6 60.3 %block.1 = (bf16[2,324,2,384]{3,2,1,0:T(2,128)(2,1)}, bf16[2,324,2,384]{3,2,1,0:T(2,128)(2,1)}, bf16[4608,128]{1,0:T(8,128)(2,1)}, f32[128,256]{1,0:T(8,128)}) custom-call(s32[2,4]{1,0:T(2,128)} %class_ref.1, s32[192]{0:T(256)} %extent_ref.3, f32[2,64,192]{2,1,0:T(8,128)} %bitcast.12, f32[2,64,192]{2,1,0:T(8,128)} %bitcast.14, f32[2,64,192]{2,1,0:T(8,128)} %bitcast.16, ...), custom_call_target="tpu_custom_call" | custom-call | tf_op jit(solution)/shard_map/block/pallas_call | solution.py:1086
  61.0 5.8 %final.1 = (bf16[2,324,2,384]{3,2,1,0:T(2,128)(2,1)}, bf16[2,324,2,384]{3,2,1,0:T(2,128)(2,1)}, f32[2,64,192]{2,1,0:T(8,128)}, f32[2,64,192]{2,1,0:T(8,128)}, f3...) custom-call(s32[192]{0:T(256)} %extent_ref.3, ...), custom_call_target="tpu_custom_call" | custom-call | tf_op jit(solution)/shard_map/final/pallas_call | solution.py:1171
